TPU v7x, 128 devices: a whole 4x4x4 slice. The times are simulated.
128 devices in a mesh: sec: 16 (over z_lo, x, core), img: 8 (over y, z_hi).
Axes of the slice: x: 4, y: 4, z: 4 (z_hi: 2, z_lo: 2; z = z_hi * 2 + z_lo), core: 2. Of those that a mesh axis runs over, the one named last changes fastest.
Arguments:
- saved_last: bfloat16 [16, 4, 8, 21, 21, 384], P('sec', None, 'img'), may hold values from -6 to 6
- saved_older: bfloat16 [16, 4, 8, 21, 21, 384], P('sec', None, 'img'), may hold values from -6 to 6
- arriving: bfloat16 [16, 2, 8, 21, 21, 384], P('sec', None, 'img'), may hold values from -6 to 6
- head_adjoint: bfloat16 [3, 2, 8, 21, 21, 384], P(None, None, 'img'), may hold values from -6 to 6
- plan: int32 [16, 4], P('sec'), may hold values from 0 to 3, each once within a row
- depth_five: bfloat16 [16, 25, 384], P('sec'), may hold values from -1.25 to 1.25
- depth_three: bfloat16 [16, 9, 384], P('sec'), may hold values from -2 to 2
- point_five: bfloat16 [16, 384, 384], P('sec'), may hold values from -0.3125 to 0.3125
- point_three: bfloat16 [16, 384, 384], P('sec'), may hold values from -0.3125 to 0.3125
Outputs:
- outgoing: bfloat16 [16, 2, 8, 21, 21, 384], P('sec', None, 'img')
- grad_point_five: float32 [16, 384, 384], P('sec', 'img')
- grad_depth_five: float32 [16, 384, 25], P('sec', 'img')
- grad_point_three: float32 [16, 384, 384], P('sec', 'img')
- grad_depth_three: float32 [16, 384, 9], P('sec', 'img')
Inputs may be any that keep to these rules, and one draw needn't show every extreme that they name: `plan`: each row is a permutation of the stash slots.
All inputs are finite; a program needn't handle non-finite values.
Results may differ from a plain program's by a relative error of at most 0.012.
Values may be sent and summed in bfloat16 or wider, within the bound.
No kernel may reach another device: no remote copies, remote signals or barrier semaphores. Data moves between devices by JAX's collectives and lax.ppermute only.
A program may use at most 128 MiB of HBM per device.

v0:
```python
import functools

import jax
import jax.numpy as jnp
from jax import lax
from jax.experimental import pallas as pl
from jax.experimental.pallas import tpu as pltpu
from jax.sharding import PartitionSpec as P

SIDE = 21
PIXELS = SIDE * SIDE
ROWS = 448
CH = 384
BLOCKS = CH // 128
PITCH = 24
EDGE = 8
PITCHED = EDGE + (SIDE + 4) * PITCH + 8
F32 = jnp.float32
BF16 = jnp.bfloat16


def from_next(block):
    size = lax.axis_size("sec")
    return lax.ppermute(block, "sec", [(i + 1, i) for i in range(size - 1)])


def lanes(c):
    return slice(c * 128, (c + 1) * 128)


def spread_taps(taps_ref, wide, count):
    for k in range(count):
        row = taps_ref[k : k + 1, :].astype(F32)
        for c in range(BLOCKS):
            wide[k, c] = jnp.broadcast_to(row[:, lanes(c)], (8, 128))


def clear_edges(pitched):
    top = EDGE + 2 * PITCH
    bottom = EDGE + (SIDE + 2) * PITCH
    for c in range(BLOCKS):
        pitched[c, 0:top, :] = jnp.zeros((top, 128), F32)
        pitched[c, bottom:PITCHED, :] = jnp.zeros((PITCHED - bottom, 128), F32)


def to_pitched(dense, pitched):
    inside = lax.broadcasted_iota(jnp.int32, (PITCH, 128), 0) < SIDE
    clear_edges(pitched)

    def row(i, carry):
        for c in range(BLOCKS):
            got = dense[c, pl.ds(i * SIDE, PITCH), :]
            at = pl.multiple_of(EDGE + (i + 2) * PITCH, 8)
            pitched[c, pl.ds(at, PITCH), :] = jnp.where(inside, got, 0.0)
        return carry

    lax.fori_loop(0, SIDE, row, 0, unroll=3)


def spread_conv(pitched, wide, dense, kernel, flipped):
    radius = kernel // 2
    last = kernel * kernel - 1

    def group(g, carry):
        for c in range(BLOCKS):
            sums = [[None] * 3 for _ in range(3)]
            start = EDGE + (3 * g + 2 - radius) * PITCH
            for b in range(kernel + 2):
                for shift in range(-radius, 3 + radius):
                    got = pitched[c, pl.ds(start + b * PITCH + shift, 8, stride=3), :]
                    for a in range(3):
                        p = b - a
                        if p < 0 or p >= kernel:
                            continue
                        for r in range(3):
                            q = shift - r + radius
                            if q < 0 or q >= kernel:
                                continue
                            k = p * kernel + q
                            term = wide[last - k if flipped else k, c] * got
                            old = sums[a][r]
                            sums[a][r] = term if old is None else old + term
            for a in range(3):
                for r in range(3):
                    dense[c, pl.ds((3 * g + a) * SIDE + r, 8, stride=3), :] = sums[a][r]
        return carry

    lax.fori_loop(0, SIDE // 3, group, 0)


def tap_sums(back, active, sums_ref, kernel):
    radius = kernel // 2
    count = kernel * kernel
    for c in range(BLOCKS):

        def row(i, sums):
            sums = list(sums)
            here = EDGE + (i + 2) * PITCH
            centre = [back[c, pl.ds(here + r, 8, stride=3), :] for r in range(3)]
            for p in range(kernel):
                for shift in range(-radius, 3 + radius):
                    got = active[c, pl.ds(here + (p - radius) * PITCH + shift, 8, stride=3), :]
                    for r in range(3):
                        q = shift - r + radius
                        if 0 <= q < kernel:
                            sums[p * kernel + q] = sums[p * kernel + q] + got * centre[r]
            return tuple(sums)

        sums = lax.fori_loop(0, SIDE, row, tuple(jnp.zeros((8, 128), F32) for _ in range(count)))
        for k in range(count):
            sums_ref[k : k + 1, lanes(c)] = jnp.sum(sums[k], axis=0, keepdims=True)


def pieces(ref, width):
    whole = PIXELS // 16

    def read(i):
        return ref[pl.ds(i * 16, 16)]

    tail = jnp.concatenate(
        [ref[whole * 16 : PIXELS], jnp.zeros((16 - PIXELS % 16, width, CH), BF16)], 0
    )
    return whole, read, tail


def unpack(ref, width, put):
    whole, read, tail = pieces(ref, width)

    def body(i, carry):
        put(pl.multiple_of(i * 16, 16), jnp.swapaxes(read(i), 0, 1))
        return carry

    lax.fori_loop(0, whole, body, 0)
    put(whole * 16, jnp.swapaxes(tail, 0, 1))


def prepare_kernel(turn_ref, last_ref, older_ref, arriving_ref, act_last, act_older, pair):
    for source, target in ((last_ref, act_last), (older_ref, act_older)):

        def put(at, block, target=target):
            block = jnp.maximum(block, 0)
            for k in range(4):
                target[turn_ref[k], pl.ds(at, 16), :] = block[k]

        unpack(source, 4, put)

    def put_pair(at, block):
        pair[:, pl.ds(at, 16), :] = block

    unpack(arriving_ref, 2, put_pair)


def dense_product(left, weight_ref, dense):
    for c in range(BLOCKS):
        dense[c, 0:ROWS, :] = lax.dot_general(
            left, weight_ref[lanes(c), :], (((1,), (1,)), ((), ())), preferred_element_type=F32
        )


def step_kernel(first, final, *refs):
    refs = list(refs)
    if first:
        pair_ref = refs.pop(0)
        grad_out, grad_pass = pair_ref.at[0], pair_ref.at[1]
    else:
        top_ref, out_in, pass_in, head_ref = refs[:4]
        refs = refs[4:]
    last_ref, older_ref, weight_five, weight_three, taps_five, taps_three = refs[:6]
    refs = refs[6:]
    if final:
        outgoing = refs.pop(0)
    else:
        grad_last, grad_older = refs[:2]
        refs = refs[2:]
    back_five, back_three = refs[:2]
    refs = refs[2:]
    if not first:
        grad_out = refs.pop(0)
    wide_five, wide_three, dense, dense_three, chosen_pass = refs
    if not first:
        grad_pass = chosen_pass

        @pl.when(top_ref[0] == 1)
        def _():
            def put(at, block):
                grad_out[pl.ds(at, 16), :] = block[0]
                grad_pass[pl.ds(at, 16), :] = block[1]

            unpack(head_ref, 2, put)

        @pl.when(top_ref[0] != 1)
        def _():
            grad_out[...] = out_in[...]
            grad_pass[...] = pass_in[...]

    spread_taps(taps_five, wide_five, 25)
    spread_taps(taps_three, wide_three, 9)
    left = grad_out[...]
    dense_product(left, weight_three, dense)
    to_pitched(dense, back_three)
    spread_conv(back_three, wide_three, dense_three, 3, True)
    dense_product(left, weight_five, dense)
    to_pitched(dense, back_five)
    spread_conv(back_five, wide_five, dense, 5, True)

    def finish(i, carry):
        at = pl.multiple_of(i * 16, 16)
        for c in range(BLOCKS):
            spot = (pl.ds(at, 16), lanes(c))
            older = jnp.where(older_ref[spot].astype(F32) > 0, dense_three[c, pl.ds(at, 16), :], 0.0)
            through = jnp.where(last_ref[spot].astype(F32) > 0, dense[c, pl.ds(at, 16), :], 0.0)
            last = grad_pass[spot].astype(F32) + grad_out[spot].astype(F32) + through
            if final:
                both = jnp.stack([last.astype(BF16), older.astype(BF16)], 0)
                outgoing[pl.ds(at, 16), :, lanes(c)] = jnp.swapaxes(both, 0, 1)
            else:
                grad_last[spot] = last.astype(BF16)
                grad_older[spot] = older.astype(BF16)
        return carry

    if final:
        lax.fori_loop(0, PIXELS // 16, finish, 0)
        at = PIXELS // 16 * 16
        for c in range(BLOCKS):
            spot = (slice(at, at + 16), lanes(c))
            older = jnp.where(older_ref[spot].astype(F32) > 0, dense_three[c, at : at + 16, :], 0.0)
            through = jnp.where(last_ref[spot].astype(F32) > 0, dense[c, at : at + 16, :], 0.0)
            last = grad_pass[spot].astype(F32) + grad_out[spot].astype(F32) + through
            both = jnp.stack([last.astype(BF16), older.astype(BF16)], 0)
            outgoing[at:PIXELS, :, lanes(c)] = jnp.swapaxes(both, 0, 1)[: PIXELS - at]
    else:
        lax.fori_loop(0, ROWS // 16, finish, 0)


def mix_kernel(act, taps, mixed, pitched, dense, wide, kernel):
    def widen(i, carry):
        at = pl.multiple_of(i * 16, 16)
        for c in range(BLOCKS):
            dense[c, pl.ds(at, 16), :] = act[pl.ds(at, 16), lanes(c)].astype(F32)
        return carry

    lax.fori_loop(0, ROWS // 16, widen, 0)
    to_pitched(dense, pitched)
    spread_taps(taps, wide, kernel * kernel)
    for c in range(BLOCKS):
        dense[c, ROWS - 8 : ROWS, :] = jnp.zeros((8, 128), F32)
    spread_conv(pitched, wide, dense, kernel, False)

    def narrow(i, carry):
        at = pl.multiple_of(i * 16, 16)
        for c in range(BLOCKS):
            mixed[pl.ds(at, 16), lanes(c)] = dense[c, pl.ds(at, 16), :].astype(BF16)
        return carry

    lax.fori_loop(0, ROWS // 16, narrow, 0)


def grads_kernel(first, *refs):
    refs = list(refs)
    grad_out, last_ref, older_ref, taps_five, taps_three, back_five, back_three = refs[:7]
    refs = refs[7:]
    olds = None
    if not first:
        olds = refs[:4]
        refs = refs[4:]
    sums = refs[:4]
    pitched, dense, wide, mixed = refs[4:]
    left = grad_out[0] if first else grad_out[...]
    for which, act, taps, back, kernel in (
        (0, last_ref, taps_five, back_five, 5),
        (2, older_ref, taps_three, back_three, 3),
    ):
        mix_kernel(act, taps, mixed, pitched, dense, wide, kernel)
        got = lax.dot_general(
            mixed[...], left, (((0,), (0,)), ((), ())), preferred_element_type=F32
        )
        sums[which][...] = got if first else got + olds[which][...]
        tap_sums(back, pitched, sums[which + 1], kernel)
        if not first:
            sums[which + 1][...] = sums[which + 1][...] + olds[which + 1][...]


def in_vmem():
    return pl.BlockSpec(memory_space=pltpu.VMEM)


def in_smem():
    return pl.BlockSpec(memory_space=pltpu.SMEM)


def picked(t):
    return pl.BlockSpec((None, ROWS, CH), lambda i: (t, 0, 0))


def whole(shape):
    zeros = (0,) * len(shape)
    return pl.BlockSpec(shape, lambda i: zeros)


PARAMS = pltpu.CompilerParams(vmem_limit_bytes=48 << 20)
FLAT = jax.ShapeDtypeStruct((ROWS, CH), BF16)
BACK = jax.ShapeDtypeStruct((BLOCKS, PITCHED, 128), F32)
SUMS = (
    jax.ShapeDtypeStruct((CH, CH), F32),
    jax.ShapeDtypeStruct((32, CH), F32),
    jax.ShapeDtypeStruct((CH, CH), F32),
    jax.ShapeDtypeStruct((16, CH), F32),
)


def call_prepare(turns, last, older, arriving):
    return pl.pallas_call(
        prepare_kernel,
        out_shape=(
            jax.ShapeDtypeStruct((4, ROWS, CH), BF16),
            jax.ShapeDtypeStruct((4, ROWS, CH), BF16),
            jax.ShapeDtypeStruct((2, ROWS, CH), BF16),
        ),
        in_specs=[in_smem(), in_vmem(), in_vmem(), in_vmem()],
        out_specs=(in_vmem(), in_vmem(), in_vmem()),
        compiler_params=PARAMS,
        name="prepare",
    )(turns, last, older, arriving)


def call_step(t, turns, given, act_last, act_older, weights, taps):
    first, final = t == 0, t == turns - 1
    if first:
        specs = [whole((2, ROWS, CH))]
    else:
        specs = [
            in_smem(),
            whole((ROWS, CH)),
            whole((ROWS, CH)),
            pl.BlockSpec((None, PIXELS, 2, CH), lambda i: (t - 1, 0, 0, 0)),
        ]
    specs += [picked(t), picked(t), whole((CH, CH)), whole((CH, CH)), whole((25, CH)), whole((9, CH))]
    shapes = [jax.ShapeDtypeStruct((PIXELS, 2, CH), BF16)] if final else [FLAT, FLAT]
    shapes += [BACK, BACK]
    if not first:
        shapes += [FLAT]
    return pl.pallas_call(
        functools.partial(step_kernel, first, final),
        grid=(1,),
        out_shape=tuple(shapes),
        in_specs=specs,
        out_specs=tuple(whole(s.shape) for s in shapes),
        scratch_shapes=[
            pltpu.VMEM((25, BLOCKS, 8, 128), F32),
            pltpu.VMEM((9, BLOCKS, 8, 128), F32),
            pltpu.VMEM((BLOCKS, ROWS + 8, 128), F32),
            pltpu.VMEM((BLOCKS, ROWS + 8, 128), F32),
            pltpu.VMEM((ROWS, CH), BF16),
        ],
        compiler_params=PARAMS,
        name=f"step_{t}",
    )(*given, act_last, act_older, *weights, *taps)


def call_grads(t, grad_out, act_last, act_older, taps, backs, olds):
    first = t == 0
    specs = [whole((1, ROWS, CH)) if first else whole((ROWS, CH))]
    specs += [picked(t), picked(t), whole((25, CH)), whole((9, CH)), whole(BACK.shape), whole(BACK.shape)]
    if not first:
        specs += [whole(s.shape) for s in SUMS]
    return pl.pallas_call(
        functools.partial(grads_kernel, first),
        grid=(1,),
        out_shape=SUMS,
        in_specs=specs,
        out_specs=tuple(whole(s.shape) for s in SUMS),
        scratch_shapes=[
            pltpu.VMEM((BLOCKS, PITCHED, 128), F32),
            pltpu.VMEM((BLOCKS, ROWS + 8, 128), F32),
            pltpu.VMEM((25, BLOCKS, 8, 128), F32),
            pltpu.VMEM((ROWS, CH), BF16),
        ],
        compiler_params=PARAMS,
        name=f"grads_{t}",
    )(grad_out, act_last, act_older, *taps, *backs, *olds)


def by_pixel(stack):
    return jnp.transpose(stack, (0, 2, 3, 4, 1, 5)).reshape(PIXELS, stack.shape[1], CH)


def local(
    saved_last,
    saved_older,
    arriving,
    head_adjoint,
    plan,
    depth_five,
    depth_three,
    point_five,
    point_three,
):
    turns = saved_last.shape[1]
    top = (lax.axis_index("sec") == lax.axis_size("sec") - 1).astype(jnp.int32)[None]
    slots = lax.broadcasted_iota(jnp.int32, (turns, turns), 0)
    steps = lax.broadcasted_iota(jnp.int32, (turns, turns), 1)
    turn_of_slot = jnp.sum(jnp.where(plan == slots, steps, 0), axis=1)
    head = jnp.transpose(head_adjoint, (0, 2, 3, 4, 1, 5)).reshape(turns - 1, PIXELS, 2, CH)
    act_last, act_older, pair = call_prepare(
        turn_of_slot, by_pixel(saved_last), by_pixel(saved_older), by_pixel(arriving)
    )
    weights = (point_five[0], point_three[0])
    taps = (depth_five[0], depth_three[0])
    given = (pair,)
    sums = ()
    for t in range(turns):
        made = list(call_step(t, turns, given, act_last, act_older, weights, taps))
        if t < turns - 1:
            next_pass = from_next(made[1])
            next_out = from_next(made[0])
            made = made[2:]
        else:
            outgoing = made.pop(0)
        backs = made[:2]
        used = pair if t == 0 else made[2]
        sums = call_grads(t, used, act_last, act_older, taps, backs, sums)
        if t < turns - 1:
            given = (top, next_out, next_pass, head)
    scale = 1.0 / PIXELS
    tap_rows = jnp.concatenate([sums[1][:25], sums[3][:9]], 0).T
    packed = jnp.concatenate([sums[0], sums[2], tap_rows], 1) * scale
    packed = packed.astype(BF16)
    devices = lax.axis_size("img")
    packed = packed.reshape(devices, CH // devices, packed.shape[1])
    landed = lax.all_to_all(packed, "img", 0, 0, tiled=True)
    total = jnp.sum(landed.astype(F32), axis=0)[None]
    outgoing = outgoing.reshape(1, 1, SIDE, SIDE, 2, CH).transpose(0, 4, 1, 2, 3, 5)
    return (
        outgoing,
        total[:, :, :CH],
        total[:, :, 2 * CH : 2 * CH + 25],
        total[:, :, CH : 2 * CH],
        total[:, :, 2 * CH + 25 :],
    )


def solution(mesh):
    placed = (
        P("sec", None, "img", None, None, None),
        P("sec", None, "img", None, None, None),
        P("sec", None, "img", None, None, None),
        P(None, None, "img", None, None, None),
        P("sec", None),
        P("sec", None, None),
        P("sec", None, None),
        P("sec", None, None),
        P("sec", None, None),
    )
    return jax.shard_map(
        local,
        mesh=mesh,
        in_specs=placed,
        out_specs=(
            P("sec", None, "img", None, None, None),
            P("sec", "img", None),
            P("sec", "img", None),
            P("sec", "img", None),
            P("sec", "img", None),
        ),
        check_vma=False,
    )
```

profile of v0, /device:TPU:32, one launch (start us, length us, event | category | flops | bytes accessed | tf_op | source)
XLA Modules:
  0.0 118.2 jit_solution(4246769439776209083)
XLA Ops:
  0.6 0.8 select_reduce_fusion.turn_ref
  1.4 0.0 copy-start.3
  1.4 1.3 %copy-done.3 = bf16[1,4,1,21,21,384]{5,1,4,3,2,0:T(4,128)(2,1)S(1)} copy-done((bf16[1,4,1,21,21,384]{5,1,4,3,2,0:T(4,128)(2,1)S(1)}, bf16[1,4,1,21,21,384]{5,1,4,3,2,0:T(4,128)(2,1)}, u32[]{:S(2)}) %copy-start.3) | copy-done | bytes 1354776
  2.7 0.0 copy-start.4
  2.7 1.3 %copy-done.4 = bf16[1,4,1,21,21,384]{5,1,4,3,2,0:T(4,128)(2,1)S(1)} copy-done((bf16[1,4,1,21,21,384]{5,1,4,3,2,0:T(4,128)(2,1)S(1)}, bf16[1,4,1,21,21,384]{5,1,4,3,2,0:T(4,128)(2,1)}, u32[]{:S(2)}) %copy-start.4) | copy-done | bytes 1354776
  4.1 0.0 copy-start.10
  4.1 1.1 copy-done.10
  5.2 0.0 copy-start
  5.2 0.0 copy-start.1
  5.2 3.2 %prepare.1 = (bf16[4,448,384]{2,1,0:T(8,128)(2,1)S(1)}, bf16[4,448,384]{2,1,0:T(8,128)(2,1)}, bf16[2,448,384]{2,1,0:T(8,128)(2,1)S(1)}) custom-call(s32[4]{0:T(128)S(1)} %select_reduce_fusion.turn_ref, bf16[441,4,384]{2,1,0:T(4,128)(2,1)S(1)} %bitcast.45, bf16[441,4,384]{2,1,0:T(4,128)(2,1)S(1)} %bitcast.46, bf16[441,2,384]{2,1,0:T(2,128)(2,1)S(1)} %bitcast.55), custom_call_target="tpu_custom_call" | custom-call | tf_op jit(solution)/shard_map/prepare/pallas_call | solution.py:312
  8.4 0.0 copy-done
  8.4 0.0 copy-done.1
  8.4 0.0 copy-done.2
  8.4 0.0 copy-done.9
  8.4 5.3 %step_0.1 = (bf16[448,384]{1,0:T(8,128)(2,1)}, bf16[448,384]{1,0:T(8,128)(2,1)}, f32[3,616,128]{2,1,0:T(8,128)S(1)}, f32[3,616,128]{2,1,0:T(8,128)S(1)}) custom-call(bf16[2,448,384]{2,1,0:T(8,128)(2,1)S(1)} %get-tuple-element.42.refs_0_, bf16[4,448,384]{2,1,0:T(8,128)(2,1)S(1)} %get-tuple-element.43.refs_1_.refs_4_, ...), custom_call_target="tpu_custom_call" | custom-call | tf_op jit(solution)/shard_map/step_0/pallas_call | solution.py:342
  13.8 0.9 copy-done.5
  14.7 0.9 copy-done.7
  15.6 3.6 %collective-permute-start = (bf16[448,384]{1,0:T(8,128)(2,1)}, bf16[448,384]{1,0:T(8,128)(2,1)S(1)}, u32[]{:S(2)}, u32[]{:S(2)}) collective-permute-start(bf16[448,384]{1,0:T(8,128)(2,1)} %get-tuple-element.45), channel_id=1, source_target_pairs={{8,0},{16,8},{24,16},{32,24},{40,32},{48,40},{56,48},{64,56},{72,6... | collective-permute-start | bytes 1032200 | tf_op jit(solution)/shard_map/ppermute | solution.py:24
  19.3 2.6 %collective-permute-start.1 = (bf16[448,384]{1,0:T(8,128)(2,1)}, bf16[448,384]{1,0:T(8,128)(2,1)S(1)}, u32[]{:S(2)}, u32[]{:S(2)}) collective-permute-start(bf16[448,384]{1,0:T(8,128)(2,1)} %get-tuple-element.46), channel_id=1, source_target_pairs={{8,0},{16,8},{24,16},{32,24},{40,32},{48,40},{56,48},{64,56},{72,6... | collective-permute-start | bytes 1032200 | tf_op jit(solution)/shard_map/ppermute | solution.py:24
  21.9 2.5 %collective-permute-done.refs_1_ = bf16[448,384]{1,0:T(8,128)(2,1)S(1)} collective-permute-done((bf16[448,384]{1,0:T(8,128)(2,1)}, bf16[448,384]{1,0:T(8,128)(2,1)S(1)}, u32[]{:S(2)}, u32[]{:S(2)}) %collective-permute-start) | collective-permute-done | bytes 344096 | tf_op jit(solution)/shard_map/ppermute | solution.py:24
  24.4 3.7 %collective-permute-done.1.refs_2_ = bf16[448,384]{1,0:T(8,128)(2,1)S(1)} collective-permute-done((bf16[448,384]{1,0:T(8,128)(2,1)}, bf16[448,384]{1,0:T(8,128)(2,1)S(1)}, u32[]{:S(2)}, u32[]{:S(2)}) %collective-permute-start.1) | collective-permute-done | bytes 344096 | tf_op jit(solution)/shard_map/ppermute | solution.py:24
  28.0 4.7 %step_1.1 = (bf16[448,384]{1,0:T(8,128)(2,1)S(1)}, bf16[448,384]{1,0:T(8,128)(2,1)S(1)}, f32[3,616,128]{2,1,0:T(8,128)S(1)}, f32[3,616,128]{2,1,0:T(8,128)S(1)}, bf16[448,384]{1,0:T(8,128)(2,1)S(1)}) custom-call(s32[1]{0:T(128)} %bitcast.refs_0_, bf16[448,384]{1,0:T(8,128)(2,1)S(1)} %collective-permute-done.refs_1_, ...), custom_call_target="tpu_custom_call" | custom-call | tf_op jit(solution)/shard_map/step_1/pallas_call | solution.py:342
  32.8 5.8 %collective-permute-start.2 = (bf16[448,384]{1,0:T(8,128)(2,1)S(1)}, bf16[448,384]{1,0:T(8,128)(2,1)S(1)}, u32[]{:S(2)}, u32[]{:S(2)}) collective-permute-start(bf16[448,384]{1,0:T(8,128)(2,1)S(1)} %get-tuple-element.47), channel_id=1, source_target_pairs={{8,0},{16,8},{24,16},{32,24},{40,32},{48,40},{56,48},{64,56},{72,6... | collective-permute-start | bytes 1032200 | tf_op jit(solution)/shard_map/ppermute | solution.py:24
  38.6 0.0 copy-start.6
  38.6 0.0 copy-start.8
  38.6 2.1 %collective-permute-start.3 = (bf16[448,384]{1,0:T(8,128)(2,1)S(1)}, bf16[448,384]{1,0:T(8,128)(2,1)S(1)}, u32[]{:S(2)}, u32[]{:S(2)}) collective-permute-start(bf16[448,384]{1,0:T(8,128)(2,1)S(1)} %get-tuple-element.48), channel_id=1, source_target_pairs={{8,0},{16,8},{24,16},{32,24},{40,32},{48,40},{56,48},{64,56},{72,6... | collective-permute-start | bytes 1032200 | tf_op jit(solution)/shard_map/ppermute | solution.py:24
  40.7 2.7 %collective-permute-done.2.refs_1_ = bf16[448,384]{1,0:T(8,128)(2,1)S(1)} collective-permute-done((bf16[448,384]{1,0:T(8,128)(2,1)S(1)}, bf16[448,384]{1,0:T(8,128)(2,1)S(1)}, u32[]{:S(2)}, u32[]{:S(2)}) %collective-permute-start.2) | collective-permute-done | bytes 344096 | tf_op jit(solution)/shard_map/ppermute | solution.py:24
  43.4 3.7 %collective-permute-done.3.refs_2_ = bf16[448,384]{1,0:T(8,128)(2,1)S(1)} collective-permute-done((bf16[448,384]{1,0:T(8,128)(2,1)S(1)}, bf16[448,384]{1,0:T(8,128)(2,1)S(1)}, u32[]{:S(2)}, u32[]{:S(2)}) %collective-permute-start.3) | collective-permute-done | bytes 344096 | tf_op jit(solution)/shard_map/ppermute | solution.py:24
  47.1 4.8 %step_2.1 = (bf16[448,384]{1,0:T(8,128)(2,1)S(1)}, bf16[448,384]{1,0:T(8,128)(2,1)S(1)}, f32[3,616,128]{2,1,0:T(8,128)S(1)}, f32[3,616,128]{2,1,0:T(8,128)S(1)}, bf16[448,384]{1,0:T(8,128)(2,1)S(1)}) custom-call(s32[1]{0:T(128)} %bitcast.refs_0_, bf16[448,384]{1,0:T(8,128)(2,1)S(1)} %collective-permute-done.2.refs_1_, ...), custom_call_target="tpu_custom_call" | custom-call | tf_op jit(solution)/shard_map/step_2/pallas_call | solution.py:342
  51.8 5.9 %collective-permute-start.4 = (bf16[448,384]{1,0:T(8,128)(2,1)S(1)}, bf16[448,384]{1,0:T(8,128)(2,1)S(1)}, u32[]{:S(2)}, u32[]{:S(2)}) collective-permute-start(bf16[448,384]{1,0:T(8,128)(2,1)S(1)} %get-tuple-element.49), channel_id=1, source_target_pairs={{8,0},{16,8},{24,16},{32,24},{40,32},{48,40},{56,48},{64,56},{72,6... | collective-permute-start | bytes 1032200 | tf_op jit(solution)/shard_map/ppermute | solution.py:24
  57.7 1.9 %collective-permute-start.5 = (bf16[448,384]{1,0:T(8,128)(2,1)S(1)}, bf16[448,384]{1,0:T(8,128)(2,1)S(1)}, u32[]{:S(2)}, u32[]{:S(2)}) collective-permute-start(bf16[448,384]{1,0:T(8,128)(2,1)S(1)} %get-tuple-element.50), channel_id=1, source_target_pairs={{8,0},{16,8},{24,16},{32,24},{40,32},{48,40},{56,48},{64,56},{72,6... | collective-permute-start | bytes 1032200 | tf_op jit(solution)/shard_map/ppermute | solution.py:24
  59.7 0.0 copy-done.6
  59.7 0.0 copy-done.8
  59.7 7.3 %grads_0.1 = (f32[384,384]{1,0:T(8,128)S(1)}, f32[32,384]{1,0:T(8,128)S(1)}, f32[384,384]{1,0:T(8,128)S(1)}, f32[16,384]{1,0:T(8,128)S(1)}) custom-call(bf16[2,448,384]{2,1,0:T(8,128)(2,1)S(1)} %get-tuple-element.42.refs_0_, bf16[4,448,384]{2,1,0:T(8,128)(2,1)S(1)} %get-tuple-element.43.refs_1_.refs_4_, ...), custom_call_target="tpu_custom_call" | custom-call | tf_op jit(solution)/shard_map/grads_0/pallas_call | solution.py:366
  67.0 7.3 %grads_1.1 = (f32[384,384]{1,0:T(8,128)S(1)}, f32[32,384]{1,0:T(8,128)S(1)}, f32[384,384]{1,0:T(8,128)S(1)}, f32[16,384]{1,0:T(8,128)S(1)}) custom-call(bf16[448,384]{1,0:T(8,128)(2,1)S(1)} %get-tuple-element.58.refs_0_, bf16[4,448,384]{2,1,0:T(8,128)(2,1)S(1)} %get-tuple-element.43.refs_1_.refs_4_, bf16[4,448,384]{2,1,0:T(8,128)(2,1)} %get-tuple-element.44.refs_2_.refs_5_, ...), custom_call_target="tpu_custom_call" | custom-call | tf_op jit(solution)/shard_map/grads_1/pallas_call | solution.py:366
  74.3 7.3 %grads_2.1 = (f32[384,384]{1,0:T(8,128)S(1)}, f32[32,384]{1,0:T(8,128)S(1)}, f32[384,384]{1,0:T(8,128)S(1)}, f32[16,384]{1,0:T(8,128)S(1)}) custom-call(bf16[448,384]{1,0:T(8,128)(2,1)S(1)} %get-tuple-element.55.refs_0_, bf16[4,448,384]{2,1,0:T(8,128)(2,1)S(1)} %get-tuple-element.43.refs_1_.refs_4_, bf16[4,448,384]{2,1,0:T(8,128)(2,1)} %get-tuple-element.44.refs_2_.refs_5_, ...), custom_call_target="tpu_custom_call" | custom-call | tf_op jit(solution)/shard_map/grads_2/pallas_call | solution.py:366
  81.6 0.0 collective-permute-done.4.refs_1_
  81.6 0.0 collective-permute-done.5.refs_2_
  81.6 6.0 %step_3.1 = (bf16[441,2,384]{2,1,0:T(2,128)(2,1)}, f32[3,616,128]{2,1,0:T(8,128)S(1)}, f32[3,616,128]{2,1,0:T(8,128)S(1)}, bf16[448,384]{1,0:T(8,128)(2,1)S(1)}) custom-call(s32[1]{0:T(128)} %bitcast.refs_0_, bf16[448,384]{1,0:T(8,128)(2,1)S(1)} %collective-permute-done.4.refs_1_, bf16[448,384]{1,0:T(8,128)(2,1)S(1)} %collective-permute-done.5.refs_2_, ...), custom_call_target="tpu_custom_call" | custom-call | tf_op jit(solution)/shard_map/step_3/pallas_call | solution.py:342
  87.6 7.3 %grads_3.1 = (f32[384,384]{1,0:T(8,128)S(1)}, f32[32,384]{1,0:T(8,128)S(1)}, f32[384,384]{1,0:T(8,128)S(1)}, f32[16,384]{1,0:T(8,128)S(1)}) custom-call(bf16[448,384]{1,0:T(8,128)(2,1)S(1)} %get-tuple-element.52.refs_0_, bf16[4,448,384]{2,1,0:T(8,128)(2,1)S(1)} %get-tuple-element.43.refs_1_.refs_4_, bf16[4,448,384]{2,1,0:T(8,128)(2,1)} %get-tuple-element.44.refs_2_.refs_5_, ...), custom_call_target="tpu_custom_call" | custom-call | tf_op jit(solution)/shard_map/grads_3/pallas_call | solution.py:366
  94.9 0.1 copy.23
  95.1 0.1 fusion
  95.2 20.8 %all_to_all.5 = bf16[8,48,802]{2,1,0:T(8,128)(2,1)S(1)} all-to-all(bf16[8,48,802]{2,1,0:T(8,128)(2,1)S(1)} %fusion), channel_id=1, replica_groups=mesh['sec'=16,'img'=8] {'img'}, dimensions={0} | all-to-all | bytes 1231872 | tf_op jit(solution)/shard_map/all_to_all | solution.py:430
  116.0 0.1 convert_reduce_fusion
  116.1 0.1 slice.27
  116.1 0.7 fusion.1
  116.8 0.7 copy.21
  117.5 0.7 copy.22
  (6 shorter events, 0.0 us)
Async XLA Ops:
  1.4 1.3 %copy-start.3 = (bf16[1,4,1,21,21,384]{5,1,4,3,2,0:T(4,128)(2,1)S(1)}, bf16[1,4,1,21,21,384]{5,1,4,3,2,0:T(4,128)(2,1)}, u32[]{:S(2)}) copy-start(bf16[1,4,1,21,21,384]{5,1,4,3,2,0:T(4,128)(2,1)} %param.9) | copy-start | bytes 4064260
  2.7 1.3 %copy-start.4 = (bf16[1,4,1,21,21,384]{5,1,4,3,2,0:T(4,128)(2,1)S(1)}, bf16[1,4,1,21,21,384]{5,1,4,3,2,0:T(4,128)(2,1)}, u32[]{:S(2)}) copy-start(bf16[1,4,1,21,21,384]{5,1,4,3,2,0:T(4,128)(2,1)} %param.10) | copy-start | bytes 4064260
  4.1 1.1 copy-start.10
  5.2 3.2 %copy-start = (bf16[1,384,384]{2,1,0:T(8,128)(2,1)S(1)}, bf16[1,384,384]{2,1,0:T(8,128)(2,1)}, u32[]{:S(2)}) copy-start(bf16[1,384,384]{2,1,0:T(8,128)(2,1)} %param.16) | copy-start | bytes 884740
  5.2 3.2 %copy-start.1 = (bf16[1,384,384]{2,1,0:T(8,128)(2,1)S(1)}, bf16[1,384,384]{2,1,0:T(8,128)(2,1)}, u32[]{:S(2)}) copy-start(bf16[1,384,384]{2,1,0:T(8,128)(2,1)} %param.17) | copy-start | bytes 884740
  5.2 3.2 %copy-start.2 = (bf16[1,25,384]{2,1,0:T(8,128)(2,1)S(1)}, bf16[1,25,384]{2,1,0:T(8,128)(2,1)}, u32[]{:S(2)}) copy-start(bf16[1,25,384]{2,1,0:T(8,128)(2,1)} %param.14) | copy-start | bytes 57604
  5.2 3.2 %copy-start.9 = (bf16[1,9,384]{2,1,0:T(8,128)(2,1)S(1)}, bf16[1,9,384]{2,1,0:T(8,128)(2,1)}, u32[]{:S(2)}) copy-start(bf16[1,9,384]{2,1,0:T(8,128)(2,1)} %param.15) | copy-start | bytes 20740
  13.8 0.9 copy-start.5
  14.7 1.0 copy-start.7
  15.6 8.7 %collective-permute-start = (bf16[448,384]{1,0:T(8,128)(2,1)}, bf16[448,384]{1,0:T(8,128)(2,1)S(1)}, u32[]{:S(2)}, u32[]{:S(2)}) collective-permute-start(bf16[448,384]{1,0:T(8,128)(2,1)} %get-tuple-element.45), channel_id=1, source_target_pairs={{8,0},{16,8},{24,16},{32,24},{40,32},{48,40},{56,48},{64,56},{72,6... | collective-permute-start | bytes 1032200 | tf_op jit(solution)/shard_map/ppermute | solution.py:24
  19.3 8.7 %collective-permute-start.1 = (bf16[448,384]{1,0:T(8,128)(2,1)}, bf16[448,384]{1,0:T(8,128)(2,1)S(1)}, u32[]{:S(2)}, u32[]{:S(2)}) collective-permute-start(bf16[448,384]{1,0:T(8,128)(2,1)} %get-tuple-element.46), channel_id=1, source_target_pairs={{8,0},{16,8},{24,16},{32,24},{40,32},{48,40},{56,48},{64,56},{72,6... | collective-permute-start | bytes 1032200 | tf_op jit(solution)/shard_map/ppermute | solution.py:24
  32.8 10.6 %collective-permute-start.2 = (bf16[448,384]{1,0:T(8,128)(2,1)S(1)}, bf16[448,384]{1,0:T(8,128)(2,1)S(1)}, u32[]{:S(2)}, u32[]{:S(2)}) collective-permute-start(bf16[448,384]{1,0:T(8,128)(2,1)S(1)} %get-tuple-element.47), channel_id=1, source_target_pairs={{8,0},{16,8},{24,16},{32,24},{40,32},{48,40},{56,48},{64,56},{72,6... | collective-permute-start | bytes 1032200 | tf_op jit(solution)/shard_map/ppermute | solution.py:24
  38.6 21.1 %copy-start.6 = (f32[3,616,128]{2,1,0:T(8,128)S(1)}, f32[3,616,128]{2,1,0:T(8,128)}, u32[]{:S(2)}) copy-start(f32[3,616,128]{2,1,0:T(8,128)} %copy-done.5) | copy-start | bytes 2838532
  38.6 21.1 %copy-start.8 = (f32[3,616,128]{2,1,0:T(8,128)S(1)}, f32[3,616,128]{2,1,0:T(8,128)}, u32[]{:S(2)}) copy-start(f32[3,616,128]{2,1,0:T(8,128)} %copy-done.7) | copy-start | bytes 2838532
  38.6 8.4 %collective-permute-start.3 = (bf16[448,384]{1,0:T(8,128)(2,1)S(1)}, bf16[448,384]{1,0:T(8,128)(2,1)S(1)}, u32[]{:S(2)}, u32[]{:S(2)}) collective-permute-start(bf16[448,384]{1,0:T(8,128)(2,1)S(1)} %get-tuple-element.48), channel_id=1, source_target_pairs={{8,0},{16,8},{24,16},{32,24},{40,32},{48,40},{56,48},{64,56},{72,6... | collective-permute-start | bytes 1032200 | tf_op jit(solution)/shard_map/ppermute | solution.py:24
  51.8 29.8 %collective-permute-start.4 = (bf16[448,384]{1,0:T(8,128)(2,1)S(1)}, bf16[448,384]{1,0:T(8,128)(2,1)S(1)}, u32[]{:S(2)}, u32[]{:S(2)}) collective-permute-start(bf16[448,384]{1,0:T(8,128)(2,1)S(1)} %get-tuple-element.49), channel_id=1, source_target_pairs={{8,0},{16,8},{24,16},{32,24},{40,32},{48,40},{56,48},{64,56},{72,6... | collective-permute-start | bytes 1032200 | tf_op jit(solution)/shard_map/ppermute | solution.py:24
  57.7 23.8 %collective-permute-start.5 = (bf16[448,384]{1,0:T(8,128)(2,1)S(1)}, bf16[448,384]{1,0:T(8,128)(2,1)S(1)}, u32[]{:S(2)}, u32[]{:S(2)}) collective-permute-start(bf16[448,384]{1,0:T(8,128)(2,1)S(1)} %get-tuple-element.50), channel_id=1, source_target_pairs={{8,0},{16,8},{24,16},{32,24},{40,32},{48,40},{56,48},{64,56},{72,6... | collective-permute-start | bytes 1032200 | tf_op jit(solution)/shard_map/ppermute | solution.py:24
where the time goes:
time: 119 us; the launch traced here: 118 us
  Pallas kernels  53.3 us (45%)
  starting transfers between devices  21.9 us (18%)
  blocking collectives  20.8 us (17%)
  waiting for transfers between devices  12.5 us (11%)
  local copies, waits for them, and re-layouts  7.88 us (7%)
    pallas_call x4, Pallas kernels, call_grads(): pl.pallas_call(functools.partial(grads_kernel, first), grid=(1,), out_sha...  29.2 us
    ppermute x6, starting transfers between devices, from_next(): return lax.ppermute(block, 'sec', [(i + 1, i) for i in range(size - 1)])  21.9 us
    pallas_call x4, Pallas kernels, call_step(): pl.pallas_call(functools.partial(step_kernel, first, final), grid=(1,), o...  20.9 us
    all_to_all x1, blocking collectives, local(): landed = lax.all_to_all(packed, 'img', 0, 0, tiled=True)  20.8 us
    ppermute x6, waiting for transfers between devices, from_next(): return lax.ppermute(block, 'sec', [(i + 1, i) for i in range(size - 1)])  12.5 us
    unnamed x24, local copies, waits for them, and re-layouts  7.01 us
    pallas_call x1, Pallas kernels, call_prepare(): pl.pallas_call(prepare_kernel, out_shape=(jax.ShapeDtypeStruct((4, ROWS,...  3.22 us
  transfers between devices with their start and end apart: 6, of which 4 were waited for; matrix products, arithmetic and copies ran while one was open for 0% of the time, Pallas kernels for 18%

commit v1 on v0

v1 whole, which is shorter than its diff:
```python
import functools

import jax
import jax.numpy as jnp
from jax import lax
from jax.experimental import pallas as pl
from jax.experimental.pallas import tpu as pltpu
from jax.sharding import PartitionSpec as P

SIDE = 21
PIXELS = SIDE * SIDE
ROWS = 448
CH = 384
BLOCKS = CH // 128
PITCH = 24
EDGE = 8
PITCHED = EDGE + (SIDE + 4) * PITCH + 8
F32 = jnp.float32
BF16 = jnp.bfloat16


def from_next(block):
    size = lax.axis_size("sec")
    return lax.ppermute(block, "sec", [(i + 1, i) for i in range(size - 1)])


def lanes(c):
    return slice(c * 128, (c + 1) * 128)


def spread_taps(taps_ref, wide, count):
    for k in range(count):
        row = taps_ref[k : k + 1, :].astype(F32)
        for c in range(BLOCKS):
            wide[k, c] = jnp.broadcast_to(row[:, lanes(c)], (8, 128))


def clear_edges(pitched):
    top = EDGE + 2 * PITCH
    bottom = EDGE + (SIDE + 2) * PITCH
    for c in range(BLOCKS):
        pitched[c, 0:top, :] = jnp.zeros((top, 128), F32)
        pitched[c, bottom:PITCHED, :] = jnp.zeros((PITCHED - bottom, 128), F32)


def to_pitched(dense, pitched):
    inside = lax.broadcasted_iota(jnp.int32, (PITCH, 128), 0) < SIDE
    clear_edges(pitched)

    def row(i, carry):
        for c in range(BLOCKS):
            got = dense[c, pl.ds(i * SIDE, PITCH), :]
            at = pl.multiple_of(EDGE + (i + 2) * PITCH, 8)
            pitched[c, pl.ds(at, PITCH), :] = jnp.where(inside, got, 0.0)
        return carry

    lax.fori_loop(0, SIDE, row, 0, unroll=3)


def spread_conv(pitched, wide, dense, kernel, flipped):
    radius = kernel // 2
    last = kernel * kernel - 1

    def group(g, carry):
        for c in range(BLOCKS):
            sums = [[None] * 3 for _ in range(3)]
            start = EDGE + (3 * g + 2 - radius) * PITCH
            for b in range(kernel + 2):
                for shift in range(-radius, 3 + radius):
                    got = pitched[c, pl.ds(start + b * PITCH + shift, 8, stride=3), :]
                    for a in range(3):
                        p = b - a
                        if p < 0 or p >= kernel:
                            continue
                        for r in range(3):
                            q = shift - r + radius
                            if q < 0 or q >= kernel:
                                continue
                            k = p * kernel + q
                            term = wide[last - k if flipped else k, c] * got
                            old = sums[a][r]
                            sums[a][r] = term if old is None else old + term
            for a in range(3):
                for r in range(3):
                    dense[c, pl.ds((3 * g + a) * SIDE + r, 8, stride=3), :] = sums[a][r]
        return carry

    lax.fori_loop(0, SIDE // 3, group, 0)


def tap_sums(back, active, sums_ref, kernel):
    radius = kernel // 2
    count = kernel * kernel
    for c in range(BLOCKS):

        def row(i, sums):
            sums = list(sums)
            here = EDGE + (i + 2) * PITCH
            centre = [back[c, pl.ds(here + r, 8, stride=3), :] for r in range(3)]
            for p in range(kernel):
                for shift in range(-radius, 3 + radius):
                    got = active[c, pl.ds(here + (p - radius) * PITCH + shift, 8, stride=3), :]
                    for r in range(3):
                        q = shift - r + radius
                        if 0 <= q < kernel:
                            sums[p * kernel + q] = sums[p * kernel + q] + got * centre[r]
            return tuple(sums)

        sums = lax.fori_loop(0, SIDE, row, tuple(jnp.zeros((8, 128), F32) for _ in range(count)))
        for k in range(count):
            sums_ref[k : k + 1, lanes(c)] = jnp.sum(sums[k], axis=0, keepdims=True)


def pieces(ref, width):
    whole = PIXELS // 16

    def read(i):
        return ref[pl.ds(i * 16, 16)]

    tail = jnp.concatenate(
        [ref[whole * 16 : PIXELS], jnp.zeros((16 - PIXELS % 16, width, CH), BF16)], 0
    )
    return whole, read, tail


def unpack(ref, width, put):
    whole, read, tail = pieces(ref, width)

    def body(i, carry):
        put(pl.multiple_of(i * 16, 16), jnp.swapaxes(read(i), 0, 1))
        return carry

    lax.fori_loop(0, whole, body, 0)
    put(whole * 16, jnp.swapaxes(tail, 0, 1))


def dense_product(left, weight_ref, dense):
    for c in range(BLOCKS):
        dense[c, 0:ROWS, :] = lax.dot_general(
            left, weight_ref[lanes(c), :], (((1,), (1,)), ((), ())), preferred_element_type=F32
        )


def masked(act, t, dense, c, rows):
    return jnp.where(act[t, rows, lanes(c)].astype(F32) > 0, dense[c, rows, :], 0.0)


def finish_older(act_older, t, dense, grad_older):
    def body(i, carry):
        rows = pl.ds(pl.multiple_of(i * 16, 16), 16)
        for c in range(BLOCKS):
            grad_older[rows, lanes(c)] = masked(act_older, t, dense, c, rows).astype(BF16)
        return carry

    lax.fori_loop(0, ROWS // 16, body, 0)


def last_piece(act_last, t, dense, grad_out, grad_pass, c, rows):
    skip = grad_pass[rows, lanes(c)].astype(F32) + grad_out[rows, lanes(c)].astype(F32)
    return (skip + masked(act_last, t, dense, c, rows)).astype(BF16)


def finish_last(act_last, t, dense, grad_out, grad_pass, grad_last):
    def body(i, carry):
        rows = pl.ds(pl.multiple_of(i * 16, 16), 16)
        for c in range(BLOCKS):
            grad_last[rows, lanes(c)] = last_piece(act_last, t, dense, grad_out, grad_pass, c, rows)
        return carry

    lax.fori_loop(0, ROWS // 16, body, 0)


def copies(pairs, sems):
    return [pltpu.make_async_copy(a, b, sems.at[n]) for n, (a, b) in enumerate(pairs)]


def relay(
    t,
    grad_out,
    grad_pass,
    act_last,
    act_older,
    weight_five,
    weight_three,
    taps_five,
    taps_three,
    back_five,
    back_three,
    made_last,
    made_older,
    wide_five,
    wide_three,
    dense,
    older_ready,
    last_ready,
):
    spread_taps(taps_five, wide_five, 25)
    spread_taps(taps_three, wide_three, 9)
    left = grad_out[...]
    dense_product(left, weight_three, dense)
    to_pitched(dense, back_three)
    spread_conv(back_three, wide_three, dense, 3, True)
    older_ready()
    finish_older(act_older, t, dense, made_older)
    dense_product(left, weight_five, dense)
    to_pitched(dense, back_five)
    spread_conv(back_five, wide_five, dense, 5, True)
    last_ready()
    finish_last(act_last, t, dense, grad_out, grad_pass, made_last)


def first_kernel(
    turn_ref,
    last_hbm,
    older_hbm,
    arriving_hbm,
    weight_five,
    weight_three,
    taps_five,
    taps_three,
    grad_last,
    grad_older,
    act_last,
    act_older,
    grad_out,
    back_five,
    back_three,
    last_in,
    older_in,
    arriving_in,
    grad_pass,
    wide_five,
    wide_three,
    dense,
    sems,
):
    half = 224
    gets = copies(
        [
            (arriving_hbm.at[0:half], arriving_in.at[0:half]),
            (arriving_hbm.at[half:], arriving_in.at[half:]),
            (older_hbm.at[0:half], older_in.at[0:half]),
            (older_hbm.at[half:], older_in.at[half:]),
            (last_hbm.at[0:half], last_in.at[0:half]),
            (last_hbm.at[half:], last_in.at[half:]),
        ],
        sems,
    )
    for get in gets:
        get.start()

    def put_pair(at, block):
        grad_out[pl.ds(at, 16), :] = block[0]
        grad_pass[pl.ds(at, 16), :] = block[1]

    gets[0].wait()
    gets[1].wait()
    unpack(arriving_in, 2, put_pair)

    def ready(one, two, source, target):
        def run():
            gets[one].wait()
            gets[two].wait()

            def put(at, block):
                block = jnp.maximum(block, 0)
                for k in range(4):
                    target[turn_ref[k], pl.ds(at, 16), :] = block[k]

            unpack(source, 4, put)

        return run

    relay(
        0,
        grad_out,
        grad_pass,
        act_last,
        act_older,
        weight_five,
        weight_three,
        taps_five,
        taps_three,
        back_five,
        back_three,
        grad_last,
        grad_older,
        wide_five,
        wide_three,
        dense,
        ready(2, 3, older_in, act_older),
        ready(4, 5, last_in, act_last),
    )


def take(t, top_ref, out_in, pass_in, head_hbm, grad_out, grad_pass, head_in, sem):
    @pl.when(top_ref[0] == 1)
    def _():
        get = pltpu.make_async_copy(head_hbm.at[t - 1], head_in, sem)
        get.start()
        get.wait()

        def put(at, block):
            grad_out[pl.ds(at, 16), :] = block[0]
            grad_pass[pl.ds(at, 16), :] = block[1]

        unpack(head_in, 2, put)

    @pl.when(top_ref[0] != 1)
    def _():
        grad_out[...] = out_in[...]
        grad_pass[...] = pass_in[...]


def middle_kernel(
    t,
    top_ref,
    out_in,
    pass_in,
    head_hbm,
    act_last,
    act_older,
    weight_five,
    weight_three,
    taps_five,
    taps_three,
    grad_last,
    grad_older,
    grad_out,
    back_five,
    back_three,
    head_in,
    grad_pass,
    wide_five,
    wide_three,
    dense,
    sem,
):
    take(t, top_ref, out_in, pass_in, head_hbm, grad_out, grad_pass, head_in, sem)
    relay(
        t,
        grad_out,
        grad_pass,
        act_last,
        act_older,
        weight_five,
        weight_three,
        taps_five,
        taps_three,
        back_five,
        back_three,
        grad_last,
        grad_older,
        wide_five,
        wide_three,
        dense,
        lambda: None,
        lambda: None,
    )


def widened(act, t, dense):
    def body(i, carry):
        rows = pl.ds(pl.multiple_of(i * 16, 16), 16)
        for c in range(BLOCKS):
            dense[c, rows, :] = act[t, rows, lanes(c)].astype(F32)
        return carry

    lax.fori_loop(0, ROWS // 16, body, 0)


def mix(act, t, taps, mixed, pitched, dense, wide, kernel):
    widened(act, t, dense)
    to_pitched(dense, pitched)
    spread_taps(taps, wide, kernel * kernel)
    for c in range(BLOCKS):
        dense[c, ROWS - 8 : ROWS, :] = jnp.zeros((8, 128), F32)
    spread_conv(pitched, wide, dense, kernel, False)

    def body(i, carry):
        rows = pl.ds(pl.multiple_of(i * 16, 16), 16)
        for c in range(BLOCKS):
            mixed[rows, lanes(c)] = dense[c, rows, :].astype(BF16)
        return carry

    lax.fori_loop(0, ROWS // 16, body, 0)


def across(mixed, left):
    return lax.dot_general(mixed, left, (((0,), (0,)), ((), ())), preferred_element_type=F32)


def grads_kernel(t, ahead, *refs):
    refs = list(refs)
    grad_out, act_last, act_older, taps_five, taps_three, back_five, back_three = refs[:7]
    refs = refs[7:]
    olds = None
    if t > 0:
        olds = refs[:4]
        refs = refs[4:]
    sums = refs[:4]
    refs = refs[4:]
    if ahead is not None:
        later = refs[:2]
        refs = refs[2:]
    pitched, dense, wide, mixed = refs
    left = grad_out[...]
    for n, (act, taps, back, kernel) in enumerate(
        ((act_last, taps_five, back_five, 5), (act_older, taps_three, back_three, 3))
    ):
        if ahead is not None:
            mix(act, ahead, taps, later[n], pitched, dense, wide, kernel)
        mix(act, t, taps, mixed, pitched, dense, wide, kernel)
        got = across(mixed[...], left)
        sums[2 * n][...] = got if olds is None else got + olds[2 * n][...]
        tap_sums(back, pitched, sums[2 * n + 1], kernel)
        if olds is not None:
            sums[2 * n + 1][...] = sums[2 * n + 1][...] + olds[2 * n + 1][...]


def last_grads_kernel(
    t,
    top_ref,
    out_in,
    pass_in,
    head_hbm,
    act_last,
    act_older,
    weight_five,
    weight_three,
    mixed_five,
    mixed_three,
    old_five,
    old_taps_five,
    old_three,
    old_taps_three,
    packed_hbm,
    out_hbm,
    pass_hbm,
    back_five_hbm,
    back_three_hbm,
    last_hbm,
    older_hbm,
    packed,
    grad_out,
    grad_pass,
    back_five,
    back_three,
    head_in,
    pitched,
    dense,
    rows_ref,
    sems,
):
    scale = 1.0 / PIXELS
    keep = copies(
        [
            (act_last.at[t], last_hbm),
            (act_older.at[t], older_hbm),
            (grad_out, out_hbm),
            (grad_pass, pass_hbm),
            (back_five, back_five_hbm),
            (back_three, back_three_hbm),
        ],
        sems,
    )
    points, columns = copies(
        [
            (packed.at[:, pl.ds(0, 2 * CH)], packed_hbm.at[:, pl.ds(0, 2 * CH)]),
            (packed.at[:, pl.ds(2 * CH, 128)], packed_hbm.at[:, pl.ds(2 * CH, 128)]),
        ],
        sems.at[pl.ds(6, 2)],
    )
    keep[0].start()
    keep[1].start()
    take(t, top_ref, out_in, pass_in, head_hbm, grad_out, grad_pass, head_in, sems.at[8])
    keep[2].start()
    keep[3].start()
    left = grad_out[...]
    packed[:, 0:CH] = ((across(mixed_five[...], left) + old_five[...]) * scale).astype(BF16)
    packed[:, CH : 2 * CH] = ((across(mixed_three[...], left) + old_three[...]) * scale).astype(BF16)
    points.start()
    rows_ref[...] = jnp.zeros(rows_ref.shape, F32)
    for act, weight, back, old, at, kernel, kept in (
        (act_last, weight_five, back_five, old_taps_five, 0, 5, keep[4]),
        (act_older, weight_three, back_three, old_taps_three, 32, 3, keep[5]),
    ):
        dense_product(left, weight, dense)
        to_pitched(dense, back)
        kept.start()
        widened(act, t, dense)
        to_pitched(dense, pitched)
        count = kernel * kernel
        tap_sums(back, pitched, rows_ref.at[pl.ds(at, old.shape[0])], kernel)
        rows_ref[at : at + count, :] = (rows_ref[at : at + count, :] + old[0:count, :]) * scale
    for c in range(BLOCKS):
        packed[lanes(c), 2 * CH : 2 * CH + 128] = rows_ref[:, lanes(c)].T.astype(BF16)
    columns.start()
    for copy in keep:
        copy.wait()
    points.wait()
    columns.wait()


def last_kernel(
    grad_out_hbm,
    grad_pass_hbm,
    back_five_hbm,
    back_three_hbm,
    act_last_hbm,
    act_older_hbm,
    taps_five,
    taps_three,
    outgoing_hbm,
    grad_out,
    grad_pass,
    back_five,
    back_three,
    act_last,
    act_older,
    wide_five,
    wide_three,
    dense,
    made_older,
    outgoing,
    sems,
):
    gets = copies(
        [
            (back_three_hbm, back_three),
            (act_older_hbm, act_older.at[0]),
            (back_five_hbm, back_five),
            (act_last_hbm, act_last.at[0]),
            (grad_out_hbm, grad_out),
            (grad_pass_hbm, grad_pass),
        ],
        sems,
    )
    for get in gets:
        get.start()
    spread_taps(taps_five, wide_five, 25)
    spread_taps(taps_three, wide_three, 9)
    gets[0].wait()
    spread_conv(back_three, wide_three, dense, 3, True)
    gets[1].wait()
    finish_older(act_older, 0, dense, made_older)
    gets[2].wait()
    spread_conv(back_five, wide_five, dense, 5, True)
    for get in gets[3:]:
        get.wait()

    def both(rows, c):
        last = last_piece(act_last, 0, dense, grad_out, grad_pass, c, rows)
        return jnp.swapaxes(jnp.stack([last, made_older[rows, lanes(c)]], 0), 0, 1)

    def body(i, carry):
        rows = pl.ds(pl.multiple_of(i * 16, 16), 16)
        for c in range(BLOCKS):
            outgoing[rows, :, lanes(c)] = both(rows, c)
        return carry

    half = 224
    lax.fori_loop(0, half // 16, body, 0)
    put = copies(
        [
            (outgoing.at[pl.ds(0, half)], outgoing_hbm.at[pl.ds(0, half)]),
            (outgoing.at[pl.ds(half, PIXELS - half)], outgoing_hbm.at[pl.ds(half, PIXELS - half)]),
        ],
        sems.at[pl.ds(6, 2)],
    )
    put[0].start()
    lax.fori_loop(half // 16, PIXELS // 16, body, 0)
    at = PIXELS // 16 * 16
    for c in range(BLOCKS):
        outgoing[at:PIXELS, :, lanes(c)] = both(slice(at, at + 16), c)[: PIXELS - at]
    put[1].start()
    put[0].wait()
    put[1].wait()


def total_kernel(landed, five, three, taps):
    def summed(columns):
        total = landed[0, :, columns].astype(F32)
        for n in range(1, landed.shape[0]):
            total = total + landed[n, :, columns].astype(F32)
        return total

    five[...] = summed(slice(0, CH))
    three[...] = summed(slice(CH, 2 * CH))
    taps[...] = summed(slice(2 * CH, 2 * CH + 128)).T


VMEM = pl.BlockSpec(memory_space=pltpu.VMEM)
SMEM = pl.BlockSpec(memory_space=pltpu.SMEM)
ANY = pl.BlockSpec(memory_space=pl.ANY)
ALONE = 16 << 20
OPENING = 32 << 20
FLAT = jax.ShapeDtypeStruct((ROWS, CH), BF16)
PACKED = jax.ShapeDtypeStruct((CH, 2 * CH + 128), BF16)
ACTS = jax.ShapeDtypeStruct((4, ROWS, CH), BF16)
BACK = jax.ShapeDtypeStruct((BLOCKS, PITCHED, 128), F32)
SUMS = (
    jax.ShapeDtypeStruct((CH, CH), F32),
    jax.ShapeDtypeStruct((32, CH), F32),
    jax.ShapeDtypeStruct((CH, CH), F32),
    jax.ShapeDtypeStruct((16, CH), F32),
)
FLAT_SCRATCH = pltpu.VMEM((ROWS, CH), BF16)
PAIR_SCRATCH = pltpu.VMEM((PIXELS, 2, CH), BF16)
WIDE_FIVE = pltpu.VMEM((25, BLOCKS, 8, 128), F32)
WIDE_THREE = pltpu.VMEM((9, BLOCKS, 8, 128), F32)
DENSE = pltpu.VMEM((BLOCKS, ROWS + 8, 128), F32)
PITCHED_SCRATCH = pltpu.VMEM((BLOCKS, PITCHED, 128), F32)


def run(kernel, name, operands, specs, shapes, out_specs, scratch, micros, limit=12 << 20):
    cost = pl.CostEstimate(flops=int(micros * 1e9), bytes_accessed=0, transcendentals=0)
    return pl.pallas_call(
        kernel,
        out_shape=tuple(shapes),
        in_specs=specs,
        out_specs=tuple(out_specs),
        scratch_shapes=scratch,
        compiler_params=pltpu.CompilerParams(vmem_limit_bytes=limit),
        cost_estimate=cost,
        name=name,
    )(*operands)


def call_first(turns, last, older, arriving, weights, taps):
    return run(
        first_kernel,
        "first",
        (turns, last, older, arriving, *weights, *taps),
        [SMEM, ANY, ANY, ANY] + [VMEM] * 4,
        (FLAT, FLAT, ACTS, ACTS, FLAT, BACK, BACK),
        (VMEM,) * 7,
        [
            pltpu.VMEM((PIXELS, 4, CH), BF16),
            pltpu.VMEM((PIXELS, 4, CH), BF16),
            PAIR_SCRATCH,
            FLAT_SCRATCH,
            WIDE_FIVE,
            WIDE_THREE,
            DENSE,
            pltpu.SemaphoreType.DMA((6,)),
        ],
        8,
        OPENING,
    )


def call_middle(t, given, acts, weights, taps):
    return run(
        functools.partial(middle_kernel, t),
        f"middle_{t}",
        (*given, *acts, *weights, *taps),
        [SMEM, VMEM, VMEM, ANY] + [VMEM] * 6,
        (FLAT, FLAT, FLAT, BACK, BACK),
        (VMEM,) * 5,
        [
            PAIR_SCRATCH,
            FLAT_SCRATCH,
            WIDE_FIVE,
            WIDE_THREE,
            DENSE,
            pltpu.SemaphoreType.DMA,
        ],
        5,
    )


def call_grads(t, ahead, grad_out, acts, taps, backs, olds):
    shapes = SUMS if ahead is None else SUMS + (FLAT, FLAT)
    operands = (grad_out, *acts, *taps, *backs, *olds)
    return run(
        functools.partial(grads_kernel, t, ahead),
        f"grads_{t}",
        operands,
        [VMEM] * len(operands),
        shapes,
        (VMEM,) * len(shapes),
        [PITCHED_SCRATCH, DENSE, WIDE_FIVE, FLAT_SCRATCH],
        6 if ahead is None else 8,
    )


def call_last_grads(t, given, acts, weights, mixed, olds):
    return run(
        functools.partial(last_grads_kernel, t),
        "last_grads",
        (*given, *acts, *weights, *mixed, *olds),
        [SMEM, VMEM, VMEM, ANY] + [VMEM] * 10,
        (PACKED, FLAT, FLAT, BACK, BACK, FLAT, FLAT),
        (ANY,) * 7,
        [
            pltpu.VMEM(PACKED.shape, BF16),
            FLAT_SCRATCH,
            FLAT_SCRATCH,
            PITCHED_SCRATCH,
            PITCHED_SCRATCH,
            PAIR_SCRATCH,
            PITCHED_SCRATCH,
            DENSE,
            pltpu.VMEM((128, CH), F32),
            pltpu.SemaphoreType.DMA((9,)),
        ],
        6,
        ALONE,
    )


def call_last(kept, taps):
    (outgoing,) = run(
        last_kernel,
        "last",
        (*kept, *taps),
        [ANY] * 6 + [VMEM] * 2,
        (jax.ShapeDtypeStruct((PIXELS, 2, CH), BF16),),
        (ANY,),
        [
            FLAT_SCRATCH,
            FLAT_SCRATCH,
            PITCHED_SCRATCH,
            PITCHED_SCRATCH,
            pltpu.VMEM((1, ROWS, CH), BF16),
            pltpu.VMEM((1, ROWS, CH), BF16),
            WIDE_FIVE,
            WIDE_THREE,
            DENSE,
            FLAT_SCRATCH,
            PAIR_SCRATCH,
            pltpu.SemaphoreType.DMA((8,)),
        ],
        4,
    )
    return outgoing


def call_total(landed):
    rows = landed.shape[1]
    shapes = [(rows, CH), (rows, CH), (128, rows)]
    return pl.pallas_call(
        total_kernel,
        grid=(1,),
        out_shape=tuple(jax.ShapeDtypeStruct(shape, F32) for shape in shapes),
        in_specs=[pl.BlockSpec(landed.shape, lambda i: (0, 0, 0))],
        out_specs=tuple(pl.BlockSpec(shape, lambda i: (0, 0)) for shape in shapes),
        compiler_params=pltpu.CompilerParams(vmem_limit_bytes=12 << 20),
        name="total",
    )(landed)


def by_pixel(stack):
    return jnp.transpose(stack, (0, 2, 3, 4, 1, 5)).reshape(PIXELS, stack.shape[1], CH)


def local(
    saved_last,
    saved_older,
    arriving,
    head_adjoint,
    plan,
    depth_five,
    depth_three,
    point_five,
    point_three,
):
    turns = saved_last.shape[1]
    top = (lax.axis_index("sec") == lax.axis_size("sec") - 1).astype(jnp.int32)[None]
    slots = lax.broadcasted_iota(jnp.int32, (turns, turns), 0)
    steps = lax.broadcasted_iota(jnp.int32, (turns, turns), 1)
    turn_of_slot = jnp.sum(jnp.where(plan == slots, steps, 0), axis=1)
    turn_of_slot, top = lax.optimization_barrier((turn_of_slot, top))
    head = jnp.transpose(head_adjoint, (0, 2, 3, 4, 1, 5)).reshape(turns - 1, PIXELS, 2, CH)
    weights = (point_five[0], point_three[0])
    taps = (depth_five[0], depth_three[0])
    grad_last, grad_older, act_last, act_older, grad_out, *backs = call_first(
        turn_of_slot,
        by_pixel(saved_last),
        by_pixel(saved_older),
        by_pixel(arriving),
        weights,
        taps,
    )
    acts = (act_last, act_older)
    sums = ()
    for t in range(turns - 1):
        next_pass = from_next(grad_older)
        next_out = from_next(grad_last)
        ahead = turns - 1 if t == turns - 2 else None
        made = call_grads(t, ahead, grad_out, acts, taps, backs, sums)
        next_out, next_pass, made = lax.optimization_barrier((next_out, next_pass, made))
        sums = made[:4]
        given = (top, next_out, next_pass, head)
        if t < turns - 2:
            grad_last, grad_older, grad_out, *backs = call_middle(t + 1, given, acts, weights, taps)
    packed, *kept = call_last_grads(
        turns - 1, given, acts, weights, made[4:], sums
    )
    devices = lax.axis_size("img")
    packed = packed.reshape(devices, CH // devices, packed.shape[1])
    landed = lax.all_to_all(packed, "img", 0, 0, tiled=True)
    outgoing = call_last(kept, taps)
    five, three, tap_rows = call_total(landed)
    outgoing = outgoing.reshape(1, 1, SIDE, SIDE, 2, CH).transpose(0, 4, 1, 2, 3, 5)
    return (
        outgoing,
        five[None],
        tap_rows[:25].T[None],
        three[None],
        tap_rows[32:41].T[None],
    )


def solution(mesh):
    placed = (
        P("sec", None, "img", None, None, None),
        P("sec", None, "img", None, None, None),
        P("sec", None, "img", None, None, None),
        P(None, None, "img", None, None, None),
        P("sec", None),
        P("sec", None, None),
        P("sec", None, None),
        P("sec", None, None),
        P("sec", None, None),
    )
    return jax.shard_map(
        local,
        mesh=mesh,
        in_specs=placed,
        out_specs=(
            P("sec", None, "img", None, None, None),
            P("sec", "img", None),
            P("sec", "img", None),
            P("sec", "img", None),
            P("sec", "img", None),
        ),
        check_vma=False,
    )
```

time: 119 us -> 97.6 us (0.82)
  blocking collectives: 20.8 us -> 0 us
  starting transfers between devices: 21.9 us -> 28.7 us
  waiting for transfers between devices: 12.5 us -> 6.25 us
  Pallas kernels: 53.3 us -> 48.5 us
  local copies, waits for them, and re-layouts: 7.88 us -> 11.8 us
    all_to_all x1 -> x0, blocking collectives: 20.8 us -> none  [local(): landed = lax.all_to_all(packed, 'img', 0, 0, tiled=True)]
    ppermute x6, waiting for transfers between devices: 12.5 us -> 0.2 us  [from_next(): return lax.ppermute(block, 'sec', [(i + 1, i) for i in range(size - 1)])]
    all_to_all x0 -> x1, starting transfers between devices: none -> 7.3 us  [local(): landed = lax.all_to_all(packed, 'img', 0, 0, tiled=True)]
    all_to_all x0 -> x1, waiting for transfers between devices: none -> 6.05 us  [local(): landed = lax.all_to_all(packed, 'img', 0, 0, tiled=True)]
    unnamed x24 -> x30, local copies, waits for them, and re-layouts: 7.01 us -> 11.8 us
    pallas_call x9, Pallas kernels: 53.3 us -> 48.5 us  [the longest x8 47.8 us: run(): pl.pallas_call(kernel, out_shape=tuple(shapes), in_specs=specs, out_specs...]
  transfers between devices with their start and end apart: 6 -> 7, of which waited for: 4 -> 2; matrix products, arithmetic and copies ran while one was open for 0% -> 0% of each run, Pallas kernels for 18% -> 27%
where the time goes in v1:
time: 97.6 us; the launch traced here: 96.9 us
  Pallas kernels  48.5 us (50%)
  starting transfers between devices  28.7 us (29%)
  local copies, waits for them, and re-layouts  11.8 us (12%)
  waiting for transfers between devices  6.25 us (6%)
    pallas_call x8, Pallas kernels, run(): pl.pallas_call(kernel, out_shape=tuple(shapes), in_specs=specs, out_specs...  47.8 us
    ppermute x6, starting transfers between devices, from_next(): return lax.ppermute(block, 'sec', [(i + 1, i) for i in range(size - 1)])  21.4 us
    unnamed x30, local copies, waits for them, and re-layouts  11.8 us
    all_to_all x1, starting transfers between devices, local(): landed = lax.all_to_all(packed, 'img', 0, 0, tiled=True)  7.3 us
    all_to_all x1, waiting for transfers between devices, local(): landed = lax.all_to_all(packed, 'img', 0, 0, tiled=True)  6.05 us
  transfers between devices with their start and end apart: 7, of which 2 were waited for; matrix products, arithmetic and copies ran while one was open for 0% of the time, Pallas kernels for 27%

profile of v1, /device:TPU:32, one launch (start us, length us, event | category | flops | bytes accessed | tf_op | source)
XLA Modules:
  0.0 96.9 jit_solution(9943101675149966355)
XLA Ops:
  0.6 0.8 select_reduce_fusion.turn_ref
  1.4 0.0 copy-start.1
  1.4 1.3 %copy-done.1 = bf16[1,4,1,21,21,384]{5,1,4,3,2,0:T(4,128)(2,1)S(1)} copy-done((bf16[1,4,1,21,21,384]{5,1,4,3,2,0:T(4,128)(2,1)S(1)}, bf16[1,4,1,21,21,384]{5,1,4,3,2,0:T(4,128)(2,1)}, u32[]{:S(2)}) %copy-start.1) | copy-done | bytes 1354776
  2.7 0.0 copy-start.2
  2.7 1.3 %copy-done.2 = bf16[1,4,1,21,21,384]{5,1,4,3,2,0:T(4,128)(2,1)S(1)} copy-done((bf16[1,4,1,21,21,384]{5,1,4,3,2,0:T(4,128)(2,1)S(1)}, bf16[1,4,1,21,21,384]{5,1,4,3,2,0:T(4,128)(2,1)}, u32[]{:S(2)}) %copy-start.2) | copy-done | bytes 1354776
  4.1 0.0 copy-start.3
  4.1 1.1 %copy-done.3 = bf16[1,2,1,21,21,384]{5,1,4,3,2,0:T(2,128)(2,1)S(1)} copy-done((bf16[1,2,1,21,21,384]{5,1,4,3,2,0:T(2,128)(2,1)S(1)}, bf16[1,2,1,21,21,384]{5,1,4,3,2,0:T(2,128)(2,1)}, u32[]{:S(2)}) %copy-start.3) | copy-done | bytes 677400
  5.2 0.0 copy-start.4
  5.2 1.0 copy-done.4
  6.1 1.0 copy-done.5
  7.1 0.0 copy-start.6
  7.1 0.7 copy-done.6
  7.8 0.7 copy-done.8
  8.5 7.1 %first.1 = (bf16[448,384]{1,0:T(8,128)(2,1)S(1)}, bf16[448,384]{1,0:T(8,128)(2,1)S(1)}, bf16[4,448,384]{2,1,0:T(8,128)(2,1)S(1)}, bf16[4,448,384]{2,1,0:T(8,128)...) custom-call(s32[4]{0:T(128)S(1)} %select_reduce_fusion.turn_ref, ...), custom_call_target="tpu_custom_call" | custom-call | flops 8000000000 | tf_op jit(solution)/shard_map/first/pallas_call | solution.py:618
  15.6 3.7 %collective-permute-start = (bf16[448,384]{1,0:T(8,128)(2,1)S(1)}, bf16[448,384]{1,0:T(8,128)(2,1)S(1)}, u32[]{:S(2)}, u32[]{:S(2)}) collective-permute-start(bf16[448,384]{1,0:T(8,128)(2,1)S(1)} %get-tuple-element.70), channel_id=1, source_target_pairs={{8,0},{16,8},{24,16},{32,24},{40,32},{48,40},{56,48},{64,56},{72,6... | collective-permute-start | bytes 1032200 | tf_op jit(solution)/shard_map/ppermute | solution.py:24
  19.3 2.6 %collective-permute-start.1 = (bf16[448,384]{1,0:T(8,128)(2,1)S(1)}, bf16[448,384]{1,0:T(8,128)(2,1)S(1)}, u32[]{:S(2)}, u32[]{:S(2)}) collective-permute-start(bf16[448,384]{1,0:T(8,128)(2,1)S(1)} %get-tuple-element.71), channel_id=1, source_target_pairs={{8,0},{16,8},{24,16},{32,24},{40,32},{48,40},{56,48},{64,56},{72,6... | collective-permute-start | bytes 1032200 | tf_op jit(solution)/shard_map/ppermute | solution.py:24
  21.8 0.0 copy-start
  21.9 6.3 %grads_0.1 = (f32[384,384]{1,0:T(8,128)S(1)}, f32[32,384]{1,0:T(8,128)S(1)}, f32[384,384]{1,0:T(8,128)S(1)}, f32[16,384]{1,0:T(8,128)S(1)}) custom-call(bf16[448,384]{1,0:T(8,128)(2,1)S(1)} %get-tuple-element.72.refs_0_, bf16[4,448,384]{2,1,0:T(8,128)(2,1)S(1)} %get-tuple-element.73.refs_1_.act_last, ...), custom_call_target="tpu_custom_call" | custom-call | flops 6000000000 | tf_op jit(solution)/shard_map/grads_0/pallas_call | solution.py:618
  28.2 0.0 collective-permute-done.out_in
  28.2 0.0 collective-permute-done.1.pass_in
  28.2 0.0 copy-done
  28.2 3.7 %middle_1.1 = (bf16[448,384]{1,0:T(8,128)(2,1)S(1)}, bf16[448,384]{1,0:T(8,128)(2,1)S(1)}, bf16[448,384]{1,0:T(8,128)(2,1)S(1)}, f32[3,616,128]{2,1,0:T(8,128)S(1)}, f32[3,616,128]{2,1,0:T(8,128)S(1)}) custom-call(s32[1]{0:T(128)} %bitcast.1.top_ref, bf16[448,384]{1,0:T(8,128)(2,1)S(1)} %collective-permute-done.out_in, ...), custom_call_target="tpu_custom_call" | custom-call | flops 5000000000 | tf_op jit(solution)/shard_map/middle_1/pallas_call | solution.py:618
  31.9 5.4 %collective-permute-start.2 = (bf16[448,384]{1,0:T(8,128)(2,1)S(1)}, bf16[448,384]{1,0:T(8,128)(2,1)S(1)}, u32[]{:S(2)}, u32[]{:S(2)}) collective-permute-start(bf16[448,384]{1,0:T(8,128)(2,1)S(1)} %get-tuple-element.83), channel_id=1, source_target_pairs={{8,0},{16,8},{24,16},{32,24},{40,32},{48,40},{56,48},{64,56},{72,6... | collective-permute-start | bytes 1032200 | tf_op jit(solution)/shard_map/ppermute | solution.py:24
  37.3 1.9 %collective-permute-start.3 = (bf16[448,384]{1,0:T(8,128)(2,1)S(1)}, bf16[448,384]{1,0:T(8,128)(2,1)S(1)}, u32[]{:S(2)}, u32[]{:S(2)}) collective-permute-start(bf16[448,384]{1,0:T(8,128)(2,1)S(1)} %get-tuple-element.84), channel_id=1, source_target_pairs={{8,0},{16,8},{24,16},{32,24},{40,32},{48,40},{56,48},{64,56},{72,6... | collective-permute-start | bytes 1032200 | tf_op jit(solution)/shard_map/ppermute | solution.py:24
  39.3 6.3 %grads_1.1 = (f32[384,384]{1,0:T(8,128)S(1)}, f32[32,384]{1,0:T(8,128)S(1)}, f32[384,384]{1,0:T(8,128)S(1)}, f32[16,384]{1,0:T(8,128)S(1)}) custom-call(bf16[448,384]{1,0:T(8,128)(2,1)S(1)} %get-tuple-element.85.refs_0_, bf16[4,448,384]{2,1,0:T(8,128)(2,1)S(1)} %get-tuple-element.73.refs_1_.act_last, ...), custom_call_target="tpu_custom_call" | custom-call | flops 6000000000 | tf_op jit(solution)/shard_map/grads_1/pallas_call | solution.py:618
  45.6 0.0 collective-permute-done.2.out_in
  45.6 0.2 collective-permute-done.3.pass_in
  45.8 3.7 %middle_2.1 = (bf16[448,384]{1,0:T(8,128)(2,1)S(1)}, bf16[448,384]{1,0:T(8,128)(2,1)S(1)}, bf16[448,384]{1,0:T(8,128)(2,1)S(1)}, f32[3,616,128]{2,1,0:T(8,128)S(1)}, f32[3,616,128]{2,1,0:T(8,128)S(1)}) custom-call(s32[1]{0:T(128)} %bitcast.1.top_ref, bf16[448,384]{1,0:T(8,128)(2,1)S(1)} %collective-permute-done.2.out_in, ...), custom_call_target="tpu_custom_call" | custom-call | flops 5000000000 | tf_op jit(solution)/shard_map/middle_2/pallas_call | solution.py:618
  49.5 5.9 %collective-permute-start.4 = (bf16[448,384]{1,0:T(8,128)(2,1)S(1)}, bf16[448,384]{1,0:T(8,128)(2,1)S(1)}, u32[]{:S(2)}, u32[]{:S(2)}) collective-permute-start(bf16[448,384]{1,0:T(8,128)(2,1)S(1)} %get-tuple-element.98), channel_id=1, source_target_pairs={{8,0},{16,8},{24,16},{32,24},{40,32},{48,40},{56,48},{64,56},{72,6... | collective-permute-start | bytes 1032200 | tf_op jit(solution)/shard_map/ppermute | solution.py:24
  55.4 1.9 %collective-permute-start.5 = (bf16[448,384]{1,0:T(8,128)(2,1)S(1)}, bf16[448,384]{1,0:T(8,128)(2,1)S(1)}, u32[]{:S(2)}, u32[]{:S(2)}) collective-permute-start(bf16[448,384]{1,0:T(8,128)(2,1)S(1)} %get-tuple-element.99), channel_id=1, source_target_pairs={{8,0},{16,8},{24,16},{32,24},{40,32},{48,40},{56,48},{64,56},{72,6... | collective-permute-start | bytes 1032200 | tf_op jit(solution)/shard_map/ppermute | solution.py:24
  57.3 9.2 %grads_2.1 = (f32[384,384]{1,0:T(8,128)S(1)}, f32[32,384]{1,0:T(8,128)S(1)}, f32[384,384]{1,0:T(8,128)S(1)}, f32[16,384]{1,0:T(8,128)S(1)}, bf16[448,384]{1,0:T(8,128)(2,1)S(1)}, /*index=5*/bf16[448,384]{1,0:T(8,128)(2,1)S(1)}) custom-call(bf16[448,384]{1,0:T(8,128)(2,1)S(1)} %get-tuple-element.100.refs_0_, ...), custom_call_target="tpu_custom_call" | custom-call | flops 8000000000 | tf_op jit(solution)/shard_map/grads_2/pallas_call | solution.py:618
  66.5 0.0 collective-permute-done.4.out_in
  66.5 0.0 collective-permute-done.5.pass_in
  66.6 6.8 %last_grads.1 = (bf16[384,896]{1,0:T(8,128)(2,1)}, bf16[448,384]{1,0:T(8,128)(2,1)S(1)}, bf16[448,384]{1,0:T(8,128)(2,1)S(1)}, f32[3,616,128]{2,1,0:T(8,128)S(1)...) custom-call(s32[1]{0:T(128)} %bitcast.1.top_ref, ...), custom_call_target="tpu_custom_call" | custom-call | flops 6000000000 | tf_op jit(solution)/shard_map/last_grads/pallas_call | solution.py:618
  73.3 0.0 copy-start.10
  73.3 0.7 copy-done.10
  74.0 0.7 copy-done.12
  74.8 7.3 %all-to-all-start = ((bf16[8,48,896]{2,1,0:T(8,128)(2,1)}), bf16[8,48,896]{2,1,0:T(8,128)(2,1)S(1)}, u32[]{:S(2)}, u32[]{:S(2)}) async-start(bf16[8,48,896]{2,1,0:T(8,128)(2,1)} %bitcast.16), calls=%async_computation | async-start | bytes 1376256 | tf_op jit(solution)/shard_map/all_to_all | solution.py:803
  82.1 0.0 copy-done.7
  82.1 0.0 copy-done.9
  82.1 0.0 copy-start.11
  82.1 1.0 %copy-done.11 = bf16[448,384]{1,0:T(8,128)(2,1)S(1)} copy-done((bf16[448,384]{1,0:T(8,128)(2,1)S(1)}, bf16[448,384]{1,0:T(8,128)(2,1)}, u32[]{:S(2)}) %copy-start.11) | copy-done | bytes 344088
  83.1 1.0 %copy-done.13 = bf16[448,384]{1,0:T(8,128)(2,1)S(1)} copy-done((bf16[448,384]{1,0:T(8,128)(2,1)S(1)}, bf16[448,384]{1,0:T(8,128)(2,1)}, u32[]{:S(2)}) %copy-start.13) | copy-done | bytes 344088
  84.1 4.8 %last.1 = bf16[441,2,384]{2,1,0:T(2,128)(2,1)} custom-call(bf16[448,384]{1,0:T(8,128)(2,1)S(1)} %get-tuple-element.121.grad_out_hbm, bf16[448,384]{1,0:T(8,128)(2,1)S(1)} %get-tuple-element.122.grad_pass_hbm, f32[3,616,128]{2,1,0:T(8,128)S(1)} %get-tuple-element.123.back_five_hbm, f32[3,616,128]{2,1,0:T(8,128)S(1)} %get-tuple-element.124.back_three_hbm, ...), custom_call_target="tpu_custom_call" | custom-call | flops 4000000000 | tf_op jit(solution)/shard_map/last/pallas_call | solution.py:618
  88.9 6.0 %all-to-all-done.landed = bf16[8,48,896]{2,1,0:T(8,128)(2,1)S(1)} async-done(((bf16[8,48,896]{2,1,0:T(8,128)(2,1)}), bf16[8,48,896]{2,1,0:T(8,128)(2,1)S(1)}, u32[]{:S(2)}, u32[]{:S(2)}) %all-to-all-start) | async-done | bytes 688160 | tf_op jit(solution)/shard_map/all_to_all | solution.py:803
  94.9 0.7 total.1
  95.7 0.6 copy.16
  96.3 0.6 copy.17
  (8 shorter events, 0.0 us)
Async XLA Ops:
  1.4 1.3 %copy-start.1 = (bf16[1,4,1,21,21,384]{5,1,4,3,2,0:T(4,128)(2,1)S(1)}, bf16[1,4,1,21,21,384]{5,1,4,3,2,0:T(4,128)(2,1)}, u32[]{:S(2)}) copy-start(bf16[1,4,1,21,21,384]{5,1,4,3,2,0:T(4,128)(2,1)} %param.9) | copy-start | bytes 4064260
  2.7 1.3 %copy-start.2 = (bf16[1,4,1,21,21,384]{5,1,4,3,2,0:T(4,128)(2,1)S(1)}, bf16[1,4,1,21,21,384]{5,1,4,3,2,0:T(4,128)(2,1)}, u32[]{:S(2)}) copy-start(bf16[1,4,1,21,21,384]{5,1,4,3,2,0:T(4,128)(2,1)} %param.10) | copy-start | bytes 4064260
  4.1 1.1 %copy-start.3 = (bf16[1,2,1,21,21,384]{5,1,4,3,2,0:T(2,128)(2,1)S(1)}, bf16[1,2,1,21,21,384]{5,1,4,3,2,0:T(2,128)(2,1)}, u32[]{:S(2)}) copy-start(bf16[1,2,1,21,21,384]{5,1,4,3,2,0:T(2,128)(2,1)} %param.11) | copy-start | bytes 2032132
  5.2 1.0 copy-start.4
  6.1 1.0 copy-start.5
  7.1 0.7 copy-start.6
  7.8 0.7 copy-start.8
  15.6 12.6 %collective-permute-start = (bf16[448,384]{1,0:T(8,128)(2,1)S(1)}, bf16[448,384]{1,0:T(8,128)(2,1)S(1)}, u32[]{:S(2)}, u32[]{:S(2)}) collective-permute-start(bf16[448,384]{1,0:T(8,128)(2,1)S(1)} %get-tuple-element.70), channel_id=1, source_target_pairs={{8,0},{16,8},{24,16},{32,24},{40,32},{48,40},{56,48},{64,56},{72,6... | collective-permute-start | bytes 1032200 | tf_op jit(solution)/shard_map/ppermute | solution.py:24
  19.3 8.9 %collective-permute-start.1 = (bf16[448,384]{1,0:T(8,128)(2,1)S(1)}, bf16[448,384]{1,0:T(8,128)(2,1)S(1)}, u32[]{:S(2)}, u32[]{:S(2)}) collective-permute-start(bf16[448,384]{1,0:T(8,128)(2,1)S(1)} %get-tuple-element.71), channel_id=1, source_target_pairs={{8,0},{16,8},{24,16},{32,24},{40,32},{48,40},{56,48},{64,56},{72,6... | collective-permute-start | bytes 1032200 | tf_op jit(solution)/shard_map/ppermute | solution.py:24
  21.8 6.3 %copy-start = (bf16[3,2,1,21,21,384]{5,1,4,3,2,0:T(2,128)(2,1)S(1)}, bf16[3,2,1,21,21,384]{5,1,4,3,2,0:T(2,128)(2,1)}, u32[]{:S(2)}) copy-start(bf16[3,2,1,21,21,384]{5,1,4,3,2,0:T(2,128)(2,1)} %param.12) | copy-start | bytes 6096388
  31.9 13.7 %collective-permute-start.2 = (bf16[448,384]{1,0:T(8,128)(2,1)S(1)}, bf16[448,384]{1,0:T(8,128)(2,1)S(1)}, u32[]{:S(2)}, u32[]{:S(2)}) collective-permute-start(bf16[448,384]{1,0:T(8,128)(2,1)S(1)} %get-tuple-element.83), channel_id=1, source_target_pairs={{8,0},{16,8},{24,16},{32,24},{40,32},{48,40},{56,48},{64,56},{72,6... | collective-permute-start | bytes 1032200 | tf_op jit(solution)/shard_map/ppermute | solution.py:24
  37.3 8.4 %collective-permute-start.3 = (bf16[448,384]{1,0:T(8,128)(2,1)S(1)}, bf16[448,384]{1,0:T(8,128)(2,1)S(1)}, u32[]{:S(2)}, u32[]{:S(2)}) collective-permute-start(bf16[448,384]{1,0:T(8,128)(2,1)S(1)} %get-tuple-element.84), channel_id=1, source_target_pairs={{8,0},{16,8},{24,16},{32,24},{40,32},{48,40},{56,48},{64,56},{72,6... | collective-permute-start | bytes 1032200 | tf_op jit(solution)/shard_map/ppermute | solution.py:24
  49.5 17.1 %collective-permute-start.4 = (bf16[448,384]{1,0:T(8,128)(2,1)S(1)}, bf16[448,384]{1,0:T(8,128)(2,1)S(1)}, u32[]{:S(2)}, u32[]{:S(2)}) collective-permute-start(bf16[448,384]{1,0:T(8,128)(2,1)S(1)} %get-tuple-element.98), channel_id=1, source_target_pairs={{8,0},{16,8},{24,16},{32,24},{40,32},{48,40},{56,48},{64,56},{72,6... | collective-permute-start | bytes 1032200 | tf_op jit(solution)/shard_map/ppermute | solution.py:24
  55.4 11.1 %collective-permute-start.5 = (bf16[448,384]{1,0:T(8,128)(2,1)S(1)}, bf16[448,384]{1,0:T(8,128)(2,1)S(1)}, u32[]{:S(2)}, u32[]{:S(2)}) collective-permute-start(bf16[448,384]{1,0:T(8,128)(2,1)S(1)} %get-tuple-element.99), channel_id=1, source_target_pairs={{8,0},{16,8},{24,16},{32,24},{40,32},{48,40},{56,48},{64,56},{72,6... | collective-permute-start | bytes 1032200 | tf_op jit(solution)/shard_map/ppermute | solution.py:24
  73.3 0.7 copy-start.10
  74.0 0.7 copy-start.12
  74.8 7.3 %copy-start.7 = (bf16[1,25,384]{2,1,0:T(8,128)(2,1)S(1)}, bf16[1,25,384]{2,1,0:T(8,128)(2,1)}, u32[]{:S(2)}) copy-start(bf16[1,25,384]{2,1,0:T(8,128)(2,1)} %param.14) | copy-start | bytes 57604
  74.8 7.3 %copy-start.9 = (bf16[1,9,384]{2,1,0:T(8,128)(2,1)S(1)}, bf16[1,9,384]{2,1,0:T(8,128)(2,1)}, u32[]{:S(2)}) copy-start(bf16[1,9,384]{2,1,0:T(8,128)(2,1)} %param.15) | copy-start | bytes 20740
  74.8 20.1 %all-to-all-start = ((bf16[8,48,896]{2,1,0:T(8,128)(2,1)}), bf16[8,48,896]{2,1,0:T(8,128)(2,1)S(1)}, u32[]{:S(2)}, u32[]{:S(2)}) async-start(bf16[8,48,896]{2,1,0:T(8,128)(2,1)} %bitcast.16), calls=%async_computation | async-start | bytes 1376256 | tf_op jit(solution)/shard_map/all_to_all | solution.py:803
  82.1 1.0 %copy-start.11 = (bf16[448,384]{1,0:T(8,128)(2,1)S(1)}, bf16[448,384]{1,0:T(8,128)(2,1)}, u32[]{:S(2)}) copy-start(bf16[448,384]{1,0:T(8,128)(2,1)} %copy-done.10) | copy-start | bytes 1032196
  83.1 1.0 %copy-start.13 = (bf16[448,384]{1,0:T(8,128)(2,1)S(1)}, bf16[448,384]{1,0:T(8,128)(2,1)}, u32[]{:S(2)}) copy-start(bf16[448,384]{1,0:T(8,128)(2,1)} %copy-done.12) | copy-start | bytes 1032196

commit v2 on v1

--- a/solution.py
+++ b/solution.py
@@ -170,127 +170,64 @@
     lax.fori_loop(0, ROWS // 16, body, 0)
 
 
-def copies(pairs, sems):
-    return [pltpu.make_async_copy(a, b, sems.at[n]) for n, (a, b) in enumerate(pairs)]
-
-
-def relay(
-    t,
-    grad_out,
-    grad_pass,
-    act_last,
-    act_older,
-    weight_five,
-    weight_three,
-    taps_five,
-    taps_three,
-    back_five,
-    back_three,
-    made_last,
-    made_older,
-    wide_five,
-    wide_three,
-    dense,
-    older_ready,
-    last_ready,
-):
-    spread_taps(taps_five, wide_five, 25)
-    spread_taps(taps_three, wide_three, 9)
-    left = grad_out[...]
-    dense_product(left, weight_three, dense)
-    to_pitched(dense, back_three)
-    spread_conv(back_three, wide_three, dense, 3, True)
-    older_ready()
-    finish_older(act_older, t, dense, made_older)
-    dense_product(left, weight_five, dense)
-    to_pitched(dense, back_five)
-    spread_conv(back_five, wide_five, dense, 5, True)
-    last_ready()
-    finish_last(act_last, t, dense, grad_out, grad_pass, made_last)
-
-
-def first_kernel(
-    turn_ref,
-    last_hbm,
-    older_hbm,
-    arriving_hbm,
-    weight_five,
-    weight_three,
-    taps_five,
-    taps_three,
-    grad_last,
-    grad_older,
-    act_last,
-    act_older,
-    grad_out,
-    back_five,
-    back_three,
-    last_in,
-    older_in,
-    arriving_in,
-    grad_pass,
-    wide_five,
-    wide_three,
-    dense,
-    sems,
-):
-    half = 224
-    gets = copies(
-        [
-            (arriving_hbm.at[0:half], arriving_in.at[0:half]),
-            (arriving_hbm.at[half:], arriving_in.at[half:]),
-            (older_hbm.at[0:half], older_in.at[0:half]),
-            (older_hbm.at[half:], older_in.at[half:]),
-            (last_hbm.at[0:half], last_in.at[0:half]),
-            (last_hbm.at[half:], last_in.at[half:]),
-        ],
-        sems,
-    )
-    for get in gets:
-        get.start()
-
-    def put_pair(at, block):
+def three_part(t, grad_out, act_older, weight, taps, back, grad_older, wide, dense, ready):
+    spread_taps(taps, wide, 9)
+    dense_product(grad_out[...], weight, dense)
+    to_pitched(dense, back)
+    spread_conv(back, wide, dense, 3, True)
+    ready()
+    finish_older(act_older, t, dense, grad_older)
+
+
+def five_part(t, grad_out, grad_pass, act_last, weight, taps, back, grad_last, wide, dense, ready):
+    spread_taps(taps, wide, 25)
+    dense_product(grad_out[...], weight, dense)
+    to_pitched(dense, back)
+    spread_conv(back, wide, dense, 5, True)
+    ready()
+    finish_last(act_last, t, dense, grad_out, grad_pass, grad_last)
+
+
+def order_kernel(plan_ref, turn_ref):
+    for t in range(turn_ref.shape[0]):
+        turn_ref[plan_ref[0, t]] = t
+
+
+def slots_unpacked(turn_ref, source, target):
+    def put(at, block):
+        block = jnp.maximum(block, 0)
+        for k in range(4):
+            target[turn_ref[k], pl.ds(at, 16), :] = block[k]
+
+    unpack(source, 4, put)
+
+
+def pair_unpacked(source, grad_out, grad_pass):
+    def put(at, block):
         grad_out[pl.ds(at, 16), :] = block[0]
         grad_pass[pl.ds(at, 16), :] = block[1]
 
-    gets[0].wait()
-    gets[1].wait()
-    unpack(arriving_in, 2, put_pair)
-
-    def ready(one, two, source, target):
-        def run():
-            gets[one].wait()
-            gets[two].wait()
-
-            def put(at, block):
-                block = jnp.maximum(block, 0)
-                for k in range(4):
-                    target[turn_ref[k], pl.ds(at, 16), :] = block[k]
-
-            unpack(source, 4, put)
-
-        return run
-
-    relay(
-        0,
-        grad_out,
-        grad_pass,
-        act_last,
-        act_older,
-        weight_five,
-        weight_three,
-        taps_five,
-        taps_three,
-        back_five,
-        back_three,
-        grad_last,
-        grad_older,
-        wide_five,
-        wide_three,
-        dense,
-        ready(2, 3, older_in, act_older),
-        ready(4, 5, last_in, act_last),
-    )
+    unpack(source, 2, put)
+
+
+def first_three_kernel(
+    turn_ref, older_in, arriving_in, weight, taps, grad_older, act_older, grad_out, grad_pass, back, wide, dense
+):
+    pair_unpacked(arriving_in, grad_out, grad_pass)
+
+    def ready():
+        slots_unpacked(turn_ref, older_in, act_older)
+
+    three_part(0, grad_out, act_older, weight, taps, back, grad_older, wide, dense, ready)
+
+
+def first_five_kernel(
+    turn_ref, last_in, grad_out, grad_pass, weight, taps, grad_last, act_last, back, wide, dense
+):
+    def ready():
+        slots_unpacked(turn_ref, last_in, act_last)
+
+    five_part(0, grad_out, grad_pass, act_last, weight, taps, back, grad_last, wide, dense, ready)
 
 
 def take(t, top_ref, out_in, pass_in, head_hbm, grad_out, grad_pass, head_in, sem):
@@ -299,12 +236,7 @@
         get = pltpu.make_async_copy(head_hbm.at[t - 1], head_in, sem)
         get.start()
         get.wait()
-
-        def put(at, block):
-            grad_out[pl.ds(at, 16), :] = block[0]
-            grad_pass[pl.ds(at, 16), :] = block[1]
-
-        unpack(head_in, 2, put)
+        pair_unpacked(head_in, grad_out, grad_pass)
 
     @pl.when(top_ref[0] != 1)
     def _():
@@ -312,51 +244,34 @@
         grad_pass[...] = pass_in[...]
 
 
-def middle_kernel(
+def three_kernel(
     t,
     top_ref,
     out_in,
     pass_in,
     head_hbm,
-    act_last,
     act_older,
-    weight_five,
-    weight_three,
-    taps_five,
-    taps_three,
-    grad_last,
+    weight,
+    taps,
     grad_older,
     grad_out,
-    back_five,
-    back_three,
+    grad_pass,
+    back,
     head_in,
-    grad_pass,
-    wide_five,
-    wide_three,
+    wide,
     dense,
     sem,
 ):
     take(t, top_ref, out_in, pass_in, head_hbm, grad_out, grad_pass, head_in, sem)
-    relay(
-        t,
-        grad_out,
-        grad_pass,
-        act_last,
-        act_older,
-        weight_five,
-        weight_three,
-        taps_five,
-        taps_three,
-        back_five,
-        back_three,
-        grad_last,
-        grad_older,
-        wide_five,
-        wide_three,
-        dense,
-        lambda: None,
-        lambda: None,
-    )
+    three_part(t, grad_out, act_older, weight, taps, back, grad_older, wide, dense, lambda: None)
+
+
+def five_kernel(t, grad_out, grad_pass, act_last, weight, taps, grad_last, back, wide, dense):
+    five_part(t, grad_out, grad_pass, act_last, weight, taps, back, grad_last, wide, dense, lambda: None)
+
+
+def copies(pairs, sems):
+    return [pltpu.make_async_copy(a, b, sems.at[n]) for n, (a, b) in enumerate(pairs)]
 
 
 def widened(act, t, dense):
@@ -578,7 +493,7 @@
     put[1].wait()
 
 
-def total_kernel(landed, five, three, taps):
+def total_kernel(landed, five, three, taps_five, taps_three):
     def summed(columns):
         total = landed[0, :, columns].astype(F32)
         for n in range(1, landed.shape[0]):
@@ -587,14 +502,16 @@
 
     five[...] = summed(slice(0, CH))
     three[...] = summed(slice(CH, 2 * CH))
-    taps[...] = summed(slice(2 * CH, 2 * CH + 128)).T
+    rows = summed(slice(2 * CH, 2 * CH + 128)).T
+    for taps, at in ((taps_five, 0), (taps_three, 32)):
+        for k in range(taps.shape[0]):
+            taps[k] = rows[at + k : at + k + 1, :]
 
 
 VMEM = pl.BlockSpec(memory_space=pltpu.VMEM)
 SMEM = pl.BlockSpec(memory_space=pltpu.SMEM)
 ANY = pl.BlockSpec(memory_space=pl.ANY)
 ALONE = 16 << 20
-OPENING = 32 << 20
 FLAT = jax.ShapeDtypeStruct((ROWS, CH), BF16)
 PACKED = jax.ShapeDtypeStruct((CH, 2 * CH + 128), BF16)
 ACTS = jax.ShapeDtypeStruct((4, ROWS, CH), BF16)
@@ -627,46 +544,69 @@
     )(*operands)
 
 
-def call_first(turns, last, older, arriving, weights, taps):
+def call_order(plan):
+    (turns,) = run(
+        order_kernel,
+        "order",
+        (plan,),
+        [SMEM],
+        (jax.ShapeDtypeStruct((plan.shape[1],), jnp.int32),),
+        (SMEM,),
+        [],
+        6,
+    )
+    return turns
+
+
+def call_first_three(turns, older, arriving, weight, taps):
     return run(
-        first_kernel,
-        "first",
-        (turns, last, older, arriving, *weights, *taps),
-        [SMEM, ANY, ANY, ANY] + [VMEM] * 4,
-        (FLAT, FLAT, ACTS, ACTS, FLAT, BACK, BACK),
-        (VMEM,) * 7,
-        [
-            pltpu.VMEM((PIXELS, 4, CH), BF16),
-            pltpu.VMEM((PIXELS, 4, CH), BF16),
-            PAIR_SCRATCH,
-            FLAT_SCRATCH,
-            WIDE_FIVE,
-            WIDE_THREE,
-            DENSE,
-            pltpu.SemaphoreType.DMA((6,)),
-        ],
-        8,
-        OPENING,
-    )
-
-
-def call_middle(t, given, acts, weights, taps):
+        first_three_kernel,
+        "first_three",
+        (turns, older, arriving, weight, taps),
+        [SMEM] + [VMEM] * 4,
+        (FLAT, ACTS, FLAT, FLAT, BACK),
+        (VMEM,) * 5,
+        [WIDE_THREE, DENSE],
+        4,
+    )
+
+
+def call_first_five(turns, last, grad_out, grad_pass, weight, taps):
     return run(
-        functools.partial(middle_kernel, t),
-        f"middle_{t}",
-        (*given, *acts, *weights, *taps),
-        [SMEM, VMEM, VMEM, ANY] + [VMEM] * 6,
-        (FLAT, FLAT, FLAT, BACK, BACK),
-        (VMEM,) * 5,
-        [
-            PAIR_SCRATCH,
-            FLAT_SCRATCH,
-            WIDE_FIVE,
-            WIDE_THREE,
-            DENSE,
-            pltpu.SemaphoreType.DMA,
-        ],
-        5,
+        first_five_kernel,
+        "first_five",
+        (turns, last, grad_out, grad_pass, weight, taps),
+        [SMEM] + [VMEM] * 5,
+        (FLAT, ACTS, BACK),
+        (VMEM,) * 3,
+        [WIDE_FIVE, DENSE],
+        4,
+    )
+
+
+def call_three(t, given, act, weight, taps):
+    return run(
+        functools.partial(three_kernel, t),
+        f"three_{t}",
+        (*given, act, weight, taps),
+        [SMEM, VMEM, VMEM, ANY] + [VMEM] * 3,
+        (FLAT, FLAT, FLAT, BACK),
+        (VMEM,) * 4,
+        [PAIR_SCRATCH, WIDE_THREE, DENSE, pltpu.SemaphoreType.DMA],
+        2,
+    )
+
+
+def call_five(t, grad_out, grad_pass, act, weight, taps):
+    return run(
+        functools.partial(five_kernel, t),
+        f"five_{t}",
+        (grad_out, grad_pass, act, weight, taps),
+        [VMEM] * 5,
+        (FLAT, BACK),
+        (VMEM,) * 2,
+        [WIDE_FIVE, DENSE],
+        3,
     )
 
 
@@ -737,15 +677,20 @@
     return outgoing
 
 
+def whole(shape):
+    zeros = (0,) * len(shape)
+    return pl.BlockSpec(shape, lambda i: zeros)
+
+
 def call_total(landed):
     rows = landed.shape[1]
-    shapes = [(rows, CH), (rows, CH), (128, rows)]
+    shapes = [(rows, CH), (rows, CH), (25, 1, rows), (9, 1, rows)]
     return pl.pallas_call(
         total_kernel,
         grid=(1,),
         out_shape=tuple(jax.ShapeDtypeStruct(shape, F32) for shape in shapes),
-        in_specs=[pl.BlockSpec(landed.shape, lambda i: (0, 0, 0))],
-        out_specs=tuple(pl.BlockSpec(shape, lambda i: (0, 0)) for shape in shapes),
+        in_specs=[whole(landed.shape)],
+        out_specs=tuple(whole(shape) for shape in shapes),
         compiler_params=pltpu.CompilerParams(vmem_limit_bytes=12 << 20),
         name="total",
     )(landed)
@@ -768,33 +713,35 @@
 ):
     turns = saved_last.shape[1]
     top = (lax.axis_index("sec") == lax.axis_size("sec") - 1).astype(jnp.int32)[None]
-    slots = lax.broadcasted_iota(jnp.int32, (turns, turns), 0)
-    steps = lax.broadcasted_iota(jnp.int32, (turns, turns), 1)
-    turn_of_slot = jnp.sum(jnp.where(plan == slots, steps, 0), axis=1)
+    turn_of_slot = call_order(plan)
     turn_of_slot, top = lax.optimization_barrier((turn_of_slot, top))
     head = jnp.transpose(head_adjoint, (0, 2, 3, 4, 1, 5)).reshape(turns - 1, PIXELS, 2, CH)
     weights = (point_five[0], point_three[0])
     taps = (depth_five[0], depth_three[0])
-    grad_last, grad_older, act_last, act_older, grad_out, *backs = call_first(
-        turn_of_slot,
-        by_pixel(saved_last),
-        by_pixel(saved_older),
-        by_pixel(arriving),
-        weights,
-        taps,
+    grad_older, act_older, grad_out, grad_pass, back_three = call_first_three(
+        turn_of_slot, by_pixel(saved_older), by_pixel(arriving), weights[1], taps[1]
+    )
+    next_pass = from_next(grad_older)
+    grad_last, act_last, back_five = call_first_five(
+        turn_of_slot, by_pixel(saved_last), grad_out, grad_pass, weights[0], taps[0]
     )
     acts = (act_last, act_older)
     sums = ()
     for t in range(turns - 1):
-        next_pass = from_next(grad_older)
         next_out = from_next(grad_last)
         ahead = turns - 1 if t == turns - 2 else None
-        made = call_grads(t, ahead, grad_out, acts, taps, backs, sums)
+        made = call_grads(t, ahead, grad_out, acts, taps, (back_five, back_three), sums)
         next_out, next_pass, made = lax.optimization_barrier((next_out, next_pass, made))
         sums = made[:4]
         given = (top, next_out, next_pass, head)
         if t < turns - 2:
-            grad_last, grad_older, grad_out, *backs = call_middle(t + 1, given, acts, weights, taps)
+            grad_older, grad_out, grad_pass, back_three = call_three(
+                t + 1, given, act_older, weights[1], taps[1]
+            )
+            next_pass = from_next(grad_older)
+            grad_last, back_five = call_five(
+                t + 1, grad_out, grad_pass, act_last, weights[0], taps[0]
+            )
     packed, *kept = call_last_grads(
         turns - 1, given, acts, weights, made[4:], sums
     )
@@ -802,14 +749,14 @@
     packed = packed.reshape(devices, CH // devices, packed.shape[1])
     landed = lax.all_to_all(packed, "img", 0, 0, tiled=True)
     outgoing = call_last(kept, taps)
-    five, three, tap_rows = call_total(landed)
+    five, three, tap_five, tap_three = call_total(landed)
     outgoing = outgoing.reshape(1, 1, SIDE, SIDE, 2, CH).transpose(0, 4, 1, 2, 3, 5)
     return (
         outgoing,
         five[None],
-        tap_rows[:25].T[None],
+        jnp.transpose(tap_five, (1, 2, 0)),
         three[None],
-        tap_rows[32:41].T[None],
+        jnp.transpose(tap_three, (1, 2, 0)),
     )
 
 

time: 97.6 us -> 86.6 us (0.89)
  local copies, waits for them, and re-layouts: 11.8 us -> 4.51 us
  starting transfers between devices: 28.7 us -> 25.9 us
    unnamed x30 -> x26, local copies, waits for them, and re-layouts: 11.8 us -> 4.51 us
    ppermute x6, starting transfers between devices: 21.4 us -> 18.7 us  [from_next(): return lax.ppermute(block, 'sec', [(i + 1, i) for i in range(size - 1)])]
    pallas_call x8 -> x12, Pallas kernels: 47.8 us -> 48.1 us  [run(): pl.pallas_call(kernel, out_shape=tuple(shapes), in_specs=specs, out_specs...]
  transfers between devices with their start and end apart: 7 -> 7, of which waited for: 2 -> 1; matrix products, arithmetic and copies ran while one was open for 0% -> 0% of each run, Pallas kernels for 27% -> 40%
where the time goes in v2:
time: 86.6 us; the launch traced here: 86.2 us
  Pallas kernels  48.8 us (56%)
  starting transfers between devices  25.9 us (30%)
  waiting for transfers between devices  6.07 us (7%)
  local copies, waits for them, and re-layouts  4.51 us (5%)
  between operations  0.89 us (1%)
    pallas_call x12, Pallas kernels, run(): pl.pallas_call(kernel, out_shape=tuple(shapes), in_specs=specs, out_specs...  48.1 us
    ppermute x6, starting transfers between devices, from_next(): return lax.ppermute(block, 'sec', [(i + 1, i) for i in range(size - 1)])  18.7 us
    all_to_all x1, starting transfers between devices, local(): landed = lax.all_to_all(packed, 'img', 0, 0, tiled=True)  7.19 us
    all_to_all x1, waiting for transfers between devices, local(): landed = lax.all_to_all(packed, 'img', 0, 0, tiled=True)  6.06 us
    unnamed x26, local copies, waits for them, and re-layouts  4.51 us
  transfers between devices with their start and end apart: 7, of which 1 were waited for; matrix products, arithmetic and copies ran while one was open for 0% of the time, Pallas kernels for 40%

profile of v2, /device:TPU:32, one launch (start us, length us, event | category | flops | bytes accessed | tf_op | source)
XLA Modules:
  0.0 86.2 jit_solution(14834179990521652521)
XLA Ops:
  0.6 0.0 copy-start.8
  0.6 0.6 copy-done.8
  1.3 0.0 copy-start.1
  1.3 0.0 copy-start.3
  1.3 0.0 copy-start.4
  1.3 0.0 copy-start.7
  1.3 1.1 %order.1.turn_ref = s32[4]{0:T(128)S(1)} custom-call(s32[1,4]{1,0:T(1,128)S(1)} %copy-done.8), custom_call_target="tpu_custom_call" | custom-call | flops 6000000000 | tf_op jit(solution)/shard_map/order/pallas_call | solution.py:535
  2.5 0.2 copy-done.1
  2.6 0.2 copy-done.3
  2.8 0.1 copy-done.4
  2.9 0.0 copy-done.7
  2.9 0.0 copy-start.5
  2.9 2.9 %first_three.1 = (bf16[448,384]{1,0:T(8,128)(2,1)S(1)}, bf16[4,448,384]{2,1,0:T(8,128)(2,1)S(1)}, bf16[448,384]{1,0:T(8,128)(2,1)S(1)}, bf16[448,384]{1,0:T(8,128)(2,1)S(1)}, f32[3,616,128]{2,1,0:T(8,128)S(1)}) custom-call(s32[4]{0:T(128)S(1)} %order.1.turn_ref, bf16[441,4,384]{2,1,0:T(4,128)(2,1)S(1)} %bitcast.28, bf16[441,2,384]{2,1,0:T(2,128)(2,1)S(1)} %bitcast.30, ...), custom_call_target="tpu_custom_call" | custom-call | flops 4000000000 | tf_op jit(solution)/shard_map/first_three/pallas_call | solution.py:535
  5.7 3.7 %collective-permute-start.1 = (bf16[448,384]{1,0:T(8,128)(2,1)S(1)}, bf16[448,384]{1,0:T(8,128)(2,1)S(1)}, u32[]{:S(2)}, u32[]{:S(2)}) collective-permute-start(bf16[448,384]{1,0:T(8,128)(2,1)S(1)} %get-tuple-element.77), channel_id=1, source_target_pairs={{8,0},{16,8},{24,16},{32,24},{40,32},{48,40},{56,48},{64,56},{72,6... | collective-permute-start | bytes 1032200 | tf_op jit(solution)/shard_map/ppermute | solution.py:24
  9.4 0.0 copy-done.2
  9.4 0.0 copy-done.5
  9.4 0.0 copy-done.6
  9.4 3.4 %first_five.1 = (bf16[448,384]{1,0:T(8,128)(2,1)S(1)}, bf16[4,448,384]{2,1,0:T(8,128)(2,1)S(1)}, f32[3,616,128]{2,1,0:T(8,128)S(1)}) custom-call(s32[4]{0:T(128)S(1)} %order.1.turn_ref, bf16[441,4,384]{2,1,0:T(4,128)(2,1)S(1)} %bitcast.29, bf16[448,384]{1,0:T(8,128)(2,1)S(1)} %get-tuple-element.74.grad_out.refs_0_, ...), custom_call_target="tpu_custom_call" | custom-call | flops 4000000000 | tf_op jit(solution)/shard_map/first_five/pallas_call | solution.py:535
  12.9 2.6 %collective-permute-start = (bf16[448,384]{1,0:T(8,128)(2,1)S(1)}, bf16[448,384]{1,0:T(8,128)(2,1)S(1)}, u32[]{:S(2)}, u32[]{:S(2)}) collective-permute-start(bf16[448,384]{1,0:T(8,128)(2,1)S(1)} %get-tuple-element.76), channel_id=1, source_target_pairs={{8,0},{16,8},{24,16},{32,24},{40,32},{48,40},{56,48},{64,56},{72,6... | collective-permute-start | bytes 1032200 | tf_op jit(solution)/shard_map/ppermute | solution.py:24
  15.5 0.0 copy-start
  15.5 6.3 %grads_0.1 = (f32[384,384]{1,0:T(8,128)S(1)}, f32[32,384]{1,0:T(8,128)S(1)}, f32[384,384]{1,0:T(8,128)S(1)}, f32[16,384]{1,0:T(8,128)S(1)}) custom-call(bf16[448,384]{1,0:T(8,128)(2,1)S(1)} %get-tuple-element.74.grad_out.refs_0_, bf16[4,448,384]{2,1,0:T(8,128)(2,1)S(1)} %get-tuple-element.78.refs_1_.act_last, ...), custom_call_target="tpu_custom_call" | custom-call | flops 6000000000 | tf_op jit(solution)/shard_map/grads_0/pallas_call | solution.py:535
  21.8 0.0 collective-permute-done.1.pass_in
  21.8 0.0 collective-permute-done.out_in
  21.8 0.0 copy-done
  21.8 1.4 %three_1.1 = (bf16[448,384]{1,0:T(8,128)(2,1)S(1)}, bf16[448,384]{1,0:T(8,128)(2,1)S(1)}, bf16[448,384]{1,0:T(8,128)(2,1)S(1)}, f32[3,616,128]{2,1,0:T(8,128)S(1)}) custom-call(s32[1]{0:T(128)} %bitcast.top_ref, bf16[448,384]{1,0:T(8,128)(2,1)S(1)} %collective-permute-done.out_in, bf16[448,384]{1,0:T(8,128)(2,1)S(1)} %collective-permute-done.1.pass_in, ...), custom_call_target="tpu_custom_call" | custom-call | flops 2000000000 | tf_op jit(solution)/shard_map/three_1/pallas_call | solution.py:535
  23.2 4.3 %collective-permute-start.3 = (bf16[448,384]{1,0:T(8,128)(2,1)S(1)}, bf16[448,384]{1,0:T(8,128)(2,1)S(1)}, u32[]{:S(2)}, u32[]{:S(2)}) collective-permute-start(bf16[448,384]{1,0:T(8,128)(2,1)S(1)} %get-tuple-element.91), channel_id=1, source_target_pairs={{8,0},{16,8},{24,16},{32,24},{40,32},{48,40},{56,48},{64,56},{72,6... | collective-permute-start | bytes 1032200 | tf_op jit(solution)/shard_map/ppermute | solution.py:24
  27.5 2.3 %five_1.1 = (bf16[448,384]{1,0:T(8,128)(2,1)S(1)}, f32[3,616,128]{2,1,0:T(8,128)S(1)}) custom-call(bf16[448,384]{1,0:T(8,128)(2,1)S(1)} %get-tuple-element.88.grad_out.refs_0_, bf16[448,384]{1,0:T(8,128)(2,1)S(1)} %get-tuple-element.89.grad_pass, bf16[4,448,384]{2,1,0:T(8,128)(2,1)S(1)} %get-tuple-element.78.refs_1_.act_last, bf16[384,384]{1,0:T(8,128)(2,1)S(1)} %bitcast.36, ...), custom_call_target="tpu_custom_call" | custom-call | flops 3000000000 | tf_op jit(solution)/shard_map/five_1/pallas_call | solution.py:535
  29.8 1.9 %collective-permute-start.2 = (bf16[448,384]{1,0:T(8,128)(2,1)S(1)}, bf16[448,384]{1,0:T(8,128)(2,1)S(1)}, u32[]{:S(2)}, u32[]{:S(2)}) collective-permute-start(bf16[448,384]{1,0:T(8,128)(2,1)S(1)} %get-tuple-element.90), channel_id=1, source_target_pairs={{8,0},{16,8},{24,16},{32,24},{40,32},{48,40},{56,48},{64,56},{72,6... | collective-permute-start | bytes 1032200 | tf_op jit(solution)/shard_map/ppermute | solution.py:24
  31.7 6.3 %grads_1.1 = (f32[384,384]{1,0:T(8,128)S(1)}, f32[32,384]{1,0:T(8,128)S(1)}, f32[384,384]{1,0:T(8,128)S(1)}, f32[16,384]{1,0:T(8,128)S(1)}) custom-call(bf16[448,384]{1,0:T(8,128)(2,1)S(1)} %get-tuple-element.88.grad_out.refs_0_, bf16[4,448,384]{2,1,0:T(8,128)(2,1)S(1)} %get-tuple-element.78.refs_1_.act_last, ...), custom_call_target="tpu_custom_call" | custom-call | flops 6000000000 | tf_op jit(solution)/shard_map/grads_1/pallas_call | solution.py:535
  38.1 0.0 collective-permute-done.3.pass_in
  38.1 0.0 collective-permute-done.2.out_in
  38.1 1.4 %three_2.1 = (bf16[448,384]{1,0:T(8,128)(2,1)S(1)}, bf16[448,384]{1,0:T(8,128)(2,1)S(1)}, bf16[448,384]{1,0:T(8,128)(2,1)S(1)}, f32[3,616,128]{2,1,0:T(8,128)S(1)}) custom-call(s32[1]{0:T(128)} %bitcast.top_ref, bf16[448,384]{1,0:T(8,128)(2,1)S(1)} %collective-permute-done.2.out_in, bf16[448,384]{1,0:T(8,128)(2,1)S(1)} %collective-permute-done.3.pass_in, ...), custom_call_target="tpu_custom_call" | custom-call | flops 2000000000 | tf_op jit(solution)/shard_map/three_2/pallas_call | solution.py:535
  39.4 4.3 %collective-permute-start.5 = (bf16[448,384]{1,0:T(8,128)(2,1)S(1)}, bf16[448,384]{1,0:T(8,128)(2,1)S(1)}, u32[]{:S(2)}, u32[]{:S(2)}) collective-permute-start(bf16[448,384]{1,0:T(8,128)(2,1)S(1)} %get-tuple-element.107), channel_id=1, source_target_pairs={{8,0},{16,8},{24,16},{32,24},{40,32},{48,40},{56,48},{64,56},{72,6... | collective-permute-start | bytes 1032200 | tf_op jit(solution)/shard_map/ppermute | solution.py:24
  43.8 2.3 %five_2.1 = (bf16[448,384]{1,0:T(8,128)(2,1)S(1)}, f32[3,616,128]{2,1,0:T(8,128)S(1)}) custom-call(bf16[448,384]{1,0:T(8,128)(2,1)S(1)} %get-tuple-element.104.grad_out.refs_0_, bf16[448,384]{1,0:T(8,128)(2,1)S(1)} %get-tuple-element.105.grad_pass, bf16[4,448,384]{2,1,0:T(8,128)(2,1)S(1)} %get-tuple-element.78.refs_1_.act_last, ...), custom_call_target="tpu_custom_call" | custom-call | flops 3000000000 | tf_op jit(solution)/shard_map/five_2/pallas_call | solution.py:535
  46.1 1.9 %collective-permute-start.4 = (bf16[448,384]{1,0:T(8,128)(2,1)S(1)}, bf16[448,384]{1,0:T(8,128)(2,1)S(1)}, u32[]{:S(2)}, u32[]{:S(2)}) collective-permute-start(bf16[448,384]{1,0:T(8,128)(2,1)S(1)} %get-tuple-element.106), channel_id=1, source_target_pairs={{8,0},{16,8},{24,16},{32,24},{40,32},{48,40},{56,48},{64,56},{72,6... | collective-permute-start | bytes 1032200 | tf_op jit(solution)/shard_map/ppermute | solution.py:24
  48.0 9.2 %grads_2.1 = (f32[384,384]{1,0:T(8,128)S(1)}, f32[32,384]{1,0:T(8,128)S(1)}, f32[384,384]{1,0:T(8,128)S(1)}, f32[16,384]{1,0:T(8,128)S(1)}, bf16[448,384]{1,0:T(8,128)(2,1)S(1)}, /*index=5*/bf16[448,384]{1,0:T(8,128)(2,1)S(1)}) custom-call(bf16[448,384]{1,0:T(8,128)(2,1)S(1)} %get-tuple-element.104.grad_out.refs_0_, ...), custom_call_target="tpu_custom_call" | custom-call | flops 8000000000 | tf_op jit(solution)/shard_map/grads_2/pallas_call | solution.py:535
  57.2 0.0 collective-permute-done.5.pass_in
  57.2 0.0 collective-permute-done.4.out_in
  57.2 6.7 %last_grads.1 = (bf16[384,896]{1,0:T(8,128)(2,1)}, bf16[448,384]{1,0:T(8,128)(2,1)S(1)}, bf16[448,384]{1,0:T(8,128)(2,1)S(1)}, f32[3,616,128]{2,1,0:T(8,128)S(1)...) custom-call(s32[1]{0:T(128)} %bitcast.top_ref, ...), custom_call_target="tpu_custom_call" | custom-call | flops 6000000000 | tf_op jit(solution)/shard_map/last_grads/pallas_call | solution.py:535
  64.0 0.0 copy-start.9
  64.0 0.7 copy-done.9
  64.7 0.7 copy-done.11
  65.5 7.2 %all-to-all-start = ((bf16[8,48,896]{2,1,0:T(8,128)(2,1)}), bf16[8,48,896]{2,1,0:T(8,128)(2,1)S(1)}, u32[]{:S(2)}, u32[]{:S(2)}) async-start(bf16[8,48,896]{2,1,0:T(8,128)(2,1)} %bitcast.15), calls=%async_computation | async-start | bytes 1376256 | tf_op jit(solution)/shard_map/all_to_all | solution.py:750
  72.6 1.0 %copy-done.10 = bf16[448,384]{1,0:T(8,128)(2,1)S(1)} copy-done((bf16[448,384]{1,0:T(8,128)(2,1)S(1)}, bf16[448,384]{1,0:T(8,128)(2,1)}, u32[]{:S(2)}) %copy-start.10) | copy-done | bytes 344088
  73.6 1.0 %copy-done.12 = bf16[448,384]{1,0:T(8,128)(2,1)S(1)} copy-done((bf16[448,384]{1,0:T(8,128)(2,1)S(1)}, bf16[448,384]{1,0:T(8,128)(2,1)}, u32[]{:S(2)}) %copy-start.12) | copy-done | bytes 344088
  74.6 4.8 %last.1 = bf16[441,2,384]{2,1,0:T(2,128)(2,1)} custom-call(bf16[448,384]{1,0:T(8,128)(2,1)S(1)} %get-tuple-element.128.grad_out_hbm, bf16[448,384]{1,0:T(8,128)(2,1)S(1)} %get-tuple-element.129.grad_pass_hbm, f32[3,616,128]{2,1,0:T(8,128)S(1)} %get-tuple-element.130.back_five_hbm, f32[3,616,128]{2,1,0:T(8,128)S(1)} %get-tuple-element.131.back_three_hbm, ...), custom_call_target="tpu_custom_call" | custom-call | flops 4000000000 | tf_op jit(solution)/shard_map/last/pallas_call | solution.py:535
  79.4 6.1 %all-to-all-done.landed = bf16[8,48,896]{2,1,0:T(8,128)(2,1)S(1)} async-done(((bf16[8,48,896]{2,1,0:T(8,128)(2,1)}), bf16[8,48,896]{2,1,0:T(8,128)(2,1)S(1)}, u32[]{:S(2)}, u32[]{:S(2)}) %all-to-all-start) | async-done | bytes 688160 | tf_op jit(solution)/shard_map/all_to_all | solution.py:750
  85.5 0.7 total.1
  (5 shorter events, 0.0 us)
Async XLA Ops:
  0.6 0.7 copy-start.8
  1.3 1.3 %copy-start.1 = (bf16[1,4,1,21,21,384]{5,1,4,3,2,0:T(4,128)(2,1)S(1)}, bf16[1,4,1,21,21,384]{5,1,4,3,2,0:T(4,128)(2,1)}, u32[]{:S(2)}) copy-start(bf16[1,4,1,21,21,384]{5,1,4,3,2,0:T(4,128)(2,1)} %param.10) | copy-start | bytes 4064260
  1.3 1.5 %copy-start.3 = (bf16[1,2,1,21,21,384]{5,1,4,3,2,0:T(2,128)(2,1)S(1)}, bf16[1,2,1,21,21,384]{5,1,4,3,2,0:T(2,128)(2,1)}, u32[]{:S(2)}) copy-start(bf16[1,2,1,21,21,384]{5,1,4,3,2,0:T(2,128)(2,1)} %param.11) | copy-start | bytes 2032132
  1.3 1.6 %copy-start.4 = (bf16[1,384,384]{2,1,0:T(8,128)(2,1)S(1)}, bf16[1,384,384]{2,1,0:T(8,128)(2,1)}, u32[]{:S(2)}) copy-start(bf16[1,384,384]{2,1,0:T(8,128)(2,1)} %param.17) | copy-start | bytes 884740
  1.3 1.6 %copy-start.7 = (bf16[1,9,384]{2,1,0:T(8,128)(2,1)S(1)}, bf16[1,9,384]{2,1,0:T(8,128)(2,1)}, u32[]{:S(2)}) copy-start(bf16[1,9,384]{2,1,0:T(8,128)(2,1)} %param.15) | copy-start | bytes 20740
  2.9 6.5 %copy-start.2 = (bf16[1,4,1,21,21,384]{5,1,4,3,2,0:T(4,128)(2,1)S(1)}, bf16[1,4,1,21,21,384]{5,1,4,3,2,0:T(4,128)(2,1)}, u32[]{:S(2)}) copy-start(bf16[1,4,1,21,21,384]{5,1,4,3,2,0:T(4,128)(2,1)} %param.9) | copy-start | bytes 4064260
  2.9 6.5 %copy-start.5 = (bf16[1,384,384]{2,1,0:T(8,128)(2,1)S(1)}, bf16[1,384,384]{2,1,0:T(8,128)(2,1)}, u32[]{:S(2)}) copy-start(bf16[1,384,384]{2,1,0:T(8,128)(2,1)} %param.16) | copy-start | bytes 884740
  2.9 6.5 %copy-start.6 = (bf16[1,25,384]{2,1,0:T(8,128)(2,1)S(1)}, bf16[1,25,384]{2,1,0:T(8,128)(2,1)}, u32[]{:S(2)}) copy-start(bf16[1,25,384]{2,1,0:T(8,128)(2,1)} %param.14) | copy-start | bytes 57604
  5.7 16.0 %collective-permute-start.1 = (bf16[448,384]{1,0:T(8,128)(2,1)S(1)}, bf16[448,384]{1,0:T(8,128)(2,1)S(1)}, u32[]{:S(2)}, u32[]{:S(2)}) collective-permute-start(bf16[448,384]{1,0:T(8,128)(2,1)S(1)} %get-tuple-element.77), channel_id=1, source_target_pairs={{8,0},{16,8},{24,16},{32,24},{40,32},{48,40},{56,48},{64,56},{72,6... | collective-permute-start | bytes 1032200 | tf_op jit(solution)/shard_map/ppermute | solution.py:24
  12.9 8.9 %collective-permute-start = (bf16[448,384]{1,0:T(8,128)(2,1)S(1)}, bf16[448,384]{1,0:T(8,128)(2,1)S(1)}, u32[]{:S(2)}, u32[]{:S(2)}) collective-permute-start(bf16[448,384]{1,0:T(8,128)(2,1)S(1)} %get-tuple-element.76), channel_id=1, source_target_pairs={{8,0},{16,8},{24,16},{32,24},{40,32},{48,40},{56,48},{64,56},{72,6... | collective-permute-start | bytes 1032200 | tf_op jit(solution)/shard_map/ppermute | solution.py:24
  15.5 6.3 %copy-start = (bf16[3,2,1,21,21,384]{5,1,4,3,2,0:T(2,128)(2,1)S(1)}, bf16[3,2,1,21,21,384]{5,1,4,3,2,0:T(2,128)(2,1)}, u32[]{:S(2)}) copy-start(bf16[3,2,1,21,21,384]{5,1,4,3,2,0:T(2,128)(2,1)} %param.12) | copy-start | bytes 6096388
  23.2 14.9 %collective-permute-start.3 = (bf16[448,384]{1,0:T(8,128)(2,1)S(1)}, bf16[448,384]{1,0:T(8,128)(2,1)S(1)}, u32[]{:S(2)}, u32[]{:S(2)}) collective-permute-start(bf16[448,384]{1,0:T(8,128)(2,1)S(1)} %get-tuple-element.91), channel_id=1, source_target_pairs={{8,0},{16,8},{24,16},{32,24},{40,32},{48,40},{56,48},{64,56},{72,6... | collective-permute-start | bytes 1032200 | tf_op jit(solution)/shard_map/ppermute | solution.py:24
  29.8 8.3 %collective-permute-start.2 = (bf16[448,384]{1,0:T(8,128)(2,1)S(1)}, bf16[448,384]{1,0:T(8,128)(2,1)S(1)}, u32[]{:S(2)}, u32[]{:S(2)}) collective-permute-start(bf16[448,384]{1,0:T(8,128)(2,1)S(1)} %get-tuple-element.90), channel_id=1, source_target_pairs={{8,0},{16,8},{24,16},{32,24},{40,32},{48,40},{56,48},{64,56},{72,6... | collective-permute-start | bytes 1032200 | tf_op jit(solution)/shard_map/ppermute | solution.py:24
  39.4 17.8 %collective-permute-start.5 = (bf16[448,384]{1,0:T(8,128)(2,1)S(1)}, bf16[448,384]{1,0:T(8,128)(2,1)S(1)}, u32[]{:S(2)}, u32[]{:S(2)}) collective-permute-start(bf16[448,384]{1,0:T(8,128)(2,1)S(1)} %get-tuple-element.107), channel_id=1, source_target_pairs={{8,0},{16,8},{24,16},{32,24},{40,32},{48,40},{56,48},{64,56},{72,6... | collective-permute-start | bytes 1032200 | tf_op jit(solution)/shard_map/ppermute | solution.py:24
  46.1 11.1 %collective-permute-start.4 = (bf16[448,384]{1,0:T(8,128)(2,1)S(1)}, bf16[448,384]{1,0:T(8,128)(2,1)S(1)}, u32[]{:S(2)}, u32[]{:S(2)}) collective-permute-start(bf16[448,384]{1,0:T(8,128)(2,1)S(1)} %get-tuple-element.106), channel_id=1, source_target_pairs={{8,0},{16,8},{24,16},{32,24},{40,32},{48,40},{56,48},{64,56},{72,6... | collective-permute-start | bytes 1032200 | tf_op jit(solution)/shard_map/ppermute | solution.py:24
  64.0 0.7 copy-start.9
  64.7 0.7 copy-start.11
  65.5 20.0 %all-to-all-start = ((bf16[8,48,896]{2,1,0:T(8,128)(2,1)}), bf16[8,48,896]{2,1,0:T(8,128)(2,1)S(1)}, u32[]{:S(2)}, u32[]{:S(2)}) async-start(bf16[8,48,896]{2,1,0:T(8,128)(2,1)} %bitcast.15), calls=%async_computation | async-start | bytes 1376256 | tf_op jit(solution)/shard_map/all_to_all | solution.py:750
  72.6 1.0 %copy-start.10 = (bf16[448,384]{1,0:T(8,128)(2,1)S(1)}, bf16[448,384]{1,0:T(8,128)(2,1)}, u32[]{:S(2)}) copy-start(bf16[448,384]{1,0:T(8,128)(2,1)} %copy-done.9) | copy-start | bytes 1032196
  73.6 1.0 %copy-start.12 = (bf16[448,384]{1,0:T(8,128)(2,1)S(1)}, bf16[448,384]{1,0:T(8,128)(2,1)}, u32[]{:S(2)}) copy-start(bf16[448,384]{1,0:T(8,128)(2,1)} %copy-done.11) | copy-start | bytes 1032196

commit v3 on v2

--- a/solution.py
+++ b/solution.py
@@ -57,56 +57,80 @@
     lax.fori_loop(0, SIDE, row, 0, unroll=3)
 
 
+def add_window(sums, got, weight_of, b, shift, rows, kernel):
+    radius = kernel // 2
+    for a in range(rows):
+        p = b - a
+        if p < 0 or p >= kernel:
+            continue
+        for r in range(3):
+            q = shift - r + radius
+            if q < 0 or q >= kernel:
+                continue
+            term = weight_of(p * kernel + q) * got
+            old = sums[a][r]
+            sums[a][r] = term if old is None else old + term
+
+
 def spread_conv(pitched, wide, dense, kernel, flipped):
     radius = kernel // 2
     last = kernel * kernel - 1
+    rows = 3 if kernel == 5 else 7
 
     def group(g, carry):
         for c in range(BLOCKS):
-            sums = [[None] * 3 for _ in range(3)]
-            start = EDGE + (3 * g + 2 - radius) * PITCH
-            for b in range(kernel + 2):
+            sums = [[None] * 3 for _ in range(rows)]
+            start = EDGE + (rows * g + 2 - radius) * PITCH
+            for b in range(kernel + rows - 1):
                 for shift in range(-radius, 3 + radius):
                     got = pitched[c, pl.ds(start + b * PITCH + shift, 8, stride=3), :]
-                    for a in range(3):
+                    add_window(
+                        sums,
+                        got,
+                        lambda k: wide[last - k if flipped else k, c],
+                        b,
+                        shift,
+                        rows,
+                        kernel,
+                    )
+            for a in range(rows):
+                for r in range(3):
+                    dense[c, pl.ds((rows * g + a) * SIDE + r, 8, stride=3), :] = sums[a][r]
+        return carry
+
+    lax.fori_loop(0, SIDE // rows, group, 0)
+
+
+def tap_sums(back, active, sums_ref, kernel):
+    radius = kernel // 2
+    count = kernel * kernel
+    rows = 7
+    for c in range(BLOCKS):
+
+        def group(g, sums):
+            sums = list(sums)
+            here = EDGE + (rows * g + 2) * PITCH
+            centre = [
+                [back[c, pl.ds(here + a * PITCH + r, 8, stride=3), :] for r in range(3)]
+                for a in range(rows)
+            ]
+            for b in range(kernel + rows - 1):
+                for shift in range(-radius, 3 + radius):
+                    at = here + (b - radius) * PITCH + shift
+                    got = active[c, pl.ds(at, 8, stride=3), :]
+                    for a in range(rows):
                         p = b - a
                         if p < 0 or p >= kernel:
                             continue
                         for r in range(3):
                             q = shift - r + radius
-                            if q < 0 or q >= kernel:
-                                continue
-                            k = p * kernel + q
-                            term = wide[last - k if flipped else k, c] * got
-                            old = sums[a][r]
-                            sums[a][r] = term if old is None else old + term
-            for a in range(3):
-                for r in range(3):
-                    dense[c, pl.ds((3 * g + a) * SIDE + r, 8, stride=3), :] = sums[a][r]
-        return carry
-
-    lax.fori_loop(0, SIDE // 3, group, 0)
-
-
-def tap_sums(back, active, sums_ref, kernel):
-    radius = kernel // 2
-    count = kernel * kernel
-    for c in range(BLOCKS):
-
-        def row(i, sums):
-            sums = list(sums)
-            here = EDGE + (i + 2) * PITCH
-            centre = [back[c, pl.ds(here + r, 8, stride=3), :] for r in range(3)]
-            for p in range(kernel):
-                for shift in range(-radius, 3 + radius):
-                    got = active[c, pl.ds(here + (p - radius) * PITCH + shift, 8, stride=3), :]
-                    for r in range(3):
-                        q = shift - r + radius
-                        if 0 <= q < kernel:
-                            sums[p * kernel + q] = sums[p * kernel + q] + got * centre[r]
+                            if 0 <= q < kernel:
+                                k = p * kernel + q
+                                sums[k] = sums[k] + got * centre[a][r]
             return tuple(sums)
 
-        sums = lax.fori_loop(0, SIDE, row, tuple(jnp.zeros((8, 128), F32) for _ in range(count)))
+        empty = tuple(jnp.zeros((8, 128), F32) for _ in range(count))
+        sums = lax.fori_loop(0, SIDE // rows, group, empty)
         for k in range(count):
             sums_ref[k : k + 1, lanes(c)] = jnp.sum(sums[k], axis=0, keepdims=True)
 
@@ -135,10 +159,15 @@
 
 
 def dense_product(left, weight_ref, dense):
-    for c in range(BLOCKS):
-        dense[c, 0:ROWS, :] = lax.dot_general(
-            left, weight_ref[lanes(c), :], (((1,), (1,)), ((), ())), preferred_element_type=F32
+    for first, blocks in ((0, 2), (2, 1)):
+        got = lax.dot_general(
+            left,
+            weight_ref[first * 128 : (first + blocks) * 128, :],
+            (((1,), (1,)), ((), ())),
+            preferred_element_type=F32,
         )
+        for c in range(blocks):
+            dense[first + c, 0:ROWS, :] = got[:, lanes(c)]
 
 
 def masked(act, t, dense, c, rows):
@@ -350,12 +379,8 @@
     old_three,
     old_taps_three,
     packed_hbm,
-    out_hbm,
-    pass_hbm,
-    back_five_hbm,
-    back_three_hbm,
-    last_hbm,
-    older_hbm,
+    flats_hbm,
+    backs_hbm,
     packed,
     grad_out,
     grad_pass,
@@ -370,12 +395,12 @@
     scale = 1.0 / PIXELS
     keep = copies(
         [
-            (act_last.at[t], last_hbm),
-            (act_older.at[t], older_hbm),
-            (grad_out, out_hbm),
-            (grad_pass, pass_hbm),
-            (back_five, back_five_hbm),
-            (back_three, back_three_hbm),
+            (act_last.at[t], flats_hbm.at[0]),
+            (act_older.at[t], flats_hbm.at[1]),
+            (grad_out, flats_hbm.at[2]),
+            (grad_pass, flats_hbm.at[3]),
+            (back_five, backs_hbm.at[0]),
+            (back_three, backs_hbm.at[1]),
         ],
         sems,
     )
@@ -418,12 +443,8 @@
 
 
 def last_kernel(
-    grad_out_hbm,
-    grad_pass_hbm,
-    back_five_hbm,
-    back_three_hbm,
-    act_last_hbm,
-    act_older_hbm,
+    flats_hbm,
+    backs_hbm,
     taps_five,
     taps_three,
     outgoing_hbm,
@@ -442,12 +463,12 @@
 ):
     gets = copies(
         [
-            (back_three_hbm, back_three),
-            (act_older_hbm, act_older.at[0]),
-            (back_five_hbm, back_five),
-            (act_last_hbm, act_last.at[0]),
-            (grad_out_hbm, grad_out),
-            (grad_pass_hbm, grad_pass),
+            (backs_hbm.at[1], back_three),
+            (flats_hbm.at[1], act_older.at[0]),
+            (backs_hbm.at[0], back_five),
+            (flats_hbm.at[0], act_last.at[0]),
+            (flats_hbm.at[2], grad_out),
+            (flats_hbm.at[3], grad_pass),
         ],
         sems,
     )
@@ -631,8 +652,8 @@
         "last_grads",
         (*given, *acts, *weights, *mixed, *olds),
         [SMEM, VMEM, VMEM, ANY] + [VMEM] * 10,
-        (PACKED, FLAT, FLAT, BACK, BACK, FLAT, FLAT),
-        (ANY,) * 7,
+        (PACKED, ACTS, jax.ShapeDtypeStruct((2, *BACK.shape), F32)),
+        (ANY,) * 3,
         [
             pltpu.VMEM(PACKED.shape, BF16),
             FLAT_SCRATCH,
@@ -655,7 +676,7 @@
         last_kernel,
         "last",
         (*kept, *taps),
-        [ANY] * 6 + [VMEM] * 2,
+        [ANY] * 2 + [VMEM] * 2,
         (jax.ShapeDtypeStruct((PIXELS, 2, CH), BF16),),
         (ANY,),
         [

time: 86.6 us -> 84.3 us (0.973)
  Pallas kernels: 48.8 us -> 45.4 us
  starting transfers between devices: 25.9 us -> 27.4 us
  local copies, waits for them, and re-layouts: 4.51 us -> 3.52 us
    pallas_call x12, Pallas kernels: 48.1 us -> 44.7 us  [run(): pl.pallas_call(kernel, out_shape=tuple(shapes), in_specs=specs, out_specs...]
    ppermute x6, starting transfers between devices: 18.7 us -> 20.2 us  [from_next(): return lax.ppermute(block, 'sec', [(i + 1, i) for i in range(size - 1)])]
    unnamed x26 -> x22, local copies, waits for them, and re-layouts: 4.51 us -> 3.52 us
  transfers between devices with their start and end apart: 7 -> 7, of which waited for: 1 -> 1; matrix products, arithmetic and copies ran while one was open for 0% -> 0% of each run, Pallas kernels for 40% -> 38%
where the time goes in v3:
time: 84.3 us; the launch traced here: 83.9 us
  Pallas kernels  45.4 us (54%)
  starting transfers between devices  27.4 us (33%)
  waiting for transfers between devices  6.71 us (8%)
  local copies, waits for them, and re-layouts  3.52 us (4%)
  between operations  0.88 us (1%)
    pallas_call x12, Pallas kernels, run(): pl.pallas_call(kernel, out_shape=tuple(shapes), in_specs=specs, out_specs...  44.7 us
    ppermute x6, starting transfers between devices, from_next(): return lax.ppermute(block, 'sec', [(i + 1, i) for i in range(size - 1)])  20.2 us
    all_to_all x1, starting transfers between devices, local(): landed = lax.all_to_all(packed, 'img', 0, 0, tiled=True)  7.17 us
    all_to_all x1, waiting for transfers between devices, local(): landed = lax.all_to_all(packed, 'img', 0, 0, tiled=True)  6.69 us
    unnamed x22, local copies, waits for them, and re-layouts  3.52 us
  transfers between devices with their start and end apart: 7, of which 1 were waited for; matrix products, arithmetic and copies ran while one was open for 0% of the time, Pallas kernels for 38%

profile of v3, /device:TPU:32, one launch (start us, length us, event | category | flops | bytes accessed | tf_op | source)
XLA Modules:
  0.0 83.9 jit_solution(6827834939116489623)
XLA Ops:
  0.6 0.0 copy-start.8
  0.6 0.6 copy-done.8
  1.3 0.0 copy-start.1
  1.3 0.0 copy-start.3
  1.3 0.0 copy-start.4
  1.3 0.0 copy-start.7
  1.3 1.1 %order.1.turn_ref = s32[4]{0:T(128)S(1)} custom-call(s32[1,4]{1,0:T(1,128)S(1)} %copy-done.8), custom_call_target="tpu_custom_call" | custom-call | flops 6000000000 | tf_op jit(solution)/shard_map/order/pallas_call | solution.py:556
  2.5 0.2 copy-done.1
  2.6 0.2 copy-done.3
  2.8 0.1 copy-done.4
  2.9 0.0 copy-done.7
  2.9 0.0 copy-start.2
  2.9 0.0 copy-start.5
  2.9 0.0 copy-start.6
  2.9 2.8 %first_three.1 = (bf16[448,384]{1,0:T(8,128)(2,1)S(1)}, bf16[4,448,384]{2,1,0:T(8,128)(2,1)S(1)}, bf16[448,384]{1,0:T(8,128)(2,1)S(1)}, bf16[448,384]{1,0:T(8,128)(2,1)S(1)}, f32[3,616,128]{2,1,0:T(8,128)S(1)}) custom-call(s32[4]{0:T(128)S(1)} %order.1.turn_ref, bf16[441,4,384]{2,1,0:T(4,128)(2,1)S(1)} %bitcast.28, bf16[441,2,384]{2,1,0:T(2,128)(2,1)S(1)} %bitcast.30, ...), custom_call_target="tpu_custom_call" | custom-call | flops 4000000000 | tf_op jit(solution)/shard_map/first_three/pallas_call | solution.py:556
  5.7 3.7 %collective-permute-start.1 = (bf16[448,384]{1,0:T(8,128)(2,1)S(1)}, bf16[448,384]{1,0:T(8,128)(2,1)S(1)}, u32[]{:S(2)}, u32[]{:S(2)}) collective-permute-start(bf16[448,384]{1,0:T(8,128)(2,1)S(1)} %get-tuple-element.73), channel_id=1, source_target_pairs={{8,0},{16,8},{24,16},{32,24},{40,32},{48,40},{56,48},{64,56},{72,6... | collective-permute-start | bytes 1032200 | tf_op jit(solution)/shard_map/ppermute | solution.py:24
  9.3 0.0 copy-done.2
  9.3 0.0 copy-done.5
  9.3 0.0 copy-done.6
  9.3 3.4 %first_five.1 = (bf16[448,384]{1,0:T(8,128)(2,1)S(1)}, bf16[4,448,384]{2,1,0:T(8,128)(2,1)S(1)}, f32[3,616,128]{2,1,0:T(8,128)S(1)}) custom-call(s32[4]{0:T(128)S(1)} %order.1.turn_ref, bf16[441,4,384]{2,1,0:T(4,128)(2,1)S(1)} %bitcast.29, bf16[448,384]{1,0:T(8,128)(2,1)S(1)} %get-tuple-element.70.grad_out.refs_0_, ...), custom_call_target="tpu_custom_call" | custom-call | flops 4000000000 | tf_op jit(solution)/shard_map/first_five/pallas_call | solution.py:556
  12.7 2.6 %collective-permute-start = (bf16[448,384]{1,0:T(8,128)(2,1)S(1)}, bf16[448,384]{1,0:T(8,128)(2,1)S(1)}, u32[]{:S(2)}, u32[]{:S(2)}) collective-permute-start(bf16[448,384]{1,0:T(8,128)(2,1)S(1)} %get-tuple-element.72), channel_id=1, source_target_pairs={{8,0},{16,8},{24,16},{32,24},{40,32},{48,40},{56,48},{64,56},{72,6... | collective-permute-start | bytes 1032200 | tf_op jit(solution)/shard_map/ppermute | solution.py:24
  15.3 0.0 copy-start
  15.3 5.6 %grads_0.1 = (f32[384,384]{1,0:T(8,128)S(1)}, f32[32,384]{1,0:T(8,128)S(1)}, f32[384,384]{1,0:T(8,128)S(1)}, f32[16,384]{1,0:T(8,128)S(1)}) custom-call(bf16[448,384]{1,0:T(8,128)(2,1)S(1)} %get-tuple-element.70.grad_out.refs_0_, bf16[4,448,384]{2,1,0:T(8,128)(2,1)S(1)} %get-tuple-element.74.refs_1_.act_last, ...), custom_call_target="tpu_custom_call" | custom-call | flops 6000000000 | tf_op jit(solution)/shard_map/grads_0/pallas_call | solution.py:556
  20.9 0.0 collective-permute-done.1.pass_in
  20.9 0.0 collective-permute-done.out_in
  20.9 0.0 copy-done
  20.9 1.3 %three_1.1 = (bf16[448,384]{1,0:T(8,128)(2,1)S(1)}, bf16[448,384]{1,0:T(8,128)(2,1)S(1)}, bf16[448,384]{1,0:T(8,128)(2,1)S(1)}, f32[3,616,128]{2,1,0:T(8,128)S(1)}) custom-call(s32[1]{0:T(128)} %bitcast.top_ref, bf16[448,384]{1,0:T(8,128)(2,1)S(1)} %collective-permute-done.out_in, bf16[448,384]{1,0:T(8,128)(2,1)S(1)} %collective-permute-done.1.pass_in, ...), custom_call_target="tpu_custom_call" | custom-call | flops 2000000000 | tf_op jit(solution)/shard_map/three_1/pallas_call | solution.py:556
  22.2 5.1 %collective-permute-start.3 = (bf16[448,384]{1,0:T(8,128)(2,1)S(1)}, bf16[448,384]{1,0:T(8,128)(2,1)S(1)}, u32[]{:S(2)}, u32[]{:S(2)}) collective-permute-start(bf16[448,384]{1,0:T(8,128)(2,1)S(1)} %get-tuple-element.87), channel_id=1, source_target_pairs={{8,0},{16,8},{24,16},{32,24},{40,32},{48,40},{56,48},{64,56},{72,6... | collective-permute-start | bytes 1032200 | tf_op jit(solution)/shard_map/ppermute | solution.py:24
  27.3 2.3 %five_1.1 = (bf16[448,384]{1,0:T(8,128)(2,1)S(1)}, f32[3,616,128]{2,1,0:T(8,128)S(1)}) custom-call(bf16[448,384]{1,0:T(8,128)(2,1)S(1)} %get-tuple-element.84.grad_out.refs_0_, bf16[448,384]{1,0:T(8,128)(2,1)S(1)} %get-tuple-element.85.grad_pass, bf16[4,448,384]{2,1,0:T(8,128)(2,1)S(1)} %get-tuple-element.74.refs_1_.act_last, bf16[384,384]{1,0:T(8,128)(2,1)S(1)} %bitcast.36, ...), custom_call_target="tpu_custom_call" | custom-call | flops 3000000000 | tf_op jit(solution)/shard_map/five_1/pallas_call | solution.py:556
  29.5 1.9 %collective-permute-start.2 = (bf16[448,384]{1,0:T(8,128)(2,1)S(1)}, bf16[448,384]{1,0:T(8,128)(2,1)S(1)}, u32[]{:S(2)}, u32[]{:S(2)}) collective-permute-start(bf16[448,384]{1,0:T(8,128)(2,1)S(1)} %get-tuple-element.86), channel_id=1, source_target_pairs={{8,0},{16,8},{24,16},{32,24},{40,32},{48,40},{56,48},{64,56},{72,6... | collective-permute-start | bytes 1032200 | tf_op jit(solution)/shard_map/ppermute | solution.py:24
  31.5 5.6 %grads_1.1 = (f32[384,384]{1,0:T(8,128)S(1)}, f32[32,384]{1,0:T(8,128)S(1)}, f32[384,384]{1,0:T(8,128)S(1)}, f32[16,384]{1,0:T(8,128)S(1)}) custom-call(bf16[448,384]{1,0:T(8,128)(2,1)S(1)} %get-tuple-element.84.grad_out.refs_0_, bf16[4,448,384]{2,1,0:T(8,128)(2,1)S(1)} %get-tuple-element.74.refs_1_.act_last, ...), custom_call_target="tpu_custom_call" | custom-call | flops 6000000000 | tf_op jit(solution)/shard_map/grads_1/pallas_call | solution.py:556
  37.0 0.0 collective-permute-done.3.pass_in
  37.1 0.0 collective-permute-done.2.out_in
  37.1 1.3 %three_2.1 = (bf16[448,384]{1,0:T(8,128)(2,1)S(1)}, bf16[448,384]{1,0:T(8,128)(2,1)S(1)}, bf16[448,384]{1,0:T(8,128)(2,1)S(1)}, f32[3,616,128]{2,1,0:T(8,128)S(1)}) custom-call(s32[1]{0:T(128)} %bitcast.top_ref, bf16[448,384]{1,0:T(8,128)(2,1)S(1)} %collective-permute-done.2.out_in, bf16[448,384]{1,0:T(8,128)(2,1)S(1)} %collective-permute-done.3.pass_in, ...), custom_call_target="tpu_custom_call" | custom-call | flops 2000000000 | tf_op jit(solution)/shard_map/three_2/pallas_call | solution.py:556
  38.3 5.1 %collective-permute-start.5 = (bf16[448,384]{1,0:T(8,128)(2,1)S(1)}, bf16[448,384]{1,0:T(8,128)(2,1)S(1)}, u32[]{:S(2)}, u32[]{:S(2)}) collective-permute-start(bf16[448,384]{1,0:T(8,128)(2,1)S(1)} %get-tuple-element.103), channel_id=1, source_target_pairs={{8,0},{16,8},{24,16},{32,24},{40,32},{48,40},{56,48},{64,56},{72,6... | collective-permute-start | bytes 1032200 | tf_op jit(solution)/shard_map/ppermute | solution.py:24
  43.4 2.3 %five_2.1 = (bf16[448,384]{1,0:T(8,128)(2,1)S(1)}, f32[3,616,128]{2,1,0:T(8,128)S(1)}) custom-call(bf16[448,384]{1,0:T(8,128)(2,1)S(1)} %get-tuple-element.100.grad_out.refs_0_, bf16[448,384]{1,0:T(8,128)(2,1)S(1)} %get-tuple-element.101.grad_pass, bf16[4,448,384]{2,1,0:T(8,128)(2,1)S(1)} %get-tuple-element.74.refs_1_.act_last, ...), custom_call_target="tpu_custom_call" | custom-call | flops 3000000000 | tf_op jit(solution)/shard_map/five_2/pallas_call | solution.py:556
  45.7 1.9 %collective-permute-start.4 = (bf16[448,384]{1,0:T(8,128)(2,1)S(1)}, bf16[448,384]{1,0:T(8,128)(2,1)S(1)}, u32[]{:S(2)}, u32[]{:S(2)}) collective-permute-start(bf16[448,384]{1,0:T(8,128)(2,1)S(1)} %get-tuple-element.102), channel_id=1, source_target_pairs={{8,0},{16,8},{24,16},{32,24},{40,32},{48,40},{56,48},{64,56},{72,6... | collective-permute-start | bytes 1032200 | tf_op jit(solution)/shard_map/ppermute | solution.py:24
  47.6 8.4 %grads_2.1 = (f32[384,384]{1,0:T(8,128)S(1)}, f32[32,384]{1,0:T(8,128)S(1)}, f32[384,384]{1,0:T(8,128)S(1)}, f32[16,384]{1,0:T(8,128)S(1)}, bf16[448,384]{1,0:T(8,128)(2,1)S(1)}, /*index=5*/bf16[448,384]{1,0:T(8,128)(2,1)S(1)}) custom-call(bf16[448,384]{1,0:T(8,128)(2,1)S(1)} %get-tuple-element.100.grad_out.refs_0_, ...), custom_call_target="tpu_custom_call" | custom-call | flops 8000000000 | tf_op jit(solution)/shard_map/grads_2/pallas_call | solution.py:556
  56.0 0.0 collective-permute-done.5.pass_in
  56.1 0.0 collective-permute-done.4.out_in
  56.1 6.0 %last_grads.1 = (bf16[384,896]{1,0:T(8,128)(2,1)}, bf16[4,448,384]{2,1,0:T(8,128)(2,1)S(1)}, f32[2,3,616,128]{3,2,1,0:T(8,128)S(1)}) custom-call(s32[1]{0:T(128)} %bitcast.top_ref, bf16[448,384]{1,0:T(8,128)(2,1)S(1)} %collective-permute-done.4.out_in, bf16[448,384]{1,0:T(8,128)(2,1)S(1)} %collective-permute-done.5.pass_in, ...), custom_call_target="tpu_custom_call" | custom-call | flops 6000000000 | tf_op jit(solution)/shard_map/last_grads/pallas_call | solution.py:556
  62.1 0.0 copy-start.9
  62.1 1.1 %copy-done.9 = bf16[4,448,384]{2,1,0:T(8,128)(2,1)} copy-done((bf16[4,448,384]{2,1,0:T(8,128)(2,1)}, bf16[4,448,384]{2,1,0:T(8,128)(2,1)S(1)}, u32[]{:S(2)}) %copy-start.9) | copy-done | bytes 1376280
  63.2 7.2 %all-to-all-start = ((bf16[8,48,896]{2,1,0:T(8,128)(2,1)}), bf16[8,48,896]{2,1,0:T(8,128)(2,1)S(1)}, u32[]{:S(2)}, u32[]{:S(2)}) async-start(bf16[8,48,896]{2,1,0:T(8,128)(2,1)} %bitcast.15), calls=%async_computation | async-start | bytes 1376256 | tf_op jit(solution)/shard_map/all_to_all | solution.py:771
  70.3 1.3 %copy-done.10 = bf16[4,448,384]{2,1,0:T(8,128)(2,1)S(1)} copy-done((bf16[4,448,384]{2,1,0:T(8,128)(2,1)S(1)}, bf16[4,448,384]{2,1,0:T(8,128)(2,1)}, u32[]{:S(2)}) %copy-start.10) | copy-done | bytes 1376280
  71.7 4.8 %last.1 = bf16[441,2,384]{2,1,0:T(2,128)(2,1)} custom-call(bf16[4,448,384]{2,1,0:T(8,128)(2,1)S(1)} %copy-done.10, f32[2,3,616,128]{3,2,1,0:T(8,128)S(1)} %get-tuple-element.125.backs_hbm, bf16[25,384]{1,0:T(8,128)(2,1)S(1)} %bitcast.45, bf16[9,384]{1,0:T(8,128)(2,1)S(1)} %bitcast.52), custom_call_target="tpu_custom_call" | custom-call | flops 4000000000 | tf_op jit(solution)/shard_map/last/pallas_call | solution.py:556
  76.5 6.7 %all-to-all-done.landed = bf16[8,48,896]{2,1,0:T(8,128)(2,1)S(1)} async-done(((bf16[8,48,896]{2,1,0:T(8,128)(2,1)}), bf16[8,48,896]{2,1,0:T(8,128)(2,1)S(1)}, u32[]{:S(2)}, u32[]{:S(2)}) %all-to-all-start) | async-done | bytes 688160 | tf_op jit(solution)/shard_map/all_to_all | solution.py:771
  83.2 0.7 total.1
  (1 shorter events, 0.0 us)
Async XLA Ops:
  0.6 0.7 copy-start.8
  1.3 1.3 %copy-start.1 = (bf16[1,4,1,21,21,384]{5,1,4,3,2,0:T(4,128)(2,1)S(1)}, bf16[1,4,1,21,21,384]{5,1,4,3,2,0:T(4,128)(2,1)}, u32[]{:S(2)}) copy-start(bf16[1,4,1,21,21,384]{5,1,4,3,2,0:T(4,128)(2,1)} %param.10) | copy-start | bytes 4064260
  1.3 1.5 %copy-start.3 = (bf16[1,2,1,21,21,384]{5,1,4,3,2,0:T(2,128)(2,1)S(1)}, bf16[1,2,1,21,21,384]{5,1,4,3,2,0:T(2,128)(2,1)}, u32[]{:S(2)}) copy-start(bf16[1,2,1,21,21,384]{5,1,4,3,2,0:T(2,128)(2,1)} %param.11) | copy-start | bytes 2032132
  1.3 1.6 %copy-start.4 = (bf16[1,384,384]{2,1,0:T(8,128)(2,1)S(1)}, bf16[1,384,384]{2,1,0:T(8,128)(2,1)}, u32[]{:S(2)}) copy-start(bf16[1,384,384]{2,1,0:T(8,128)(2,1)} %param.17) | copy-start | bytes 884740
  1.3 1.6 %copy-start.7 = (bf16[1,9,384]{2,1,0:T(8,128)(2,1)S(1)}, bf16[1,9,384]{2,1,0:T(8,128)(2,1)}, u32[]{:S(2)}) copy-start(bf16[1,9,384]{2,1,0:T(8,128)(2,1)} %param.15) | copy-start | bytes 20740
  2.9 6.4 %copy-start.2 = (bf16[1,4,1,21,21,384]{5,1,4,3,2,0:T(4,128)(2,1)S(1)}, bf16[1,4,1,21,21,384]{5,1,4,3,2,0:T(4,128)(2,1)}, u32[]{:S(2)}) copy-start(bf16[1,4,1,21,21,384]{5,1,4,3,2,0:T(4,128)(2,1)} %param.9) | copy-start | bytes 4064260
  2.9 6.5 %copy-start.5 = (bf16[1,384,384]{2,1,0:T(8,128)(2,1)S(1)}, bf16[1,384,384]{2,1,0:T(8,128)(2,1)}, u32[]{:S(2)}) copy-start(bf16[1,384,384]{2,1,0:T(8,128)(2,1)} %param.16) | copy-start | bytes 884740
  2.9 6.5 %copy-start.6 = (bf16[1,25,384]{2,1,0:T(8,128)(2,1)S(1)}, bf16[1,25,384]{2,1,0:T(8,128)(2,1)}, u32[]{:S(2)}) copy-start(bf16[1,25,384]{2,1,0:T(8,128)(2,1)} %param.14) | copy-start | bytes 57604
  5.7 15.3 %collective-permute-start.1 = (bf16[448,384]{1,0:T(8,128)(2,1)S(1)}, bf16[448,384]{1,0:T(8,128)(2,1)S(1)}, u32[]{:S(2)}, u32[]{:S(2)}) collective-permute-start(bf16[448,384]{1,0:T(8,128)(2,1)S(1)} %get-tuple-element.73), channel_id=1, source_target_pairs={{8,0},{16,8},{24,16},{32,24},{40,32},{48,40},{56,48},{64,56},{72,6... | collective-permute-start | bytes 1032200 | tf_op jit(solution)/shard_map/ppermute | solution.py:24
  12.7 8.2 %collective-permute-start = (bf16[448,384]{1,0:T(8,128)(2,1)S(1)}, bf16[448,384]{1,0:T(8,128)(2,1)S(1)}, u32[]{:S(2)}, u32[]{:S(2)}) collective-permute-start(bf16[448,384]{1,0:T(8,128)(2,1)S(1)} %get-tuple-element.72), channel_id=1, source_target_pairs={{8,0},{16,8},{24,16},{32,24},{40,32},{48,40},{56,48},{64,56},{72,6... | collective-permute-start | bytes 1032200 | tf_op jit(solution)/shard_map/ppermute | solution.py:24
  15.3 5.6 %copy-start = (bf16[3,2,1,21,21,384]{5,1,4,3,2,0:T(2,128)(2,1)S(1)}, bf16[3,2,1,21,21,384]{5,1,4,3,2,0:T(2,128)(2,1)}, u32[]{:S(2)}) copy-start(bf16[3,2,1,21,21,384]{5,1,4,3,2,0:T(2,128)(2,1)} %param.12) | copy-start | bytes 6096388
  22.2 14.8 %collective-permute-start.3 = (bf16[448,384]{1,0:T(8,128)(2,1)S(1)}, bf16[448,384]{1,0:T(8,128)(2,1)S(1)}, u32[]{:S(2)}, u32[]{:S(2)}) collective-permute-start(bf16[448,384]{1,0:T(8,128)(2,1)S(1)} %get-tuple-element.87), channel_id=1, source_target_pairs={{8,0},{16,8},{24,16},{32,24},{40,32},{48,40},{56,48},{64,56},{72,6... | collective-permute-start | bytes 1032200 | tf_op jit(solution)/shard_map/ppermute | solution.py:24
  29.5 7.5 %collective-permute-start.2 = (bf16[448,384]{1,0:T(8,128)(2,1)S(1)}, bf16[448,384]{1,0:T(8,128)(2,1)S(1)}, u32[]{:S(2)}, u32[]{:S(2)}) collective-permute-start(bf16[448,384]{1,0:T(8,128)(2,1)S(1)} %get-tuple-element.86), channel_id=1, source_target_pairs={{8,0},{16,8},{24,16},{32,24},{40,32},{48,40},{56,48},{64,56},{72,6... | collective-permute-start | bytes 1032200 | tf_op jit(solution)/shard_map/ppermute | solution.py:24
  38.3 17.7 %collective-permute-start.5 = (bf16[448,384]{1,0:T(8,128)(2,1)S(1)}, bf16[448,384]{1,0:T(8,128)(2,1)S(1)}, u32[]{:S(2)}, u32[]{:S(2)}) collective-permute-start(bf16[448,384]{1,0:T(8,128)(2,1)S(1)} %get-tuple-element.103), channel_id=1, source_target_pairs={{8,0},{16,8},{24,16},{32,24},{40,32},{48,40},{56,48},{64,56},{72,6... | collective-permute-start | bytes 1032200 | tf_op jit(solution)/shard_map/ppermute | solution.py:24
  45.7 10.4 %collective-permute-start.4 = (bf16[448,384]{1,0:T(8,128)(2,1)S(1)}, bf16[448,384]{1,0:T(8,128)(2,1)S(1)}, u32[]{:S(2)}, u32[]{:S(2)}) collective-permute-start(bf16[448,384]{1,0:T(8,128)(2,1)S(1)} %get-tuple-element.102), channel_id=1, source_target_pairs={{8,0},{16,8},{24,16},{32,24},{40,32},{48,40},{56,48},{64,56},{72,6... | collective-permute-start | bytes 1032200 | tf_op jit(solution)/shard_map/ppermute | solution.py:24
  62.1 1.1 %copy-start.9 = (bf16[4,448,384]{2,1,0:T(8,128)(2,1)}, bf16[4,448,384]{2,1,0:T(8,128)(2,1)S(1)}, u32[]{:S(2)}) copy-start(bf16[4,448,384]{2,1,0:T(8,128)(2,1)S(1)} %get-tuple-element.124.flats_hbm) | copy-start | bytes 4128772
  63.2 20.0 %all-to-all-start = ((bf16[8,48,896]{2,1,0:T(8,128)(2,1)}), bf16[8,48,896]{2,1,0:T(8,128)(2,1)S(1)}, u32[]{:S(2)}, u32[]{:S(2)}) async-start(bf16[8,48,896]{2,1,0:T(8,128)(2,1)} %bitcast.15), calls=%async_computation | async-start | bytes 1376256 | tf_op jit(solution)/shard_map/all_to_all | solution.py:771
  70.3 1.3 %copy-start.10 = (bf16[4,448,384]{2,1,0:T(8,128)(2,1)S(1)}, bf16[4,448,384]{2,1,0:T(8,128)(2,1)}, u32[]{:S(2)}) copy-start(bf16[4,448,384]{2,1,0:T(8,128)(2,1)} %copy-done.9) | copy-start | bytes 4128772

commit v4 on v3

--- a/solution.py
+++ b/solution.py
@@ -22,6 +22,16 @@
 def from_next(block):
     size = lax.axis_size("sec")
     return lax.ppermute(block, "sec", [(i + 1, i) for i in range(size - 1)])
+
+
+def around_rows(block, distance):
+    rows = lax.axis_size("img") // 2
+    route = [(2 * i + j, (i + distance) % rows * 2 + j) for i in range(rows) for j in range(2)]
+    return lax.ppermute(block, "img", route)
+
+
+def with_partner(block):
+    return lax.ppermute(block, "img", [(i, i ^ 1) for i in range(lax.axis_size("img"))])
 
 
 def lanes(c):
@@ -217,7 +227,10 @@
     finish_last(act_last, t, dense, grad_out, grad_pass, grad_last)
 
 
-def order_kernel(plan_ref, turn_ref):
+def order_kernel(plan_hbm, turn_ref, plan_ref, sem):
+    get = pltpu.make_async_copy(plan_hbm, plan_ref, sem)
+    get.start()
+    get.wait()
     for t in range(turn_ref.shape[0]):
         turn_ref[plan_ref[0, t]] = t
 
@@ -297,6 +310,57 @@
 
 def five_kernel(t, grad_out, grad_pass, act_last, weight, taps, grad_last, back, wide, dense):
     five_part(t, grad_out, grad_pass, act_last, weight, taps, back, grad_last, wide, dense, lambda: None)
+
+
+def both_kernel(
+    t,
+    top_ref,
+    out_in,
+    pass_in,
+    head_hbm,
+    act_last,
+    act_older,
+    weight_five,
+    weight_three,
+    taps_five,
+    taps_three,
+    made,
+    grad_out,
+    back_five,
+    back_three,
+    grad_pass,
+    head_in,
+    wide_five,
+    wide_three,
+    dense,
+    sem,
+):
+    take(t, top_ref, out_in, pass_in, head_hbm, grad_out, grad_pass, head_in, sem)
+    three_part(
+        t,
+        grad_out,
+        act_older,
+        weight_three,
+        taps_three,
+        back_three,
+        made.at[1],
+        wide_three,
+        dense,
+        lambda: None,
+    )
+    five_part(
+        t,
+        grad_out,
+        grad_pass,
+        act_last,
+        weight_five,
+        taps_five,
+        back_five,
+        made.at[0],
+        wide_five,
+        dense,
+        lambda: None,
+    )
 
 
 def copies(pairs, sems):
@@ -365,8 +429,8 @@
 def last_grads_kernel(
     t,
     top_ref,
-    out_in,
-    pass_in,
+    row_ref,
+    pair_in,
     head_hbm,
     act_last,
     act_older,
@@ -378,82 +442,53 @@
     old_taps_five,
     old_three,
     old_taps_three,
-    packed_hbm,
-    flats_hbm,
-    backs_hbm,
-    packed,
-    grad_out,
-    grad_pass,
-    back_five,
-    back_three,
-    head_in,
-    pitched,
-    dense,
-    rows_ref,
-    sems,
+    *refs,
 ):
+    sends, refs = refs[:3], refs[3:]
+    own, grad_out, grad_pass, back_five, back_three = refs[:5]
+    packed, head_in, pitched, dense, rows_ref, sem = refs[5:]
     scale = 1.0 / PIXELS
-    keep = copies(
-        [
-            (act_last.at[t], flats_hbm.at[0]),
-            (act_older.at[t], flats_hbm.at[1]),
-            (grad_out, flats_hbm.at[2]),
-            (grad_pass, flats_hbm.at[3]),
-            (back_five, backs_hbm.at[0]),
-            (back_three, backs_hbm.at[1]),
-        ],
-        sems,
-    )
-    points, columns = copies(
-        [
-            (packed.at[:, pl.ds(0, 2 * CH)], packed_hbm.at[:, pl.ds(0, 2 * CH)]),
-            (packed.at[:, pl.ds(2 * CH, 128)], packed_hbm.at[:, pl.ds(2 * CH, 128)]),
-        ],
-        sems.at[pl.ds(6, 2)],
-    )
-    keep[0].start()
-    keep[1].start()
-    take(t, top_ref, out_in, pass_in, head_hbm, grad_out, grad_pass, head_in, sems.at[8])
-    keep[2].start()
-    keep[3].start()
+    take(t, top_ref, pair_in.at[0], pair_in.at[1], head_hbm, grad_out, grad_pass, head_in, sem)
     left = grad_out[...]
-    packed[:, 0:CH] = ((across(mixed_five[...], left) + old_five[...]) * scale).astype(BF16)
-    packed[:, CH : 2 * CH] = ((across(mixed_three[...], left) + old_three[...]) * scale).astype(BF16)
-    points.start()
+    packed[:, 0:CH] = (across(mixed_five[...], left) + old_five[...]) * scale
+    packed[:, CH : 2 * CH] = (across(mixed_three[...], left) + old_three[...]) * scale
     rows_ref[...] = jnp.zeros(rows_ref.shape, F32)
-    for act, weight, back, old, at, kernel, kept in (
-        (act_last, weight_five, back_five, old_taps_five, 0, 5, keep[4]),
-        (act_older, weight_three, back_three, old_taps_three, 32, 3, keep[5]),
+    for act, weight, back, old, at, kernel in (
+        (act_last, weight_five, back_five, old_taps_five, 0, 5),
+        (act_older, weight_three, back_three, old_taps_three, 32, 3),
     ):
         dense_product(left, weight, dense)
         to_pitched(dense, back)
-        kept.start()
         widened(act, t, dense)
         to_pitched(dense, pitched)
         count = kernel * kernel
         tap_sums(back, pitched, rows_ref.at[pl.ds(at, old.shape[0])], kernel)
         rows_ref[at : at + count, :] = (rows_ref[at : at + count, :] + old[0:count, :]) * scale
     for c in range(BLOCKS):
-        packed[lanes(c), 2 * CH : 2 * CH + 128] = rows_ref[:, lanes(c)].T.astype(BF16)
-    columns.start()
-    for copy in keep:
-        copy.wait()
-    points.wait()
-    columns.wait()
+        packed[lanes(c), 2 * CH : 2 * CH + 128] = rows_ref[:, lanes(c)].T
+    height = own.shape[0]
+    groups = CH // height
+
+    def rows(distance):
+        at = lax.rem(row_ref[0] + distance, groups) * height
+        return pl.ds(pl.multiple_of(at, 16), height)
+
+    own[...] = packed[rows(0), :]
+    for distance, send in enumerate(sends, 1):
+        send[...] = packed[rows(distance), :].astype(BF16)
 
 
 def last_kernel(
-    flats_hbm,
-    backs_hbm,
-    taps_five,
-    taps_three,
-    outgoing_hbm,
+    t,
     grad_out,
     grad_pass,
     back_five,
     back_three,
     act_last,
     act_older,
+    taps_five,
+    taps_three,
+    outgoing_hbm,
     wide_five,
     wide_three,
     dense,
@@ -461,32 +496,14 @@
     outgoing,
     sems,
 ):
-    gets = copies(
-        [
-            (backs_hbm.at[1], back_three),
-            (flats_hbm.at[1], act_older.at[0]),
-            (backs_hbm.at[0], back_five),
-            (flats_hbm.at[0], act_last.at[0]),
-            (flats_hbm.at[2], grad_out),
-            (flats_hbm.at[3], grad_pass),
-        ],
-        sems,
-    )
-    for get in gets:
-        get.start()
     spread_taps(taps_five, wide_five, 25)
     spread_taps(taps_three, wide_three, 9)
-    gets[0].wait()
     spread_conv(back_three, wide_three, dense, 3, True)
-    gets[1].wait()
-    finish_older(act_older, 0, dense, made_older)
-    gets[2].wait()
+    finish_older(act_older, t, dense, made_older)
     spread_conv(back_five, wide_five, dense, 5, True)
-    for get in gets[3:]:
-        get.wait()
 
     def both(rows, c):
-        last = last_piece(act_last, 0, dense, grad_out, grad_pass, c, rows)
+        last = last_piece(act_last, t, dense, grad_out, grad_pass, c, rows)
         return jnp.swapaxes(jnp.stack([last, made_older[rows, lanes(c)]], 0), 0, 1)
 
     def body(i, carry):
@@ -502,7 +519,7 @@
             (outgoing.at[pl.ds(0, half)], outgoing_hbm.at[pl.ds(0, half)]),
             (outgoing.at[pl.ds(half, PIXELS - half)], outgoing_hbm.at[pl.ds(half, PIXELS - half)]),
         ],
-        sems.at[pl.ds(6, 2)],
+        sems,
     )
     put[0].start()
     lax.fori_loop(half // 16, PIXELS // 16, body, 0)
@@ -514,16 +531,24 @@
     put[1].wait()
 
 
-def total_kernel(landed, five, three, taps_five, taps_three):
-    def summed(columns):
-        total = landed[0, :, columns].astype(F32)
-        for n in range(1, landed.shape[0]):
-            total = total + landed[n, :, columns].astype(F32)
+def half_total_kernel(half_ref, own, one, two, three, kept, send):
+    height = kept.shape[0]
+
+    def summed(which):
+        rows = pl.ds(pl.multiple_of(which * height, 16), height)
+        total = own[rows, :]
+        for landed in (one, two, three):
+            total = total + landed[rows, :].astype(F32)
         return total
 
-    five[...] = summed(slice(0, CH))
-    three[...] = summed(slice(CH, 2 * CH))
-    rows = summed(slice(2 * CH, 2 * CH + 128)).T
+    kept[...] = summed(half_ref[0])
+    send[...] = summed(1 - half_ref[0]).astype(BF16)
+
+
+def total_kernel(kept, landed, five, three, taps_five, taps_three):
+    five[...] = kept[:, 0:CH] + landed[:, 0:CH].astype(F32)
+    three[...] = kept[:, CH : 2 * CH] + landed[:, CH : 2 * CH].astype(F32)
+    rows = (kept[:, 2 * CH :] + landed[:, 2 * CH :].astype(F32)).T
     for taps, at in ((taps_five, 0), (taps_three, 32)):
         for k in range(taps.shape[0]):
             taps[k] = rows[at + k : at + k + 1, :]
@@ -532,9 +557,8 @@
 VMEM = pl.BlockSpec(memory_space=pltpu.VMEM)
 SMEM = pl.BlockSpec(memory_space=pltpu.SMEM)
 ANY = pl.BlockSpec(memory_space=pl.ANY)
-ALONE = 16 << 20
 FLAT = jax.ShapeDtypeStruct((ROWS, CH), BF16)
-PACKED = jax.ShapeDtypeStruct((CH, 2 * CH + 128), BF16)
+WIDE = 2 * CH + 128
 ACTS = jax.ShapeDtypeStruct((4, ROWS, CH), BF16)
 BACK = jax.ShapeDtypeStruct((BLOCKS, PITCHED, 128), F32)
 SUMS = (
@@ -570,10 +594,10 @@
         order_kernel,
         "order",
         (plan,),
-        [SMEM],
+        [ANY],
         (jax.ShapeDtypeStruct((plan.shape[1],), jnp.int32),),
         (SMEM,),
-        [],
+        [pltpu.SMEM(plan.shape, jnp.int32), pltpu.SemaphoreType.DMA],
         6,
     )
     return turns
@@ -628,6 +652,19 @@
         (VMEM,) * 2,
         [WIDE_FIVE, DENSE],
         3,
+    )
+
+
+def call_both(t, given, acts, weights, taps):
+    return run(
+        functools.partial(both_kernel, t),
+        f"both_{t}",
+        (*given, *acts, *weights, *taps),
+        [SMEM, VMEM, VMEM, ANY] + [VMEM] * 6,
+        (jax.ShapeDtypeStruct((2, ROWS, CH), BF16), FLAT, BACK, BACK),
+        (VMEM,) * 4,
+        [FLAT_SCRATCH, PAIR_SCRATCH, WIDE_FIVE, WIDE_THREE, DENSE, pltpu.SemaphoreType.DMA],
+        5,
     )
 
 
@@ -646,56 +683,54 @@
     )
 
 
-def call_last_grads(t, given, acts, weights, mixed, olds):
+def call_last_grads(t, height, given, acts, weights, mixed, olds):
+    send = jax.ShapeDtypeStruct((height, WIDE), BF16)
+    own = jax.ShapeDtypeStruct((height, WIDE), F32)
     return run(
         functools.partial(last_grads_kernel, t),
         "last_grads",
         (*given, *acts, *weights, *mixed, *olds),
-        [SMEM, VMEM, VMEM, ANY] + [VMEM] * 10,
-        (PACKED, ACTS, jax.ShapeDtypeStruct((2, *BACK.shape), F32)),
-        (ANY,) * 3,
+        [SMEM, SMEM, VMEM, ANY] + [VMEM] * 10,
+        (send, send, send, own, FLAT, FLAT, BACK, BACK),
+        (VMEM,) * 8,
         [
-            pltpu.VMEM(PACKED.shape, BF16),
-            FLAT_SCRATCH,
-            FLAT_SCRATCH,
-            PITCHED_SCRATCH,
-            PITCHED_SCRATCH,
+            pltpu.VMEM((CH, WIDE), F32),
             PAIR_SCRATCH,
             PITCHED_SCRATCH,
             DENSE,
             pltpu.VMEM((128, CH), F32),
-            pltpu.SemaphoreType.DMA((9,)),
+            pltpu.SemaphoreType.DMA,
         ],
         6,
-        ALONE,
-    )
-
-
-def call_last(kept, taps):
+    )
+
+
+def call_last(t, grads, backs, acts, taps):
     (outgoing,) = run(
-        last_kernel,
+        functools.partial(last_kernel, t),
         "last",
-        (*kept, *taps),
-        [ANY] * 2 + [VMEM] * 2,
+        (*grads, *backs, *acts, *taps),
+        [VMEM] * 8,
         (jax.ShapeDtypeStruct((PIXELS, 2, CH), BF16),),
         (ANY,),
-        [
-            FLAT_SCRATCH,
-            FLAT_SCRATCH,
-            PITCHED_SCRATCH,
-            PITCHED_SCRATCH,
-            pltpu.VMEM((1, ROWS, CH), BF16),
-            pltpu.VMEM((1, ROWS, CH), BF16),
-            WIDE_FIVE,
-            WIDE_THREE,
-            DENSE,
-            FLAT_SCRATCH,
-            PAIR_SCRATCH,
-            pltpu.SemaphoreType.DMA((8,)),
-        ],
+        [WIDE_FIVE, WIDE_THREE, DENSE, FLAT_SCRATCH, PAIR_SCRATCH, pltpu.SemaphoreType.DMA((2,))],
         4,
     )
     return outgoing
+
+
+def call_half_total(half, own, landed):
+    height = own.shape[0] // 2
+    return run(
+        half_total_kernel,
+        "half_total",
+        (half, own, *landed),
+        [SMEM] + [VMEM] * 4,
+        (jax.ShapeDtypeStruct((height, WIDE), F32), jax.ShapeDtypeStruct((height, WIDE), BF16)),
+        (VMEM,) * 2,
+        [],
+        1,
+    )
 
 
 def whole(shape):
@@ -703,18 +738,18 @@
     return pl.BlockSpec(shape, lambda i: zeros)
 
 
-def call_total(landed):
-    rows = landed.shape[1]
+def call_total(kept, landed):
+    rows = kept.shape[0]
     shapes = [(rows, CH), (rows, CH), (25, 1, rows), (9, 1, rows)]
     return pl.pallas_call(
         total_kernel,
         grid=(1,),
         out_shape=tuple(jax.ShapeDtypeStruct(shape, F32) for shape in shapes),
-        in_specs=[whole(landed.shape)],
+        in_specs=[whole(kept.shape), whole(landed.shape)],
         out_specs=tuple(whole(shape) for shape in shapes),
         compiler_params=pltpu.CompilerParams(vmem_limit_bytes=12 << 20),
         name="total",
-    )(landed)
+    )(kept, landed)
 
 
 def by_pixel(stack):
@@ -735,7 +770,9 @@
     turns = saved_last.shape[1]
     top = (lax.axis_index("sec") == lax.axis_size("sec") - 1).astype(jnp.int32)[None]
     turn_of_slot = call_order(plan)
-    turn_of_slot, top = lax.optimization_barrier((turn_of_slot, top))
+    image = lax.axis_index("img").astype(jnp.int32)
+    group, half = (image // 2)[None], (image % 2)[None]
+    turn_of_slot, top, group, half = lax.optimization_barrier((turn_of_slot, top, group, half))
     head = jnp.transpose(head_adjoint, (0, 2, 3, 4, 1, 5)).reshape(turns - 1, PIXELS, 2, CH)
     weights = (point_five[0], point_three[0])
     taps = (depth_five[0], depth_three[0])
@@ -746,16 +783,14 @@
     grad_last, act_last, back_five = call_first_five(
         turn_of_slot, by_pixel(saved_last), grad_out, grad_pass, weights[0], taps[0]
     )
+    next_out = from_next(grad_last)
     acts = (act_last, act_older)
     sums = ()
-    for t in range(turns - 1):
-        next_out = from_next(grad_last)
-        ahead = turns - 1 if t == turns - 2 else None
-        made = call_grads(t, ahead, grad_out, acts, taps, (back_five, back_three), sums)
-        next_out, next_pass, made = lax.optimization_barrier((next_out, next_pass, made))
-        sums = made[:4]
+    for t in range(turns - 2):
+        made = call_grads(t, None, grad_out, acts, taps, (back_five, back_three), sums)
+        next_out, next_pass, sums = lax.optimization_barrier((next_out, next_pass, made))
         given = (top, next_out, next_pass, head)
-        if t < turns - 2:
+        if t < turns - 3:
             grad_older, grad_out, grad_pass, back_three = call_three(
                 t + 1, given, act_older, weights[1], taps[1]
             )
@@ -763,14 +798,29 @@
             grad_last, back_five = call_five(
                 t + 1, grad_out, grad_pass, act_last, weights[0], taps[0]
             )
-    packed, *kept = call_last_grads(
-        turns - 1, given, acts, weights, made[4:], sums
-    )
-    devices = lax.axis_size("img")
-    packed = packed.reshape(devices, CH // devices, packed.shape[1])
-    landed = lax.all_to_all(packed, "img", 0, 0, tiled=True)
-    outgoing = call_last(kept, taps)
-    five, three, tap_five, tap_three = call_total(landed)
+            next_out = from_next(grad_last)
+    both, grad_out, back_five, back_three = call_both(turns - 2, given, acts, weights, taps)
+    next_pair = from_next(both)
+    made = call_grads(
+        turns - 2, turns - 1, grad_out, acts, taps, (back_five, back_three), sums
+    )
+    next_pair, made = lax.optimization_barrier((next_pair, made))
+    *sends, own, grad_out, grad_pass, back_five, back_three = call_last_grads(
+        turns - 1,
+        CH * 2 // lax.axis_size("img"),
+        (top, group, next_pair, head),
+        acts,
+        weights,
+        made[4:],
+        made[:4],
+    )
+    landed = [around_rows(sends[distance - 1], distance) for distance in (2, 1, 3)]
+    outgoing = call_last(
+        turns - 1, (grad_out, grad_pass), (back_five, back_three), acts, taps
+    )
+    *landed, outgoing = lax.optimization_barrier((*landed, outgoing))
+    kept, send = call_half_total(half, own, landed)
+    five, three, tap_five, tap_three = call_total(kept, with_partner(send))
     outgoing = outgoing.reshape(1, 1, SIDE, SIDE, 2, CH).transpose(0, 4, 1, 2, 3, 5)
     return (
         outgoing,

time: 84.3 us -> 77.1 us (0.915)
  waiting for transfers between devices: 6.71 us -> 3.58 us
  Pallas kernels: 45.4 us -> 42.9 us
  local copies, waits for them, and re-layouts: 3.52 us -> 1.06 us
    ppermute x0 -> x4, starting transfers between devices: none -> 9.85 us  [the longest x3 6.5 us: around_rows(): return lax.ppermute(block, 'img', route)]
    all_to_all x1 -> x0, starting transfers between devices: 7.17 us -> none  [local(): landed = lax.all_to_all(packed, 'img', 0, 0, tiled=True)]
    all_to_all x1 -> x0, waiting for transfers between devices: 6.69 us -> none  [local(): landed = lax.all_to_all(packed, 'img', 0, 0, tiled=True)]
    ppermute x0 -> x4, waiting for transfers between devices: none -> 3.57 us  [the longest x1 2.71 us: with_partner(): lax.ppermute(block, 'img', [(i, i ^ 1) for i in range(lax.axis_size('img'...]
    unnamed x22 -> x18, local copies, waits for them, and re-layouts: 3.52 us -> 1.06 us
    pallas_call x12, Pallas kernels: 44.7 us -> 42.3 us  [run(): pl.pallas_call(kernel, out_shape=tuple(shapes), in_specs=specs, out_specs...]
    ppermute x6 -> x5, starting transfers between devices: 20.2 us -> 18.3 us  [from_next(): return lax.ppermute(block, 'sec', [(i + 1, i) for i in range(size - 1)])]
  transfers between devices with their start and end apart: 7 -> 9, of which waited for: 1 -> 2; matrix products, arithmetic and copies ran while one was open for 0% -> 0% of each run, Pallas kernels for 38% -> 38%
where the time goes in v4:
time: 77.1 us; the launch traced here: 76.6 us
  Pallas kernels  42.9 us (56%)
  starting transfers between devices  28.1 us (36%)
  waiting for transfers between devices  3.58 us (5%)
  local copies, waits for them, and re-layouts  1.06 us (1%)
  between operations  0.89 us (1%)
    pallas_call x12, Pallas kernels, run(): pl.pallas_call(kernel, out_shape=tuple(shapes), in_specs=specs, out_specs...  42.3 us
    ppermute x5, starting transfers between devices, from_next(): return lax.ppermute(block, 'sec', [(i + 1, i) for i in range(size - 1)])  18.3 us
    ppermute x3, starting transfers between devices, around_rows(): return lax.ppermute(block, 'img', route)  6.5 us
    ppermute x1, starting transfers between devices, with_partner(): lax.ppermute(block, 'img', [(i, i ^ 1) for i in range(lax.axis_size('img'...  3.35 us
    ppermute x1, waiting for transfers between devices, with_partner(): lax.ppermute(block, 'img', [(i, i ^ 1) for i in range(lax.axis_size('img'...  2.71 us
  transfers between devices with their start and end apart: 9, of which 2 were waited for; matrix products, arithmetic and copies ran while one was open for 0% of the time, Pallas kernels for 38%

profile of v4, /device:TPU:32, one launch (start us, length us, event | category | flops | bytes accessed | tf_op | source)
XLA Modules:
  0.0 76.6 jit_solution(3118205150835271098)
XLA Ops:
  0.7 0.0 copy-start.8
  0.7 0.6 copy-done.8
  1.3 0.0 copy-start.1
  1.3 0.0 copy-start.3
  1.3 0.0 copy-start.4
  1.3 0.0 copy-start.7
  1.3 1.1 %order.1.turn_ref = s32[4]{0:T(128)S(1)} custom-call(s32[1,4]{1,0:T(1,128)S(1)} %copy-done.8), custom_call_target="tpu_custom_call" | custom-call | flops 6000000000 | tf_op jit(solution)/shard_map/order/pallas_call | solution.py:580
  2.5 0.1 copy-done.1
  2.6 0.2 copy-done.3
  2.8 0.1 copy-done.4
  2.9 0.0 copy-done.7
  2.9 0.0 copy-start.2
  2.9 0.0 copy-start.5
  2.9 2.8 %first_three.1 = (bf16[448,384]{1,0:T(8,128)(2,1)S(1)}, bf16[4,448,384]{2,1,0:T(8,128)(2,1)S(1)}, bf16[448,384]{1,0:T(8,128)(2,1)S(1)}, bf16[448,384]{1,0:T(8,128)(2,1)S(1)}, f32[3,616,128]{2,1,0:T(8,128)S(1)}) custom-call(s32[4]{0:T(128)S(1)} %order.1.turn_ref, bf16[441,4,384]{2,1,0:T(4,128)(2,1)S(1)} %bitcast.29, bf16[441,2,384]{2,1,0:T(2,128)(2,1)S(1)} %bitcast.31, ...), custom_call_target="tpu_custom_call" | custom-call | flops 4000000000 | tf_op jit(solution)/shard_map/first_three/pallas_call | solution.py:580
  5.7 3.7 %collective-permute-start.1 = (bf16[448,384]{1,0:T(8,128)(2,1)S(1)}, bf16[448,384]{1,0:T(8,128)(2,1)S(1)}, u32[]{:S(2)}, u32[]{:S(2)}) collective-permute-start(bf16[448,384]{1,0:T(8,128)(2,1)S(1)} %get-tuple-element.84), channel_id=1, source_target_pairs={{8,0},{16,8},{24,16},{32,24},{40,32},{48,40},{56,48},{64,56},{72,6... | collective-permute-start | bytes 1032200 | tf_op jit(solution)/shard_map/ppermute | solution.py:24
  9.3 0.0 copy-done.2
  9.3 0.0 copy-done.5
  9.3 0.0 copy-done.6
  9.4 3.4 %first_five.1 = (bf16[448,384]{1,0:T(8,128)(2,1)S(1)}, bf16[4,448,384]{2,1,0:T(8,128)(2,1)S(1)}, f32[3,616,128]{2,1,0:T(8,128)S(1)}) custom-call(s32[4]{0:T(128)S(1)} %order.1.turn_ref, bf16[441,4,384]{2,1,0:T(4,128)(2,1)S(1)} %bitcast.30, bf16[448,384]{1,0:T(8,128)(2,1)S(1)} %get-tuple-element.81.grad_out.refs_0_, ...), custom_call_target="tpu_custom_call" | custom-call | flops 4000000000 | tf_op jit(solution)/shard_map/first_five/pallas_call | solution.py:580
  12.8 2.6 %collective-permute-start = (bf16[448,384]{1,0:T(8,128)(2,1)S(1)}, bf16[448,384]{1,0:T(8,128)(2,1)S(1)}, u32[]{:S(2)}, u32[]{:S(2)}) collective-permute-start(bf16[448,384]{1,0:T(8,128)(2,1)S(1)} %get-tuple-element.83), channel_id=1, source_target_pairs={{8,0},{16,8},{24,16},{32,24},{40,32},{48,40},{56,48},{64,56},{72,6... | collective-permute-start | bytes 1032200 | tf_op jit(solution)/shard_map/ppermute | solution.py:24
  15.3 0.0 copy-start
  15.4 5.6 %grads_0.1 = (f32[384,384]{1,0:T(8,128)S(1)}, f32[32,384]{1,0:T(8,128)S(1)}, f32[384,384]{1,0:T(8,128)S(1)}, f32[16,384]{1,0:T(8,128)S(1)}) custom-call(bf16[448,384]{1,0:T(8,128)(2,1)S(1)} %get-tuple-element.81.grad_out.refs_0_, bf16[4,448,384]{2,1,0:T(8,128)(2,1)S(1)} %get-tuple-element.85.refs_1_.act_last, ...), custom_call_target="tpu_custom_call" | custom-call | flops 6000000000 | tf_op jit(solution)/shard_map/grads_0/pallas_call | solution.py:580
  20.9 0.0 collective-permute-done.1.pass_in
  20.9 0.0 collective-permute-done.out_in
  20.9 0.0 copy-done
  20.9 1.3 %three_1.1 = (bf16[448,384]{1,0:T(8,128)(2,1)S(1)}, bf16[448,384]{1,0:T(8,128)(2,1)S(1)}, bf16[448,384]{1,0:T(8,128)(2,1)S(1)}, f32[3,616,128]{2,1,0:T(8,128)S(1)}) custom-call(s32[1]{0:T(128)} %bitcast.top_ref, bf16[448,384]{1,0:T(8,128)(2,1)S(1)} %collective-permute-done.out_in, bf16[448,384]{1,0:T(8,128)(2,1)S(1)} %collective-permute-done.1.pass_in, ...), custom_call_target="tpu_custom_call" | custom-call | flops 2000000000 | tf_op jit(solution)/shard_map/three_1/pallas_call | solution.py:580
  22.2 5.1 %collective-permute-start.3 = (bf16[448,384]{1,0:T(8,128)(2,1)S(1)}, bf16[448,384]{1,0:T(8,128)(2,1)S(1)}, u32[]{:S(2)}, u32[]{:S(2)}) collective-permute-start(bf16[448,384]{1,0:T(8,128)(2,1)S(1)} %get-tuple-element.98), channel_id=1, source_target_pairs={{8,0},{16,8},{24,16},{32,24},{40,32},{48,40},{56,48},{64,56},{72,6... | collective-permute-start | bytes 1032200 | tf_op jit(solution)/shard_map/ppermute | solution.py:24
  27.3 2.3 %five_1.1 = (bf16[448,384]{1,0:T(8,128)(2,1)S(1)}, f32[3,616,128]{2,1,0:T(8,128)S(1)}) custom-call(bf16[448,384]{1,0:T(8,128)(2,1)S(1)} %get-tuple-element.95.grad_out.refs_0_, bf16[448,384]{1,0:T(8,128)(2,1)S(1)} %get-tuple-element.96.grad_pass, bf16[4,448,384]{2,1,0:T(8,128)(2,1)S(1)} %get-tuple-element.85.refs_1_.act_last, bf16[384,384]{1,0:T(8,128)(2,1)S(1)} %bitcast.37, ...), custom_call_target="tpu_custom_call" | custom-call | flops 3000000000 | tf_op jit(solution)/shard_map/five_1/pallas_call | solution.py:580
  29.6 1.9 %collective-permute-start.2 = (bf16[448,384]{1,0:T(8,128)(2,1)S(1)}, bf16[448,384]{1,0:T(8,128)(2,1)S(1)}, u32[]{:S(2)}, u32[]{:S(2)}) collective-permute-start(bf16[448,384]{1,0:T(8,128)(2,1)S(1)} %get-tuple-element.97), channel_id=1, source_target_pairs={{8,0},{16,8},{24,16},{32,24},{40,32},{48,40},{56,48},{64,56},{72,6... | collective-permute-start | bytes 1032200 | tf_op jit(solution)/shard_map/ppermute | solution.py:24
  31.5 5.6 %grads_1.1 = (f32[384,384]{1,0:T(8,128)S(1)}, f32[32,384]{1,0:T(8,128)S(1)}, f32[384,384]{1,0:T(8,128)S(1)}, f32[16,384]{1,0:T(8,128)S(1)}) custom-call(bf16[448,384]{1,0:T(8,128)(2,1)S(1)} %get-tuple-element.95.grad_out.refs_0_, bf16[4,448,384]{2,1,0:T(8,128)(2,1)S(1)} %get-tuple-element.85.refs_1_.act_last, ...), custom_call_target="tpu_custom_call" | custom-call | flops 6000000000 | tf_op jit(solution)/shard_map/grads_1/pallas_call | solution.py:580
  37.1 0.0 collective-permute-done.3.pass_in
  37.1 0.0 collective-permute-done.2.out_in
  37.1 3.6 %both_2.1 = (bf16[2,448,384]{2,1,0:T(8,128)(2,1)S(1)}, bf16[448,384]{1,0:T(8,128)(2,1)S(1)}, f32[3,616,128]{2,1,0:T(8,128)S(1)}, f32[3,616,128]{2,1,0:T(8,128)S(1)}) custom-call(s32[1]{0:T(128)} %bitcast.top_ref, bf16[448,384]{1,0:T(8,128)(2,1)S(1)} %collective-permute-done.2.out_in, bf16[448,384]{1,0:T(8,128)(2,1)S(1)} %collective-permute-done.3.pass_in, ...), custom_call_target="tpu_custom_call" | custom-call | flops 5000000000 | tf_op jit(solution)/shard_map/both_2/pallas_call | solution.py:580
  40.7 5.1 %collective-permute-start.4 = (bf16[2,448,384]{2,1,0:T(8,128)(2,1)S(1)}, bf16[2,448,384]{2,1,0:T(8,128)(2,1)S(1)}, u32[]{:S(2)}, u32[]{:S(2)}) collective-permute-start(bf16[2,448,384]{2,1,0:T(8,128)(2,1)S(1)} %get-tuple-element.111), channel_id=1, source_target_pairs={{8,0},{16,8},{24,16},{32,24},{40,32},{48,40},{56,48},{64,56},{72,6... | collective-permute-start | bytes 2064392 | tf_op jit(solution)/shard_map/ppermute | solution.py:24
  45.8 8.4 %grads_2.1 = (f32[384,384]{1,0:T(8,128)S(1)}, f32[32,384]{1,0:T(8,128)S(1)}, f32[384,384]{1,0:T(8,128)S(1)}, f32[16,384]{1,0:T(8,128)S(1)}, bf16[448,384]{1,0:T(8,128)(2,1)S(1)}, /*index=5*/bf16[448,384]{1,0:T(8,128)(2,1)S(1)}) custom-call(bf16[448,384]{1,0:T(8,128)(2,1)S(1)} %get-tuple-element.112.refs_0_, ...), custom_call_target="tpu_custom_call" | custom-call | flops 8000000000 | tf_op jit(solution)/shard_map/grads_2/pallas_call | solution.py:580
  54.2 0.0 collective-permute-done.4.pair_in
  54.2 4.4 %last_grads.1 = (bf16[96,896]{1,0:T(8,128)(2,1)S(1)}, bf16[96,896]{1,0:T(8,128)(2,1)S(1)}, bf16[96,896]{1,0:T(8,128)(2,1)S(1)}, f32[96,896]{1,0:T(8,128)S(1)}, b...) custom-call(s32[1]{0:T(128)} %bitcast.top_ref, ...), custom_call_target="tpu_custom_call" | custom-call | flops 6000000000 | tf_op jit(solution)/shard_map/last_grads/pallas_call | solution.py:580
  58.6 3.3 %collective-permute-start.5 = (bf16[96,896]{1,0:T(8,128)(2,1)S(1)}, bf16[96,896]{1,0:T(8,128)(2,1)S(1)}, u32[]{:S(2)}, u32[]{:S(2)}) collective-permute-start(bf16[96,896]{1,0:T(8,128)(2,1)S(1)} %get-tuple-element.132), channel_id=1, source_target_pairs={{0,4},{1,5},{2,6},{3,7},{4,0},{5,1},{6,2},{7,3},{8,12},{9,13},{10,... | collective-permute-start | bytes 516104 | tf_op jit(solution)/shard_map/ppermute | solution.py:30
  61.9 0.7 collective-permute-start.6
  62.6 2.6 %collective-permute-start.7 = (bf16[96,896]{1,0:T(8,128)(2,1)S(1)}, bf16[96,896]{1,0:T(8,128)(2,1)S(1)}, u32[]{:S(2)}, u32[]{:S(2)}) collective-permute-start(bf16[96,896]{1,0:T(8,128)(2,1)S(1)} %get-tuple-element.134), channel_id=1, source_target_pairs={{0,6},{1,7},{2,0},{3,1},{4,2},{5,3},{6,4},{7,5},{8,14},{9,15},{10,... | collective-permute-start | bytes 516104 | tf_op jit(solution)/shard_map/ppermute | solution.py:30
  65.1 3.8 %last.1 = bf16[441,2,384]{2,1,0:T(2,128)(2,1)} custom-call(bf16[448,384]{1,0:T(8,128)(2,1)S(1)} %get-tuple-element.135.grad_out, bf16[448,384]{1,0:T(8,128)(2,1)S(1)} %get-tuple-element.136.grad_pass, f32[3,616,128]{2,1,0:T(8,128)S(1)} %get-tuple-element.137.back_five, f32[3,616,128]{2,1,0:T(8,128)S(1)} %get-tuple-element.138.back_three, ...), custom_call_target="tpu_custom_call" | custom-call | flops 4000000000 | tf_op jit(solution)/shard_map/last/pallas_call | solution.py:580
  68.9 0.0 collective-permute-done.5.one
  68.9 0.9 %collective-permute-done.6.two = bf16[96,896]{1,0:T(8,128)(2,1)S(1)} collective-permute-done((bf16[96,896]{1,0:T(8,128)(2,1)S(1)}, bf16[96,896]{1,0:T(8,128)(2,1)S(1)}, u32[]{:S(2)}, u32[]{:S(2)}) %collective-permute-start.6) | collective-permute-done | bytes 172064 | tf_op jit(solution)/shard_map/ppermute | solution.py:30
  69.7 0.0 collective-permute-done.7.three
  69.7 0.1 half_total.1
  69.8 3.4 %collective-permute-start.8 = (bf16[48,896]{1,0:T(8,128)(2,1)S(1)}, bf16[48,896]{1,0:T(8,128)(2,1)S(1)}, u32[]{:S(2)}, u32[]{:S(2)}) collective-permute-start(bf16[48,896]{1,0:T(8,128)(2,1)S(1)} %get-tuple-element.146), channel_id=1, source_target_pairs={{0,1},{1,0},{2,3},{3,2},{4,5},{5,4},{6,7},{7,6},{8,9},{9,8},{10,11... | collective-permute-start | bytes 258056 | tf_op jit(solution)/shard_map/ppermute | solution.py:34
  73.2 2.7 %collective-permute-done.8.landed = bf16[48,896]{1,0:T(8,128)(2,1)S(1)} collective-permute-done((bf16[48,896]{1,0:T(8,128)(2,1)S(1)}, bf16[48,896]{1,0:T(8,128)(2,1)S(1)}, u32[]{:S(2)}, u32[]{:S(2)}) %collective-permute-start.8) | collective-permute-done | bytes 86048 | tf_op jit(solution)/shard_map/ppermute | solution.py:34
  75.9 0.7 total.1
  (1 shorter events, 0.0 us)
Async XLA Ops:
  0.7 0.7 copy-start.8
  1.3 1.3 %copy-start.1 = (bf16[1,4,1,21,21,384]{5,1,4,3,2,0:T(4,128)(2,1)S(1)}, bf16[1,4,1,21,21,384]{5,1,4,3,2,0:T(4,128)(2,1)}, u32[]{:S(2)}) copy-start(bf16[1,4,1,21,21,384]{5,1,4,3,2,0:T(4,128)(2,1)} %param.10) | copy-start | bytes 4064260
  1.3 1.5 %copy-start.3 = (bf16[1,2,1,21,21,384]{5,1,4,3,2,0:T(2,128)(2,1)S(1)}, bf16[1,2,1,21,21,384]{5,1,4,3,2,0:T(2,128)(2,1)}, u32[]{:S(2)}) copy-start(bf16[1,2,1,21,21,384]{5,1,4,3,2,0:T(2,128)(2,1)} %param.11) | copy-start | bytes 2032132
  1.3 1.6 %copy-start.4 = (bf16[1,384,384]{2,1,0:T(8,128)(2,1)S(1)}, bf16[1,384,384]{2,1,0:T(8,128)(2,1)}, u32[]{:S(2)}) copy-start(bf16[1,384,384]{2,1,0:T(8,128)(2,1)} %param.17) | copy-start | bytes 884740
  1.3 1.6 %copy-start.7 = (bf16[1,9,384]{2,1,0:T(8,128)(2,1)S(1)}, bf16[1,9,384]{2,1,0:T(8,128)(2,1)}, u32[]{:S(2)}) copy-start(bf16[1,9,384]{2,1,0:T(8,128)(2,1)} %param.15) | copy-start | bytes 20740
  2.9 6.4 %copy-start.2 = (bf16[1,4,1,21,21,384]{5,1,4,3,2,0:T(4,128)(2,1)S(1)}, bf16[1,4,1,21,21,384]{5,1,4,3,2,0:T(4,128)(2,1)}, u32[]{:S(2)}) copy-start(bf16[1,4,1,21,21,384]{5,1,4,3,2,0:T(4,128)(2,1)} %param.9) | copy-start | bytes 4064260
  2.9 6.5 %copy-start.5 = (bf16[1,384,384]{2,1,0:T(8,128)(2,1)S(1)}, bf16[1,384,384]{2,1,0:T(8,128)(2,1)}, u32[]{:S(2)}) copy-start(bf16[1,384,384]{2,1,0:T(8,128)(2,1)} %param.16) | copy-start | bytes 884740
  2.9 6.5 %copy-start.6 = (bf16[1,25,384]{2,1,0:T(8,128)(2,1)S(1)}, bf16[1,25,384]{2,1,0:T(8,128)(2,1)}, u32[]{:S(2)}) copy-start(bf16[1,25,384]{2,1,0:T(8,128)(2,1)} %param.14) | copy-start | bytes 57604
  5.7 15.3 %collective-permute-start.1 = (bf16[448,384]{1,0:T(8,128)(2,1)S(1)}, bf16[448,384]{1,0:T(8,128)(2,1)S(1)}, u32[]{:S(2)}, u32[]{:S(2)}) collective-permute-start(bf16[448,384]{1,0:T(8,128)(2,1)S(1)} %get-tuple-element.84), channel_id=1, source_target_pairs={{8,0},{16,8},{24,16},{32,24},{40,32},{48,40},{56,48},{64,56},{72,6... | collective-permute-start | bytes 1032200 | tf_op jit(solution)/shard_map/ppermute | solution.py:24
  12.8 8.2 %collective-permute-start = (bf16[448,384]{1,0:T(8,128)(2,1)S(1)}, bf16[448,384]{1,0:T(8,128)(2,1)S(1)}, u32[]{:S(2)}, u32[]{:S(2)}) collective-permute-start(bf16[448,384]{1,0:T(8,128)(2,1)S(1)} %get-tuple-element.83), channel_id=1, source_target_pairs={{8,0},{16,8},{24,16},{32,24},{40,32},{48,40},{56,48},{64,56},{72,6... | collective-permute-start | bytes 1032200 | tf_op jit(solution)/shard_map/ppermute | solution.py:24
  15.3 5.6 %copy-start = (bf16[3,2,1,21,21,384]{5,1,4,3,2,0:T(2,128)(2,1)S(1)}, bf16[3,2,1,21,21,384]{5,1,4,3,2,0:T(2,128)(2,1)}, u32[]{:S(2)}) copy-start(bf16[3,2,1,21,21,384]{5,1,4,3,2,0:T(2,128)(2,1)} %param.12) | copy-start | bytes 6096388
  22.2 14.8 %collective-permute-start.3 = (bf16[448,384]{1,0:T(8,128)(2,1)S(1)}, bf16[448,384]{1,0:T(8,128)(2,1)S(1)}, u32[]{:S(2)}, u32[]{:S(2)}) collective-permute-start(bf16[448,384]{1,0:T(8,128)(2,1)S(1)} %get-tuple-element.98), channel_id=1, source_target_pairs={{8,0},{16,8},{24,16},{32,24},{40,32},{48,40},{56,48},{64,56},{72,6... | collective-permute-start | bytes 1032200 | tf_op jit(solution)/shard_map/ppermute | solution.py:24
  29.6 7.5 %collective-permute-start.2 = (bf16[448,384]{1,0:T(8,128)(2,1)S(1)}, bf16[448,384]{1,0:T(8,128)(2,1)S(1)}, u32[]{:S(2)}, u32[]{:S(2)}) collective-permute-start(bf16[448,384]{1,0:T(8,128)(2,1)S(1)} %get-tuple-element.97), channel_id=1, source_target_pairs={{8,0},{16,8},{24,16},{32,24},{40,32},{48,40},{56,48},{64,56},{72,6... | collective-permute-start | bytes 1032200 | tf_op jit(solution)/shard_map/ppermute | solution.py:24
  40.7 13.5 %collective-permute-start.4 = (bf16[2,448,384]{2,1,0:T(8,128)(2,1)S(1)}, bf16[2,448,384]{2,1,0:T(8,128)(2,1)S(1)}, u32[]{:S(2)}, u32[]{:S(2)}) collective-permute-start(bf16[2,448,384]{2,1,0:T(8,128)(2,1)S(1)} %get-tuple-element.111), channel_id=1, source_target_pairs={{8,0},{16,8},{24,16},{32,24},{40,32},{48,40},{56,48},{64,56},{72,6... | collective-permute-start | bytes 2064392 | tf_op jit(solution)/shard_map/ppermute | solution.py:24
  58.6 10.3 %collective-permute-start.5 = (bf16[96,896]{1,0:T(8,128)(2,1)S(1)}, bf16[96,896]{1,0:T(8,128)(2,1)S(1)}, u32[]{:S(2)}, u32[]{:S(2)}) collective-permute-start(bf16[96,896]{1,0:T(8,128)(2,1)S(1)} %get-tuple-element.132), channel_id=1, source_target_pairs={{0,4},{1,5},{2,6},{3,7},{4,0},{5,1},{6,2},{7,3},{8,12},{9,13},{10,... | collective-permute-start | bytes 516104 | tf_op jit(solution)/shard_map/ppermute | solution.py:30
  61.9 7.9 %collective-permute-start.6 = (bf16[96,896]{1,0:T(8,128)(2,1)S(1)}, bf16[96,896]{1,0:T(8,128)(2,1)S(1)}, u32[]{:S(2)}, u32[]{:S(2)}) collective-permute-start(bf16[96,896]{1,0:T(8,128)(2,1)S(1)} %get-tuple-element.133), channel_id=1, source_target_pairs={{0,2},{1,3},{2,4},{3,5},{4,6},{5,7},{6,0},{7,1},{8,10},{9,11},{10,... | collective-permute-start | bytes 516104 | tf_op jit(solution)/shard_map/ppermute | solution.py:30
  62.6 7.2 %collective-permute-start.7 = (bf16[96,896]{1,0:T(8,128)(2,1)S(1)}, bf16[96,896]{1,0:T(8,128)(2,1)S(1)}, u32[]{:S(2)}, u32[]{:S(2)}) collective-permute-start(bf16[96,896]{1,0:T(8,128)(2,1)S(1)} %get-tuple-element.134), channel_id=1, source_target_pairs={{0,6},{1,7},{2,0},{3,1},{4,2},{5,3},{6,4},{7,5},{8,14},{9,15},{10,... | collective-permute-start | bytes 516104 | tf_op jit(solution)/shard_map/ppermute | solution.py:30
  69.8 6.1 %collective-permute-start.8 = (bf16[48,896]{1,0:T(8,128)(2,1)S(1)}, bf16[48,896]{1,0:T(8,128)(2,1)S(1)}, u32[]{:S(2)}, u32[]{:S(2)}) collective-permute-start(bf16[48,896]{1,0:T(8,128)(2,1)S(1)} %get-tuple-element.146), channel_id=1, source_target_pairs={{0,1},{1,0},{2,3},{3,2},{4,5},{5,4},{6,7},{7,6},{8,9},{9,8},{10,11... | collective-permute-start | bytes 258056 | tf_op jit(solution)/shard_map/ppermute | solution.py:34

commit v5 on v4

--- a/solution.py
+++ b/solution.py
@@ -227,21 +227,20 @@
     finish_last(act_last, t, dense, grad_out, grad_pass, grad_last)
 
 
-def order_kernel(plan_hbm, turn_ref, plan_ref, sem):
-    get = pltpu.make_async_copy(plan_hbm, plan_ref, sem)
-    get.start()
-    get.wait()
-    for t in range(turn_ref.shape[0]):
-        turn_ref[plan_ref[0, t]] = t
-
-
-def slots_unpacked(turn_ref, source, target):
+def opening_kernel(token_ref):
+    token_ref[0] = 0
+
+
+def slots_unpacked(plan_ref, source, target):
+    turns = target.shape[0]
+    turn_of = [sum(jnp.where(plan_ref[0, t] == k, t, 0) for t in range(1, turns)) for k in range(turns)]
+
     def put(at, block):
         block = jnp.maximum(block, 0)
-        for k in range(4):
-            target[turn_ref[k], pl.ds(at, 16), :] = block[k]
-
-    unpack(source, 4, put)
+        for k in range(turns):
+            target[turn_of[k], pl.ds(at, 16), :] = block[k]
+
+    unpack(source, turns, put)
 
 
 def pair_unpacked(source, grad_out, grad_pass):
@@ -252,24 +251,36 @@
     unpack(source, 2, put)
 
 
-def first_three_kernel(
-    turn_ref, older_in, arriving_in, weight, taps, grad_older, act_older, grad_out, grad_pass, back, wide, dense
+def first_five_kernel(
+    token_ref,
+    plan_ref,
+    last_in,
+    arriving_in,
+    weight,
+    taps,
+    grad_last,
+    act_last,
+    grad_out,
+    back,
+    grad_pass,
+    wide,
+    dense,
 ):
     pair_unpacked(arriving_in, grad_out, grad_pass)
 
     def ready():
-        slots_unpacked(turn_ref, older_in, act_older)
-
-    three_part(0, grad_out, act_older, weight, taps, back, grad_older, wide, dense, ready)
-
-
-def first_five_kernel(
-    turn_ref, last_in, grad_out, grad_pass, weight, taps, grad_last, act_last, back, wide, dense
+        slots_unpacked(plan_ref, last_in, act_last)
+
+    five_part(0, grad_out, grad_pass, act_last, weight, taps, back, grad_last, wide, dense, ready)
+
+
+def first_three_kernel(
+    plan_ref, older_in, grad_out, weight, taps, grad_older, act_older, back, wide, dense
 ):
     def ready():
-        slots_unpacked(turn_ref, last_in, act_last)
-
-    five_part(0, grad_out, grad_pass, act_last, weight, taps, back, grad_last, wide, dense, ready)
+        slots_unpacked(plan_ref, older_in, act_older)
+
+    three_part(0, grad_out, act_older, weight, taps, back, grad_older, wide, dense, ready)
 
 
 def take(t, top_ref, out_in, pass_in, head_hbm, grad_out, grad_pass, head_in, sem):
@@ -286,30 +297,30 @@
         grad_pass[...] = pass_in[...]
 
 
-def three_kernel(
+def five_kernel(
     t,
     top_ref,
     out_in,
     pass_in,
     head_hbm,
-    act_older,
+    act_last,
     weight,
     taps,
-    grad_older,
+    grad_last,
     grad_out,
+    back,
     grad_pass,
-    back,
     head_in,
     wide,
     dense,
     sem,
 ):
     take(t, top_ref, out_in, pass_in, head_hbm, grad_out, grad_pass, head_in, sem)
+    five_part(t, grad_out, grad_pass, act_last, weight, taps, back, grad_last, wide, dense, lambda: None)
+
+
+def three_kernel(t, grad_out, act_older, weight, taps, grad_older, back, wide, dense):
     three_part(t, grad_out, act_older, weight, taps, back, grad_older, wide, dense, lambda: None)
-
-
-def five_kernel(t, grad_out, grad_pass, act_last, weight, taps, grad_last, back, wide, dense):
-    five_part(t, grad_out, grad_pass, act_last, weight, taps, back, grad_last, wide, dense, lambda: None)
 
 
 def both_kernel(
@@ -409,15 +420,15 @@
     sums = refs[:4]
     refs = refs[4:]
     if ahead is not None:
-        later = refs[:2]
-        refs = refs[2:]
+        later = refs[:4]
+        refs = refs[4:]
     pitched, dense, wide, mixed = refs
     left = grad_out[...]
     for n, (act, taps, back, kernel) in enumerate(
         ((act_last, taps_five, back_five, 5), (act_older, taps_three, back_three, 3))
     ):
         if ahead is not None:
-            mix(act, ahead, taps, later[n], pitched, dense, wide, kernel)
+            mix(act, ahead, taps, later[n], later[2 + n], dense, wide, kernel)
         mix(act, t, taps, mixed, pitched, dense, wide, kernel)
         got = across(mixed[...], left)
         sums[2 * n][...] = got if olds is None else got + olds[2 * n][...]
@@ -432,12 +443,12 @@
     row_ref,
     pair_in,
     head_hbm,
-    act_last,
-    act_older,
     weight_five,
     weight_three,
     mixed_five,
     mixed_three,
+    pitched_five,
+    pitched_three,
     old_five,
     old_taps_five,
     old_three,
@@ -446,21 +457,19 @@
 ):
     sends, refs = refs[:3], refs[3:]
     own, grad_out, grad_pass, back_five, back_three = refs[:5]
-    packed, head_in, pitched, dense, rows_ref, sem = refs[5:]
+    packed, head_in, dense, rows_ref, sem = refs[5:]
     scale = 1.0 / PIXELS
     take(t, top_ref, pair_in.at[0], pair_in.at[1], head_hbm, grad_out, grad_pass, head_in, sem)
     left = grad_out[...]
     packed[:, 0:CH] = (across(mixed_five[...], left) + old_five[...]) * scale
     packed[:, CH : 2 * CH] = (across(mixed_three[...], left) + old_three[...]) * scale
     rows_ref[...] = jnp.zeros(rows_ref.shape, F32)
-    for act, weight, back, old, at, kernel in (
-        (act_last, weight_five, back_five, old_taps_five, 0, 5),
-        (act_older, weight_three, back_three, old_taps_three, 32, 3),
+    for pitched, weight, back, old, at, kernel in (
+        (pitched_five, weight_five, back_five, old_taps_five, 0, 5),
+        (pitched_three, weight_three, back_three, old_taps_three, 32, 3),
     ):
         dense_product(left, weight, dense)
         to_pitched(dense, back)
-        widened(act, t, dense)
-        to_pitched(dense, pitched)
         count = kernel * kernel
         tap_sums(back, pitched, rows_ref.at[pl.ds(at, old.shape[0])], kernel)
         rows_ref[at : at + count, :] = (rows_ref[at : at + count, :] + old[0:count, :]) * scale
@@ -589,69 +598,69 @@
     )(*operands)
 
 
-def call_order(plan):
-    (turns,) = run(
-        order_kernel,
-        "order",
-        (plan,),
-        [ANY],
-        (jax.ShapeDtypeStruct((plan.shape[1],), jnp.int32),),
+def call_opening():
+    (token,) = run(
+        opening_kernel,
+        "opening",
+        (),
+        [],
+        (jax.ShapeDtypeStruct((1,), jnp.int32),),
         (SMEM,),
-        [pltpu.SMEM(plan.shape, jnp.int32), pltpu.SemaphoreType.DMA],
+        [],
         6,
     )
-    return turns
-
-
-def call_first_three(turns, older, arriving, weight, taps):
+    return token
+
+
+def call_first_five(token, plan, last, arriving, weight, taps):
+    return run(
+        first_five_kernel,
+        "first_five",
+        (token, plan, last, arriving, weight, taps),
+        [SMEM, SMEM] + [VMEM] * 4,
+        (FLAT, ACTS, FLAT, BACK),
+        (VMEM,) * 4,
+        [FLAT_SCRATCH, WIDE_FIVE, DENSE],
+        4,
+    )
+
+
+def call_first_three(plan, older, grad_out, weight, taps):
     return run(
         first_three_kernel,
         "first_three",
-        (turns, older, arriving, weight, taps),
+        (plan, older, grad_out, weight, taps),
         [SMEM] + [VMEM] * 4,
-        (FLAT, ACTS, FLAT, FLAT, BACK),
-        (VMEM,) * 5,
-        [WIDE_THREE, DENSE],
-        4,
-    )
-
-
-def call_first_five(turns, last, grad_out, grad_pass, weight, taps):
-    return run(
-        first_five_kernel,
-        "first_five",
-        (turns, last, grad_out, grad_pass, weight, taps),
-        [SMEM] + [VMEM] * 5,
         (FLAT, ACTS, BACK),
         (VMEM,) * 3,
-        [WIDE_FIVE, DENSE],
-        4,
-    )
-
-
-def call_three(t, given, act, weight, taps):
+        [WIDE_THREE, DENSE],
+        3,
+    )
+
+
+def call_five(t, given, act, weight, taps):
+    return run(
+        functools.partial(five_kernel, t),
+        f"five_{t}",
+        (*given, act, weight, taps),
+        [SMEM, VMEM, VMEM, ANY] + [VMEM] * 3,
+        (FLAT, FLAT, BACK),
+        (VMEM,) * 3,
+        [FLAT_SCRATCH, PAIR_SCRATCH, WIDE_FIVE, DENSE, pltpu.SemaphoreType.DMA],
+        3,
+    )
+
+
+def call_three(t, grad_out, act, weight, taps):
     return run(
         functools.partial(three_kernel, t),
         f"three_{t}",
-        (*given, act, weight, taps),
-        [SMEM, VMEM, VMEM, ANY] + [VMEM] * 3,
-        (FLAT, FLAT, FLAT, BACK),
-        (VMEM,) * 4,
-        [PAIR_SCRATCH, WIDE_THREE, DENSE, pltpu.SemaphoreType.DMA],
-        2,
-    )
-
-
-def call_five(t, grad_out, grad_pass, act, weight, taps):
-    return run(
-        functools.partial(five_kernel, t),
-        f"five_{t}",
-        (grad_out, grad_pass, act, weight, taps),
-        [VMEM] * 5,
+        (grad_out, act, weight, taps),
+        [VMEM] * 4,
         (FLAT, BACK),
         (VMEM,) * 2,
-        [WIDE_FIVE, DENSE],
-        3,
+        [WIDE_THREE, DENSE],
+        2,
     )
 
 
@@ -669,7 +678,7 @@
 
 
 def call_grads(t, ahead, grad_out, acts, taps, backs, olds):
-    shapes = SUMS if ahead is None else SUMS + (FLAT, FLAT)
+    shapes = SUMS if ahead is None else SUMS + (FLAT, FLAT, BACK, BACK)
     operands = (grad_out, *acts, *taps, *backs, *olds)
     return run(
         functools.partial(grads_kernel, t, ahead),
@@ -683,20 +692,19 @@
     )
 
 
-def call_last_grads(t, height, given, acts, weights, mixed, olds):
+def call_last_grads(t, height, given, weights, mixed, olds):
     send = jax.ShapeDtypeStruct((height, WIDE), BF16)
     own = jax.ShapeDtypeStruct((height, WIDE), F32)
     return run(
         functools.partial(last_grads_kernel, t),
         "last_grads",
-        (*given, *acts, *weights, *mixed, *olds),
+        (*given, *weights, *mixed, *olds),
         [SMEM, SMEM, VMEM, ANY] + [VMEM] * 10,
         (send, send, send, own, FLAT, FLAT, BACK, BACK),
         (VMEM,) * 8,
         [
             pltpu.VMEM((CH, WIDE), F32),
             PAIR_SCRATCH,
-            PITCHED_SCRATCH,
             DENSE,
             pltpu.VMEM((128, CH), F32),
             pltpu.SemaphoreType.DMA,
@@ -769,21 +777,20 @@
 ):
     turns = saved_last.shape[1]
     top = (lax.axis_index("sec") == lax.axis_size("sec") - 1).astype(jnp.int32)[None]
-    turn_of_slot = call_order(plan)
     image = lax.axis_index("img").astype(jnp.int32)
     group, half = (image // 2)[None], (image % 2)[None]
-    turn_of_slot, top, group, half = lax.optimization_barrier((turn_of_slot, top, group, half))
+    token, top, group, half = lax.optimization_barrier((call_opening(), top, group, half))
     head = jnp.transpose(head_adjoint, (0, 2, 3, 4, 1, 5)).reshape(turns - 1, PIXELS, 2, CH)
     weights = (point_five[0], point_three[0])
     taps = (depth_five[0], depth_three[0])
-    grad_older, act_older, grad_out, grad_pass, back_three = call_first_three(
-        turn_of_slot, by_pixel(saved_older), by_pixel(arriving), weights[1], taps[1]
+    grad_last, act_last, grad_out, back_five = call_first_five(
+        token, plan, by_pixel(saved_last), by_pixel(arriving), weights[0], taps[0]
+    )
+    next_out = from_next(grad_last)
+    grad_older, act_older, back_three = call_first_three(
+        plan, by_pixel(saved_older), grad_out, weights[1], taps[1]
     )
     next_pass = from_next(grad_older)
-    grad_last, act_last, back_five = call_first_five(
-        turn_of_slot, by_pixel(saved_last), grad_out, grad_pass, weights[0], taps[0]
-    )
-    next_out = from_next(grad_last)
     acts = (act_last, act_older)
     sums = ()
     for t in range(turns - 2):
@@ -791,14 +798,12 @@
         next_out, next_pass, sums = lax.optimization_barrier((next_out, next_pass, made))
         given = (top, next_out, next_pass, head)
         if t < turns - 3:
-            grad_older, grad_out, grad_pass, back_three = call_three(
-                t + 1, given, act_older, weights[1], taps[1]
-            )
-            next_pass = from_next(grad_older)
-            grad_last, back_five = call_five(
-                t + 1, grad_out, grad_pass, act_last, weights[0], taps[0]
+            grad_last, grad_out, back_five = call_five(
+                t + 1, given, act_last, weights[0], taps[0]
             )
             next_out = from_next(grad_last)
+            grad_older, back_three = call_three(t + 1, grad_out, act_older, weights[1], taps[1])
+            next_pass = from_next(grad_older)
     both, grad_out, back_five, back_three = call_both(turns - 2, given, acts, weights, taps)
     next_pair = from_next(both)
     made = call_grads(
@@ -809,7 +814,6 @@
         turns - 1,
         CH * 2 // lax.axis_size("img"),
         (top, group, next_pair, head),
-        acts,
         weights,
         made[4:],
         made[:4],

time: 77.1 us -> 77.1 us (level)
  transfers between devices with their start and end apart: 9 -> 9, of which waited for: 2 -> 2; matrix products, arithmetic and copies ran while one was open for 0% -> 0% of each run, Pallas kernels for 38% -> 35%
where the time goes in v5:
time: 77.1 us; the launch traced here: 76.5 us
  Pallas kernels  42.7 us (55%)
  starting transfers between devices  28.7 us (37%)
  waiting for transfers between devices  3.2 us (4%)
  local copies, waits for them, and re-layouts  1 us (1%)
  between operations  0.93 us (1%)
    pallas_call x12, Pallas kernels, run(): pl.pallas_call(kernel, out_shape=tuple(shapes), in_specs=specs, out_specs...  42 us
    ppermute x5, starting transfers between devices, from_next(): return lax.ppermute(block, 'sec', [(i + 1, i) for i in range(size - 1)])  18.8 us
    ppermute x3, starting transfers between devices, around_rows(): return lax.ppermute(block, 'img', route)  6.51 us
    ppermute x1, starting transfers between devices, with_partner(): lax.ppermute(block, 'img', [(i, i ^ 1) for i in range(lax.axis_size('img'...  3.35 us
    ppermute x1, waiting for transfers between devices, with_partner(): lax.ppermute(block, 'img', [(i, i ^ 1) for i in range(lax.axis_size('img'...  2.72 us
  transfers between devices with their start and end apart: 9, of which 2 were waited for; matrix products, arithmetic and copies ran while one was open for 0% of the time, Pallas kernels for 35%

profile of v5, /device:TPU:32, one launch (start us, length us, event | category | flops | bytes accessed | tf_op | source)
XLA Modules:
  0.0 76.5 jit_solution(6827238561065439665)
XLA Ops:
  0.6 0.0 copy-start.1
  0.7 0.0 copy-start.3
  0.7 0.0 copy-start.4
  0.7 0.0 copy-start.6
  0.7 0.0 copy-start.8
  0.7 0.5 opening.1.token_ref
  1.3 0.7 copy-done.1
  2.0 0.2 copy-done.3
  2.1 0.1 copy-done.4
  2.2 0.0 copy-done.6
  2.2 0.0 copy-done.8
  2.2 0.0 copy-start.5
  2.2 0.0 copy-start.7
  2.2 4.6 %first_five.1 = (bf16[448,384]{1,0:T(8,128)(2,1)S(1)}, bf16[4,448,384]{2,1,0:T(8,128)(2,1)S(1)}, bf16[448,384]{1,0:T(8,128)(2,1)S(1)}, f32[3,616,128]{2,1,0:T(8,128)S(1)}) custom-call(s32[1]{0:T(128)} %opening.1.token_ref, s32[1,4]{1,0:T(1,128)S(1)} %copy-done.8, bf16[441,4,384]{2,1,0:T(4,128)(2,1)S(1)} %bitcast.29, bf16[441,2,384]{2,1,0:T(2,128)(2,1)S(1)} %bitcast.31, ...), custom_call_target="tpu_custom_call" | custom-call | flops 4000000000 | tf_op jit(solution)/shard_map/first_five/pallas_call | solution.py:589
  6.8 3.7 %collective-permute-start = (bf16[448,384]{1,0:T(8,128)(2,1)S(1)}, bf16[448,384]{1,0:T(8,128)(2,1)S(1)}, u32[]{:S(2)}, u32[]{:S(2)}) collective-permute-start(bf16[448,384]{1,0:T(8,128)(2,1)S(1)} %get-tuple-element.83), channel_id=1, source_target_pairs={{8,0},{16,8},{24,16},{32,24},{40,32},{48,40},{56,48},{64,56},{72,6... | collective-permute-start | bytes 1032200 | tf_op jit(solution)/shard_map/ppermute | solution.py:24
  10.5 0.0 copy-done.2
  10.5 0.0 copy-done.5
  10.5 0.0 copy-done.7
  10.5 2.4 %first_three.1 = (bf16[448,384]{1,0:T(8,128)(2,1)S(1)}, bf16[4,448,384]{2,1,0:T(8,128)(2,1)S(1)}, f32[3,616,128]{2,1,0:T(8,128)S(1)}) custom-call(s32[1,4]{1,0:T(1,128)S(1)} %copy-done.8, bf16[441,4,384]{2,1,0:T(4,128)(2,1)S(1)} %bitcast.30, bf16[448,384]{1,0:T(8,128)(2,1)S(1)} %get-tuple-element.84.grad_out.refs_0_, bf16[384,384]{1,0:T(8,128)(2,1)S(1)} %bitcast.36, ...), custom_call_target="tpu_custom_call" | custom-call | flops 3000000000 | tf_op jit(solution)/shard_map/first_three/pallas_call | solution.py:589
  12.9 2.6 %collective-permute-start.1 = (bf16[448,384]{1,0:T(8,128)(2,1)S(1)}, bf16[448,384]{1,0:T(8,128)(2,1)S(1)}, u32[]{:S(2)}, u32[]{:S(2)}) collective-permute-start(bf16[448,384]{1,0:T(8,128)(2,1)S(1)} %get-tuple-element.85), channel_id=1, source_target_pairs={{8,0},{16,8},{24,16},{32,24},{40,32},{48,40},{56,48},{64,56},{72,6... | collective-permute-start | bytes 1032200 | tf_op jit(solution)/shard_map/ppermute | solution.py:24
  15.5 0.0 copy-start
  15.5 5.6 %grads_0.1 = (f32[384,384]{1,0:T(8,128)S(1)}, f32[32,384]{1,0:T(8,128)S(1)}, f32[384,384]{1,0:T(8,128)S(1)}, f32[16,384]{1,0:T(8,128)S(1)}) custom-call(bf16[448,384]{1,0:T(8,128)(2,1)S(1)} %get-tuple-element.84.grad_out.refs_0_, bf16[4,448,384]{2,1,0:T(8,128)(2,1)S(1)} %get-tuple-element.86.refs_1_.act_last, ...), custom_call_target="tpu_custom_call" | custom-call | flops 6000000000 | tf_op jit(solution)/shard_map/grads_0/pallas_call | solution.py:589
  21.1 0.0 collective-permute-done.out_in
  21.1 0.0 collective-permute-done.1.pass_in
  21.1 0.0 copy-done
  21.1 2.3 %five_1.1 = (bf16[448,384]{1,0:T(8,128)(2,1)S(1)}, bf16[448,384]{1,0:T(8,128)(2,1)S(1)}, f32[3,616,128]{2,1,0:T(8,128)S(1)}) custom-call(s32[1]{0:T(128)} %bitcast.top_ref, bf16[448,384]{1,0:T(8,128)(2,1)S(1)} %collective-permute-done.out_in, bf16[448,384]{1,0:T(8,128)(2,1)S(1)} %collective-permute-done.1.pass_in, bf16[3,441,2,384]{3,2,1,0:T(2,128)(2,1)S(1)} %bitcast.26, ...), custom_call_target="tpu_custom_call" | custom-call | flops 3000000000 | tf_op jit(solution)/shard_map/five_1/pallas_call | solution.py:589
  23.4 5.1 %collective-permute-start.2 = (bf16[448,384]{1,0:T(8,128)(2,1)S(1)}, bf16[448,384]{1,0:T(8,128)(2,1)S(1)}, u32[]{:S(2)}, u32[]{:S(2)}) collective-permute-start(bf16[448,384]{1,0:T(8,128)(2,1)S(1)} %get-tuple-element.96), channel_id=1, source_target_pairs={{8,0},{16,8},{24,16},{32,24},{40,32},{48,40},{56,48},{64,56},{72,6... | collective-permute-start | bytes 1032200 | tf_op jit(solution)/shard_map/ppermute | solution.py:24
  28.5 1.2 %three_1.1 = (bf16[448,384]{1,0:T(8,128)(2,1)S(1)}, f32[3,616,128]{2,1,0:T(8,128)S(1)}) custom-call(bf16[448,384]{1,0:T(8,128)(2,1)S(1)} %get-tuple-element.97.grad_out.refs_0_, bf16[4,448,384]{2,1,0:T(8,128)(2,1)S(1)} %get-tuple-element.87.refs_2_.act_older, bf16[384,384]{1,0:T(8,128)(2,1)S(1)} %bitcast.37, bf16[9,384]{1,0:T(8,128)(2,1)S(1)} %bitcast.49), custom_call_target="tpu_custom_call" | custom-call | flops 2000000000 | tf_op jit(solution)/shard_map/three_1/pallas_call | solution.py:589
  29.7 1.9 %collective-permute-start.3 = (bf16[448,384]{1,0:T(8,128)(2,1)S(1)}, bf16[448,384]{1,0:T(8,128)(2,1)S(1)}, u32[]{:S(2)}, u32[]{:S(2)}) collective-permute-start(bf16[448,384]{1,0:T(8,128)(2,1)S(1)} %get-tuple-element.98), channel_id=1, source_target_pairs={{8,0},{16,8},{24,16},{32,24},{40,32},{48,40},{56,48},{64,56},{72,6... | collective-permute-start | bytes 1032200 | tf_op jit(solution)/shard_map/ppermute | solution.py:24
  31.6 5.6 %grads_1.1 = (f32[384,384]{1,0:T(8,128)S(1)}, f32[32,384]{1,0:T(8,128)S(1)}, f32[384,384]{1,0:T(8,128)S(1)}, f32[16,384]{1,0:T(8,128)S(1)}) custom-call(bf16[448,384]{1,0:T(8,128)(2,1)S(1)} %get-tuple-element.97.grad_out.refs_0_, bf16[4,448,384]{2,1,0:T(8,128)(2,1)S(1)} %get-tuple-element.86.refs_1_.act_last, ...), custom_call_target="tpu_custom_call" | custom-call | flops 6000000000 | tf_op jit(solution)/shard_map/grads_1/pallas_call | solution.py:589
  37.2 0.0 collective-permute-done.2.out_in
  37.2 0.0 collective-permute-done.3.pass_in
  37.2 3.6 %both_2.1 = (bf16[2,448,384]{2,1,0:T(8,128)(2,1)S(1)}, bf16[448,384]{1,0:T(8,128)(2,1)S(1)}, f32[3,616,128]{2,1,0:T(8,128)S(1)}, f32[3,616,128]{2,1,0:T(8,128)S(1)}) custom-call(s32[1]{0:T(128)} %bitcast.top_ref, bf16[448,384]{1,0:T(8,128)(2,1)S(1)} %collective-permute-done.2.out_in, bf16[448,384]{1,0:T(8,128)(2,1)S(1)} %collective-permute-done.3.pass_in, ...), custom_call_target="tpu_custom_call" | custom-call | flops 5000000000 | tf_op jit(solution)/shard_map/both_2/pallas_call | solution.py:589
  40.8 5.6 %collective-permute-start.4 = (bf16[2,448,384]{2,1,0:T(8,128)(2,1)S(1)}, bf16[2,448,384]{2,1,0:T(8,128)(2,1)S(1)}, u32[]{:S(2)}, u32[]{:S(2)}) collective-permute-start(bf16[2,448,384]{2,1,0:T(8,128)(2,1)S(1)} %get-tuple-element.111), channel_id=1, source_target_pairs={{8,0},{16,8},{24,16},{32,24},{40,32},{48,40},{56,48},{64,56},{72,6... | collective-permute-start | bytes 2064392 | tf_op jit(solution)/shard_map/ppermute | solution.py:24
  46.5 8.6 %grads_2.1 = (f32[384,384]{1,0:T(8,128)S(1)}, f32[32,384]{1,0:T(8,128)S(1)}, f32[384,384]{1,0:T(8,128)S(1)}, f32[16,384]{1,0:T(8,128)S(1)}, bf16[448,384]{1,0:T(...) custom-call(bf16[448,384]{1,0:T(8,128)(2,1)S(1)} %get-tuple-element.112.refs_0, ...), custom_call_target="tpu_custom_call" | custom-call | flops 8000000000 | tf_op jit(solution)/shard_map/grads_2/pallas_call | solution.py:589
  55.0 0.0 collective-permute-done.4.pair_in
  55.0 3.8 %last_grads.1 = (bf16[96,896]{1,0:T(8,128)(2,1)S(1)}, bf16[96,896]{1,0:T(8,128)(2,1)S(1)}, bf16[96,896]{1,0:T(8,128)(2,1)S(1)}, f32[96,896]{1,0:T(8,128)S(1)}, b...) custom-call(s32[1]{0:T(128)} %bitcast.top_ref, ...), custom_call_target="tpu_custom_call" | custom-call | flops 6000000000 | tf_op jit(solution)/shard_map/last_grads/pallas_call | solution.py:589
  58.9 3.3 %collective-permute-start.5 = (bf16[96,896]{1,0:T(8,128)(2,1)S(1)}, bf16[96,896]{1,0:T(8,128)(2,1)S(1)}, u32[]{:S(2)}, u32[]{:S(2)}) collective-permute-start(bf16[96,896]{1,0:T(8,128)(2,1)S(1)} %get-tuple-element.136), channel_id=1, source_target_pairs={{0,4},{1,5},{2,6},{3,7},{4,0},{5,1},{6,2},{7,3},{8,12},{9,13},{10,... | collective-permute-start | bytes 516104 | tf_op jit(solution)/shard_map/ppermute | solution.py:30
  62.2 0.7 collective-permute-start.6
  62.8 2.6 %collective-permute-start.7 = (bf16[96,896]{1,0:T(8,128)(2,1)S(1)}, bf16[96,896]{1,0:T(8,128)(2,1)S(1)}, u32[]{:S(2)}, u32[]{:S(2)}) collective-permute-start(bf16[96,896]{1,0:T(8,128)(2,1)S(1)} %get-tuple-element.138), channel_id=1, source_target_pairs={{0,6},{1,7},{2,0},{3,1},{4,2},{5,3},{6,4},{7,5},{8,14},{9,15},{10,... | collective-permute-start | bytes 516104 | tf_op jit(solution)/shard_map/ppermute | solution.py:30
  65.4 3.8 %last.1 = bf16[441,2,384]{2,1,0:T(2,128)(2,1)} custom-call(bf16[448,384]{1,0:T(8,128)(2,1)S(1)} %get-tuple-element.139.grad_out, bf16[448,384]{1,0:T(8,128)(2,1)S(1)} %get-tuple-element.140.grad_pass, f32[3,616,128]{2,1,0:T(8,128)S(1)} %get-tuple-element.141.back_five, f32[3,616,128]{2,1,0:T(8,128)S(1)} %get-tuple-element.142.back_three, ...), custom_call_target="tpu_custom_call" | custom-call | flops 4000000000 | tf_op jit(solution)/shard_map/last/pallas_call | solution.py:589
  69.2 0.0 collective-permute-done.5.one
  69.2 0.5 collective-permute-done.6.two
  69.6 0.0 collective-permute-done.7.three
  69.6 0.1 half_total.1
  69.7 3.3 %collective-permute-start.8 = (bf16[48,896]{1,0:T(8,128)(2,1)S(1)}, bf16[48,896]{1,0:T(8,128)(2,1)S(1)}, u32[]{:S(2)}, u32[]{:S(2)}) collective-permute-start(bf16[48,896]{1,0:T(8,128)(2,1)S(1)} %get-tuple-element.150), channel_id=1, source_target_pairs={{0,1},{1,0},{2,3},{3,2},{4,5},{5,4},{6,7},{7,6},{8,9},{9,8},{10,11... | collective-permute-start | bytes 258056 | tf_op jit(solution)/shard_map/ppermute | solution.py:34
  73.1 2.7 %collective-permute-done.8.landed = bf16[48,896]{1,0:T(8,128)(2,1)S(1)} collective-permute-done((bf16[48,896]{1,0:T(8,128)(2,1)S(1)}, bf16[48,896]{1,0:T(8,128)(2,1)S(1)}, u32[]{:S(2)}, u32[]{:S(2)}) %collective-permute-start.8) | collective-permute-done | bytes 86048 | tf_op jit(solution)/shard_map/ppermute | solution.py:34
  75.8 0.7 total.1
  (1 shorter events, 0.0 us)
Async XLA Ops:
  0.6 1.3 %copy-start.1 = (bf16[1,4,1,21,21,384]{5,1,4,3,2,0:T(4,128)(2,1)S(1)}, bf16[1,4,1,21,21,384]{5,1,4,3,2,0:T(4,128)(2,1)}, u32[]{:S(2)}) copy-start(bf16[1,4,1,21,21,384]{5,1,4,3,2,0:T(4,128)(2,1)} %param.9) | copy-start | bytes 4064260
  0.7 1.5 %copy-start.3 = (bf16[1,2,1,21,21,384]{5,1,4,3,2,0:T(2,128)(2,1)S(1)}, bf16[1,2,1,21,21,384]{5,1,4,3,2,0:T(2,128)(2,1)}, u32[]{:S(2)}) copy-start(bf16[1,2,1,21,21,384]{5,1,4,3,2,0:T(2,128)(2,1)} %param.11) | copy-start | bytes 2032132
  0.7 1.6 %copy-start.4 = (bf16[1,384,384]{2,1,0:T(8,128)(2,1)S(1)}, bf16[1,384,384]{2,1,0:T(8,128)(2,1)}, u32[]{:S(2)}) copy-start(bf16[1,384,384]{2,1,0:T(8,128)(2,1)} %param.16) | copy-start | bytes 884740
  0.7 1.5 %copy-start.6 = (bf16[1,25,384]{2,1,0:T(8,128)(2,1)S(1)}, bf16[1,25,384]{2,1,0:T(8,128)(2,1)}, u32[]{:S(2)}) copy-start(bf16[1,25,384]{2,1,0:T(8,128)(2,1)} %param.14) | copy-start | bytes 57604
  0.7 1.5 %copy-start.8 = (s32[1,4]{1,0:T(1,128)S(1)}, s32[1,4]{1,0:T(1,128)}, u32[]{:S(2)}) copy-start(s32[1,4]{1,0:T(1,128)} %plan_ref.3) | copy-start | bytes 52
  2.2 8.3 %copy-start.2 = (bf16[1,4,1,21,21,384]{5,1,4,3,2,0:T(4,128)(2,1)S(1)}, bf16[1,4,1,21,21,384]{5,1,4,3,2,0:T(4,128)(2,1)}, u32[]{:S(2)}) copy-start(bf16[1,4,1,21,21,384]{5,1,4,3,2,0:T(4,128)(2,1)} %param.10) | copy-start | bytes 4064260
  2.2 8.3 %copy-start.5 = (bf16[1,384,384]{2,1,0:T(8,128)(2,1)S(1)}, bf16[1,384,384]{2,1,0:T(8,128)(2,1)}, u32[]{:S(2)}) copy-start(bf16[1,384,384]{2,1,0:T(8,128)(2,1)} %param.17) | copy-start | bytes 884740
  2.2 8.3 %copy-start.7 = (bf16[1,9,384]{2,1,0:T(8,128)(2,1)S(1)}, bf16[1,9,384]{2,1,0:T(8,128)(2,1)}, u32[]{:S(2)}) copy-start(bf16[1,9,384]{2,1,0:T(8,128)(2,1)} %param.15) | copy-start | bytes 20740
  6.8 14.2 %collective-permute-start = (bf16[448,384]{1,0:T(8,128)(2,1)S(1)}, bf16[448,384]{1,0:T(8,128)(2,1)S(1)}, u32[]{:S(2)}, u32[]{:S(2)}) collective-permute-start(bf16[448,384]{1,0:T(8,128)(2,1)S(1)} %get-tuple-element.83), channel_id=1, source_target_pairs={{8,0},{16,8},{24,16},{32,24},{40,32},{48,40},{56,48},{64,56},{72,6... | collective-permute-start | bytes 1032200 | tf_op jit(solution)/shard_map/ppermute | solution.py:24
  12.9 8.2 %collective-permute-start.1 = (bf16[448,384]{1,0:T(8,128)(2,1)S(1)}, bf16[448,384]{1,0:T(8,128)(2,1)S(1)}, u32[]{:S(2)}, u32[]{:S(2)}) collective-permute-start(bf16[448,384]{1,0:T(8,128)(2,1)S(1)} %get-tuple-element.85), channel_id=1, source_target_pairs={{8,0},{16,8},{24,16},{32,24},{40,32},{48,40},{56,48},{64,56},{72,6... | collective-permute-start | bytes 1032200 | tf_op jit(solution)/shard_map/ppermute | solution.py:24
  15.5 5.6 %copy-start = (bf16[3,2,1,21,21,384]{5,1,4,3,2,0:T(2,128)(2,1)S(1)}, bf16[3,2,1,21,21,384]{5,1,4,3,2,0:T(2,128)(2,1)}, u32[]{:S(2)}) copy-start(bf16[3,2,1,21,21,384]{5,1,4,3,2,0:T(2,128)(2,1)} %param.12) | copy-start | bytes 6096388
  23.4 13.8 %collective-permute-start.2 = (bf16[448,384]{1,0:T(8,128)(2,1)S(1)}, bf16[448,384]{1,0:T(8,128)(2,1)S(1)}, u32[]{:S(2)}, u32[]{:S(2)}) collective-permute-start(bf16[448,384]{1,0:T(8,128)(2,1)S(1)} %get-tuple-element.96), channel_id=1, source_target_pairs={{8,0},{16,8},{24,16},{32,24},{40,32},{48,40},{56,48},{64,56},{72,6... | collective-permute-start | bytes 1032200 | tf_op jit(solution)/shard_map/ppermute | solution.py:24
  29.7 7.5 %collective-permute-start.3 = (bf16[448,384]{1,0:T(8,128)(2,1)S(1)}, bf16[448,384]{1,0:T(8,128)(2,1)S(1)}, u32[]{:S(2)}, u32[]{:S(2)}) collective-permute-start(bf16[448,384]{1,0:T(8,128)(2,1)S(1)} %get-tuple-element.98), channel_id=1, source_target_pairs={{8,0},{16,8},{24,16},{32,24},{40,32},{48,40},{56,48},{64,56},{72,6... | collective-permute-start | bytes 1032200 | tf_op jit(solution)/shard_map/ppermute | solution.py:24
  40.8 14.2 %collective-permute-start.4 = (bf16[2,448,384]{2,1,0:T(8,128)(2,1)S(1)}, bf16[2,448,384]{2,1,0:T(8,128)(2,1)S(1)}, u32[]{:S(2)}, u32[]{:S(2)}) collective-permute-start(bf16[2,448,384]{2,1,0:T(8,128)(2,1)S(1)} %get-tuple-element.111), channel_id=1, source_target_pairs={{8,0},{16,8},{24,16},{32,24},{40,32},{48,40},{56,48},{64,56},{72,6... | collective-permute-start | bytes 2064392 | tf_op jit(solution)/shard_map/ppermute | solution.py:24
  58.9 10.3 %collective-permute-start.5 = (bf16[96,896]{1,0:T(8,128)(2,1)S(1)}, bf16[96,896]{1,0:T(8,128)(2,1)S(1)}, u32[]{:S(2)}, u32[]{:S(2)}) collective-permute-start(bf16[96,896]{1,0:T(8,128)(2,1)S(1)} %get-tuple-element.136), channel_id=1, source_target_pairs={{0,4},{1,5},{2,6},{3,7},{4,0},{5,1},{6,2},{7,3},{8,12},{9,13},{10,... | collective-permute-start | bytes 516104 | tf_op jit(solution)/shard_map/ppermute | solution.py:30
  62.2 7.5 %collective-permute-start.6 = (bf16[96,896]{1,0:T(8,128)(2,1)S(1)}, bf16[96,896]{1,0:T(8,128)(2,1)S(1)}, u32[]{:S(2)}, u32[]{:S(2)}) collective-permute-start(bf16[96,896]{1,0:T(8,128)(2,1)S(1)} %get-tuple-element.137), channel_id=1, source_target_pairs={{0,2},{1,3},{2,4},{3,5},{4,6},{5,7},{6,0},{7,1},{8,10},{9,11},{10,... | collective-permute-start | bytes 516104 | tf_op jit(solution)/shard_map/ppermute | solution.py:30
  62.8 6.8 %collective-permute-start.7 = (bf16[96,896]{1,0:T(8,128)(2,1)S(1)}, bf16[96,896]{1,0:T(8,128)(2,1)S(1)}, u32[]{:S(2)}, u32[]{:S(2)}) collective-permute-start(bf16[96,896]{1,0:T(8,128)(2,1)S(1)} %get-tuple-element.138), channel_id=1, source_target_pairs={{0,6},{1,7},{2,0},{3,1},{4,2},{5,3},{6,4},{7,5},{8,14},{9,15},{10,... | collective-permute-start | bytes 516104 | tf_op jit(solution)/shard_map/ppermute | solution.py:30
  69.7 6.1 %collective-permute-start.8 = (bf16[48,896]{1,0:T(8,128)(2,1)S(1)}, bf16[48,896]{1,0:T(8,128)(2,1)S(1)}, u32[]{:S(2)}, u32[]{:S(2)}) collective-permute-start(bf16[48,896]{1,0:T(8,128)(2,1)S(1)} %get-tuple-element.150), channel_id=1, source_target_pairs={{0,1},{1,0},{2,3},{3,2},{4,5},{5,4},{6,7},{7,6},{8,9},{9,8},{10,11... | collective-permute-start | bytes 258056 | tf_op jit(solution)/shard_map/ppermute | solution.py:34

commit v6 on v5

--- a/solution.py
+++ b/solution.py
@@ -283,40 +283,41 @@
     three_part(0, grad_out, act_older, weight, taps, back, grad_older, wide, dense, ready)
 
 
-def take(t, top_ref, out_in, pass_in, head_hbm, grad_out, grad_pass, head_in, sem):
+def take(t, top_ref, out_in, head_hbm, grad_out, head_pass, head_in, sem):
     @pl.when(top_ref[0] == 1)
     def _():
         get = pltpu.make_async_copy(head_hbm.at[t - 1], head_in, sem)
         get.start()
         get.wait()
-        pair_unpacked(head_in, grad_out, grad_pass)
+        pair_unpacked(head_in, grad_out, head_pass)
 
     @pl.when(top_ref[0] != 1)
     def _():
         grad_out[...] = out_in[...]
-        grad_pass[...] = pass_in[...]
 
 
 def five_kernel(
-    t,
-    top_ref,
-    out_in,
-    pass_in,
-    head_hbm,
-    act_last,
-    weight,
-    taps,
-    grad_last,
-    grad_out,
-    back,
-    grad_pass,
-    head_in,
-    wide,
-    dense,
-    sem,
+    t, top_ref, out_in, head_hbm, weight, taps, through, grad_out, head_pass, back, head_in, wide, dense, sem
 ):
-    take(t, top_ref, out_in, pass_in, head_hbm, grad_out, grad_pass, head_in, sem)
-    five_part(t, grad_out, grad_pass, act_last, weight, taps, back, grad_last, wide, dense, lambda: None)
+    take(t, top_ref, out_in, head_hbm, grad_out, head_pass, head_in, sem)
+    spread_taps(taps, wide, 25)
+    dense_product(grad_out[...], weight, dense)
+    to_pitched(dense, back)
+    spread_conv(back, wide, through, 5, True)
+
+
+def finish(t, top_ref, pass_in, head_pass, grad_out, act_last, through, grad_last):
+    @pl.when(top_ref[0] == 1)
+    def _():
+        finish_last(act_last, t, through, grad_out, head_pass, grad_last)
+
+    @pl.when(top_ref[0] != 1)
+    def _():
+        finish_last(act_last, t, through, grad_out, pass_in, grad_last)
+
+
+def finish_kernel(t, top_ref, pass_in, head_pass, grad_out, act_last, through, grad_last):
+    finish(t, top_ref, pass_in, head_pass, grad_out, act_last, through, grad_last)
 
 
 def three_kernel(t, grad_out, act_older, weight, taps, grad_older, back, wide, dense):
@@ -326,52 +327,21 @@
 def both_kernel(
     t,
     top_ref,
-    out_in,
     pass_in,
-    head_hbm,
+    head_pass,
+    grad_out,
     act_last,
     act_older,
-    weight_five,
-    weight_three,
-    taps_five,
-    taps_three,
+    through,
+    weight,
+    taps,
     made,
-    grad_out,
-    back_five,
-    back_three,
-    grad_pass,
-    head_in,
-    wide_five,
-    wide_three,
+    back,
+    wide,
     dense,
-    sem,
 ):
-    take(t, top_ref, out_in, pass_in, head_hbm, grad_out, grad_pass, head_in, sem)
-    three_part(
-        t,
-        grad_out,
-        act_older,
-        weight_three,
-        taps_three,
-        back_three,
-        made.at[1],
-        wide_three,
-        dense,
-        lambda: None,
-    )
-    five_part(
-        t,
-        grad_out,
-        grad_pass,
-        act_last,
-        weight_five,
-        taps_five,
-        back_five,
-        made.at[0],
-        wide_five,
-        dense,
-        lambda: None,
-    )
+    three_part(t, grad_out, act_older, weight, taps, back, made.at[1], wide, dense, lambda: None)
+    finish(t, top_ref, pass_in, head_pass, grad_out, act_last, through, made.at[0])
 
 
 def copies(pairs, sems):
@@ -409,32 +379,41 @@
     return lax.dot_general(mixed, left, (((0,), (0,)), ((), ())), preferred_element_type=F32)
 
 
-def grads_kernel(t, ahead, *refs):
-    refs = list(refs)
-    grad_out, act_last, act_older, taps_five, taps_three, back_five, back_three = refs[:7]
-    refs = refs[7:]
-    olds = None
+def grads_kernel(t, *refs):
+    act_last, act_older, taps_five, taps_three, back_five, back_three = refs[:6]
+    refs = refs[6:]
+    olds = (None, None)
     if t > 0:
-        olds = refs[:4]
-        refs = refs[4:]
-    sums = refs[:4]
-    refs = refs[4:]
-    if ahead is not None:
-        later = refs[:4]
-        refs = refs[4:]
+        olds, refs = refs[:2], refs[2:]
+    sums, mixes = refs[:2], refs[2:4]
+    pitched, dense, wide = refs[4:]
+    for act, taps, back, kernel, old, total, mixed in (
+        (act_last, taps_five, back_five, 5, olds[0], sums[0], mixes[0]),
+        (act_older, taps_three, back_three, 3, olds[1], sums[1], mixes[1]),
+    ):
+        mix(act, t, taps, mixed, pitched, dense, wide, kernel)
+        tap_sums(back, pitched, total, kernel)
+        if old is not None:
+            total[...] = total[...] + old[...]
+
+
+def gather_kernel(t, *refs):
+    act_last, act_older, taps_five, taps_three, back_five, back_three = refs[:6]
+    old_taps, refs = refs[6:8], refs[8:]
+    grads, refs = refs[: t + 1], refs[t + 1 :]
+    mixed_before, refs = refs[: 2 * t], refs[2 * t :]
+    points, sums, ahead, refs = refs[:2], refs[2:4], refs[4:8], refs[8:]
     pitched, dense, wide, mixed = refs
-    left = grad_out[...]
     for n, (act, taps, back, kernel) in enumerate(
         ((act_last, taps_five, back_five, 5), (act_older, taps_three, back_three, 3))
     ):
-        if ahead is not None:
-            mix(act, ahead, taps, later[n], later[2 + n], dense, wide, kernel)
+        mix(act, t + 1, taps, ahead[n], ahead[2 + n], dense, wide, kernel)
         mix(act, t, taps, mixed, pitched, dense, wide, kernel)
-        got = across(mixed[...], left)
-        sums[2 * n][...] = got if olds is None else got + olds[2 * n][...]
-        tap_sums(back, pitched, sums[2 * n + 1], kernel)
-        if olds is not None:
-            sums[2 * n + 1][...] = sums[2 * n + 1][...] + olds[2 * n + 1][...]
+        points[n][...] = across(mixed[...], grads[t][...])
+        for before in range(t):
+            points[n][...] += across(mixed_before[2 * before + n][...], grads[before][...])
+        tap_sums(back, pitched, sums[n], kernel)
+        sums[n][...] = sums[n][...] + old_taps[n][...]
 
 
 def last_grads_kernel(
@@ -450,8 +429,8 @@
     pitched_five,
     pitched_three,
     old_five,
+    old_three,
     old_taps_five,
-    old_three,
     old_taps_three,
     *refs,
 ):
@@ -459,7 +438,12 @@
     own, grad_out, grad_pass, back_five, back_three = refs[:5]
     packed, head_in, dense, rows_ref, sem = refs[5:]
     scale = 1.0 / PIXELS
-    take(t, top_ref, pair_in.at[0], pair_in.at[1], head_hbm, grad_out, grad_pass, head_in, sem)
+    take(t, top_ref, pair_in.at[0], head_hbm, grad_out, grad_pass, head_in, sem)
+
+    @pl.when(top_ref[0] != 1)
+    def _():
+        grad_pass[...] = pair_in[1]
+
     left = grad_out[...]
     packed[:, 0:CH] = (across(mixed_five[...], left) + old_five[...]) * scale
     packed[:, CH : 2 * CH] = (across(mixed_three[...], left) + old_three[...]) * scale
@@ -568,14 +552,11 @@
 ANY = pl.BlockSpec(memory_space=pl.ANY)
 FLAT = jax.ShapeDtypeStruct((ROWS, CH), BF16)
 WIDE = 2 * CH + 128
+THROUGH = jax.ShapeDtypeStruct((BLOCKS, ROWS + 8, 128), F32)
 ACTS = jax.ShapeDtypeStruct((4, ROWS, CH), BF16)
 BACK = jax.ShapeDtypeStruct((BLOCKS, PITCHED, 128), F32)
-SUMS = (
-    jax.ShapeDtypeStruct((CH, CH), F32),
-    jax.ShapeDtypeStruct((32, CH), F32),
-    jax.ShapeDtypeStruct((CH, CH), F32),
-    jax.ShapeDtypeStruct((16, CH), F32),
-)
+POINTS = jax.ShapeDtypeStruct((CH, CH), F32)
+SUMS = (jax.ShapeDtypeStruct((32, CH), F32), jax.ShapeDtypeStruct((16, CH), F32))
 FLAT_SCRATCH = pltpu.VMEM((ROWS, CH), BF16)
 PAIR_SCRATCH = pltpu.VMEM((PIXELS, 2, CH), BF16)
 WIDE_FIVE = pltpu.VMEM((25, BLOCKS, 8, 128), F32)
@@ -638,17 +619,31 @@
     )
 
 
-def call_five(t, given, act, weight, taps):
+def call_five(t, given, weight, taps):
     return run(
         functools.partial(five_kernel, t),
         f"five_{t}",
-        (*given, act, weight, taps),
-        [SMEM, VMEM, VMEM, ANY] + [VMEM] * 3,
-        (FLAT, FLAT, BACK),
-        (VMEM,) * 3,
-        [FLAT_SCRATCH, PAIR_SCRATCH, WIDE_FIVE, DENSE, pltpu.SemaphoreType.DMA],
+        (*given, weight, taps),
+        [SMEM, VMEM, ANY] + [VMEM] * 2,
+        (THROUGH, FLAT, FLAT, BACK),
+        (VMEM,) * 4,
+        [PAIR_SCRATCH, WIDE_FIVE, DENSE, pltpu.SemaphoreType.DMA],
         3,
     )
+
+
+def call_finish(t, *operands):
+    (grad_last,) = run(
+        functools.partial(finish_kernel, t),
+        f"finish_{t}",
+        operands,
+        [SMEM] + [VMEM] * 5,
+        (FLAT,),
+        (VMEM,),
+        [],
+        1,
+    )
+    return grad_last
 
 
 def call_three(t, grad_out, act, weight, taps):
@@ -664,31 +659,44 @@
     )
 
 
-def call_both(t, given, acts, weights, taps):
+def call_both(t, *operands):
     return run(
         functools.partial(both_kernel, t),
         f"both_{t}",
-        (*given, *acts, *weights, *taps),
-        [SMEM, VMEM, VMEM, ANY] + [VMEM] * 6,
-        (jax.ShapeDtypeStruct((2, ROWS, CH), BF16), FLAT, BACK, BACK),
-        (VMEM,) * 4,
-        [FLAT_SCRATCH, PAIR_SCRATCH, WIDE_FIVE, WIDE_THREE, DENSE, pltpu.SemaphoreType.DMA],
-        5,
-    )
-
-
-def call_grads(t, ahead, grad_out, acts, taps, backs, olds):
-    shapes = SUMS if ahead is None else SUMS + (FLAT, FLAT, BACK, BACK)
-    operands = (grad_out, *acts, *taps, *backs, *olds)
+        operands,
+        [SMEM] + [VMEM] * 8,
+        (jax.ShapeDtypeStruct((2, ROWS, CH), BF16), BACK),
+        (VMEM,) * 2,
+        [WIDE_THREE, DENSE],
+        2,
+    )
+
+
+def call_grads(t, acts, taps, backs, olds):
+    operands = (*acts, *taps, *backs, *olds)
     return run(
-        functools.partial(grads_kernel, t, ahead),
+        functools.partial(grads_kernel, t),
         f"grads_{t}",
         operands,
         [VMEM] * len(operands),
-        shapes,
-        (VMEM,) * len(shapes),
+        (*SUMS, FLAT, FLAT),
+        (VMEM,) * 4,
+        [PITCHED_SCRATCH, DENSE, WIDE_FIVE],
+        5,
+    )
+
+
+def call_gather(t, acts, taps, backs, olds, grads, mixes):
+    operands = (*acts, *taps, *backs, *olds, *grads, *mixes)
+    return run(
+        functools.partial(gather_kernel, t),
+        f"gather_{t}",
+        operands,
+        [VMEM] * len(operands),
+        (POINTS, POINTS, *SUMS, FLAT, FLAT, BACK, BACK),
+        (VMEM,) * 8,
         [PITCHED_SCRATCH, DENSE, WIDE_FIVE, FLAT_SCRATCH],
-        6 if ahead is None else 8,
+        10,
     )
 
 
@@ -792,23 +800,25 @@
     )
     next_pass = from_next(grad_older)
     acts = (act_last, act_older)
-    sums = ()
+    sums, mixes, grads = (), (), (grad_out,)
     for t in range(turns - 2):
-        made = call_grads(t, None, grad_out, acts, taps, (back_five, back_three), sums)
-        next_out, next_pass, sums = lax.optimization_barrier((next_out, next_pass, made))
-        given = (top, next_out, next_pass, head)
+        made = call_grads(t, acts, taps, (back_five, back_three), sums)
+        next_out, made = lax.optimization_barrier((next_out, made))
+        sums, mixes = made[:2], (*mixes, *made[2:])
+        through, grad_out, head_pass, back_five = call_five(
+            t + 1, (top, next_out, head), weights[0], taps[0]
+        )
+        grads = (*grads, grad_out)
+        skip = (top, next_pass, head_pass, grad_out)
         if t < turns - 3:
-            grad_last, grad_out, back_five = call_five(
-                t + 1, given, act_last, weights[0], taps[0]
-            )
+            grad_last = call_finish(t + 1, *skip, act_last, through)
             next_out = from_next(grad_last)
-            grad_older, back_three = call_three(t + 1, grad_out, act_older, weights[1], taps[1])
+            ready, _ = lax.optimization_barrier((grad_out, grad_last))
+            grad_older, back_three = call_three(t + 1, ready, act_older, weights[1], taps[1])
             next_pass = from_next(grad_older)
-    both, grad_out, back_five, back_three = call_both(turns - 2, given, acts, weights, taps)
+    both, back_three = call_both(turns - 2, *skip, *acts, through, weights[1], taps[1])
     next_pair = from_next(both)
-    made = call_grads(
-        turns - 2, turns - 1, grad_out, acts, taps, (back_five, back_three), sums
-    )
+    made = call_gather(turns - 2, acts, taps, (back_five, back_three), sums, grads, mixes)
     next_pair, made = lax.optimization_barrier((next_pair, made))
     *sends, own, grad_out, grad_pass, back_five, back_three = call_last_grads(
         turns - 1,

time: 77.1 us -> 73.8 us (0.957)
  starting transfers between devices: 28.7 us -> 26.6 us
  Pallas kernels: 42.7 us -> 41.4 us
    ppermute x5, starting transfers between devices: 18.8 us -> 16.8 us  [from_next(): return lax.ppermute(block, 'sec', [(i + 1, i) for i in range(size - 1)])]
    pallas_call x12 -> x14, Pallas kernels: 42 us -> 40.7 us  [run(): pl.pallas_call(kernel, out_shape=tuple(shapes), in_specs=specs, out_specs...]
  transfers between devices with their start and end apart: 9 -> 9, of which waited for: 2 -> 2; matrix products, arithmetic and copies ran while one was open for 0% -> 0% of each run, Pallas kernels for 35% -> 41%
where the time goes in v6:
time: 73.8 us; the launch traced here: 73.3 us
  Pallas kernels  41.4 us (56%)
  starting transfers between devices  26.6 us (36%)
  waiting for transfers between devices  3.34 us (5%)
  local copies, waits for them, and re-layouts  1 us (1%)
  between operations  0.95 us (1%)
    pallas_call x14, Pallas kernels, run(): pl.pallas_call(kernel, out_shape=tuple(shapes), in_specs=specs, out_specs...  40.7 us
    ppermute x5, starting transfers between devices, from_next(): return lax.ppermute(block, 'sec', [(i + 1, i) for i in range(size - 1)])  16.8 us
    ppermute x3, starting transfers between devices, around_rows(): return lax.ppermute(block, 'img', route)  6.53 us
    ppermute x1, starting transfers between devices, with_partner(): lax.ppermute(block, 'img', [(i, i ^ 1) for i in range(lax.axis_size('img'...  3.31 us
    ppermute x1, waiting for transfers between devices, with_partner(): lax.ppermute(block, 'img', [(i, i ^ 1) for i in range(lax.axis_size('img'...  2.76 us
  transfers between devices with their start and end apart: 9, of which 2 were waited for; matrix products, arithmetic and copies ran while one was open for 0% of the time, Pallas kernels for 41%

profile of v6, /device:TPU:32, one launch (start us, length us, event | category | flops | bytes accessed | tf_op | source)
XLA Modules:
  0.0 73.3 jit_solution(363098818694944642)
XLA Ops:
  0.6 0.0 copy-start.1
  0.7 0.0 copy-start.3
  0.7 0.0 copy-start.4
  0.7 0.0 copy-start.6
  0.7 0.0 copy-start.8
  0.7 0.5 opening.1.token_ref
  1.3 0.7 copy-done.1
  2.0 0.2 copy-done.3
  2.1 0.1 copy-done.4
  2.2 0.0 copy-done.6
  2.2 0.0 copy-done.8
  2.2 0.0 copy-start.7
  2.2 4.6 %first_five.1 = (bf16[448,384]{1,0:T(8,128)(2,1)S(1)}, bf16[4,448,384]{2,1,0:T(8,128)(2,1)S(1)}, bf16[448,384]{1,0:T(8,128)(2,1)S(1)}, f32[3,616,128]{2,1,0:T(8,128)S(1)}) custom-call(s32[1]{0:T(128)} %opening.1.token_ref, s32[1,4]{1,0:T(1,128)S(1)} %copy-done.8, bf16[441,4,384]{2,1,0:T(4,128)(2,1)S(1)} %bitcast.29, bf16[441,2,384]{2,1,0:T(2,128)(2,1)S(1)} %bitcast.31, ...), custom_call_target="tpu_custom_call" | custom-call | flops 4000000000 | tf_op jit(solution)/shard_map/first_five/pallas_call | solution.py:570
  6.9 3.7 %collective-permute-start = (bf16[448,384]{1,0:T(8,128)(2,1)S(1)}, bf16[448,384]{1,0:T(8,128)(2,1)S(1)}, u32[]{:S(2)}, u32[]{:S(2)}) collective-permute-start(bf16[448,384]{1,0:T(8,128)(2,1)S(1)} %get-tuple-element.85), channel_id=1, source_target_pairs={{8,0},{16,8},{24,16},{32,24},{40,32},{48,40},{56,48},{64,56},{72,6... | collective-permute-start | bytes 1032200 | tf_op jit(solution)/shard_map/ppermute | solution.py:24
  10.5 0.0 copy-done.2
  10.5 0.0 copy-done.5
  10.5 0.0 copy-done.7
  10.5 2.4 %first_three.1 = (bf16[448,384]{1,0:T(8,128)(2,1)S(1)}, bf16[4,448,384]{2,1,0:T(8,128)(2,1)S(1)}, f32[3,616,128]{2,1,0:T(8,128)S(1)}) custom-call(s32[1,4]{1,0:T(1,128)S(1)} %copy-done.8, bf16[441,4,384]{2,1,0:T(4,128)(2,1)S(1)} %bitcast.30, bf16[448,384]{1,0:T(8,128)(2,1)S(1)} %get-tuple-element.87.grad_out.refs_8_, bf16[384,384]{1,0:T(8,128)(2,1)S(1)} %bitcast.36, ...), custom_call_target="tpu_custom_call" | custom-call | flops 3000000000 | tf_op jit(solution)/shard_map/first_three/pallas_call | solution.py:570
  12.9 2.6 %collective-permute-start.1 = (bf16[448,384]{1,0:T(8,128)(2,1)S(1)}, bf16[448,384]{1,0:T(8,128)(2,1)S(1)}, u32[]{:S(2)}, u32[]{:S(2)}) collective-permute-start(bf16[448,384]{1,0:T(8,128)(2,1)S(1)} %get-tuple-element.97), channel_id=1, source_target_pairs={{8,0},{16,8},{24,16},{32,24},{40,32},{48,40},{56,48},{64,56},{72,6... | collective-permute-start | bytes 1032200 | tf_op jit(solution)/shard_map/ppermute | solution.py:24
  15.5 0.0 copy-start
  15.5 4.7 %grads_0.1 = (f32[32,384]{1,0:T(8,128)S(1)}, f32[16,384]{1,0:T(8,128)S(1)}, bf16[448,384]{1,0:T(8,128)(2,1)S(1)}, bf16[448,384]{1,0:T(8,128)(2,1)S(1)}) custom-call(bf16[4,448,384]{2,1,0:T(8,128)(2,1)S(1)} %get-tuple-element.86.refs_0_.act_last, bf16[4,448,384]{2,1,0:T(8,128)(2,1)S(1)} %get-tuple-element.88.refs_1_.act_older, bf16[25,384]{1,0:T(8,128)(2,1)S(1)} %bitcast.41, ...), custom_call_target="tpu_custom_call" | custom-call | flops 5000000000 | tf_op jit(solution)/shard_map/grads_0/pallas_call | solution.py:570
  20.3 0.0 collective-permute-done.out_in
  20.3 1.8 %five_1.1 = (f32[3,456,128]{2,1,0:T(8,128)S(1)}, bf16[448,384]{1,0:T(8,128)(2,1)S(1)}, bf16[448,384]{1,0:T(8,128)(2,1)S(1)}, f32[3,616,128]{2,1,0:T(8,128)S(1)}) custom-call(s32[1]{0:T(128)} %bitcast.top_ref, bf16[448,384]{1,0:T(8,128)(2,1)S(1)} %collective-permute-done.out_in, bf16[3,441,2,384]{3,2,1,0:T(2,128)(2,1)S(1)} %bitcast.26, ...), custom_call_target="tpu_custom_call" | custom-call | flops 3000000000 | tf_op jit(solution)/shard_map/five_1/pallas_call | solution.py:570
  22.1 0.0 collective-permute-done.1.pass_in
  22.2 0.4 finish_1.1
  22.5 4.0 %collective-permute-start.3 = (bf16[448,384]{1,0:T(8,128)(2,1)S(1)}, bf16[448,384]{1,0:T(8,128)(2,1)S(1)}, u32[]{:S(2)}, u32[]{:S(2)}) collective-permute-start(bf16[448,384]{1,0:T(8,128)(2,1)S(1)} %finish_1.1), channel_id=1, source_target_pairs={{8,0},{16,8},{24,16},{32,24},{40,32},{48,40},{56,48},{64,56},{72,6... | collective-permute-start | bytes 1032200 | tf_op jit(solution)/shard_map/ppermute | solution.py:24
  26.6 1.2 %three_1.1 = (bf16[448,384]{1,0:T(8,128)(2,1)S(1)}, f32[3,616,128]{2,1,0:T(8,128)S(1)}) custom-call(bf16[448,384]{1,0:T(8,128)(2,1)S(1)} %get-tuple-element.100.grad_out.refs_9_, bf16[4,448,384]{2,1,0:T(8,128)(2,1)S(1)} %get-tuple-element.88.refs_1_.act_older, bf16[384,384]{1,0:T(8,128)(2,1)S(1)} %bitcast.37, bf16[9,384]{1,0:T(8,128)(2,1)S(1)} %bitcast.49), custom_call_target="tpu_custom_call" | custom-call | flops 2000000000 | tf_op jit(solution)/shard_map/three_1/pallas_call | solution.py:570
  27.8 1.9 %collective-permute-start.2 = (bf16[448,384]{1,0:T(8,128)(2,1)S(1)}, bf16[448,384]{1,0:T(8,128)(2,1)S(1)}, u32[]{:S(2)}, u32[]{:S(2)}) collective-permute-start(bf16[448,384]{1,0:T(8,128)(2,1)S(1)} %get-tuple-element.101), channel_id=1, source_target_pairs={{8,0},{16,8},{24,16},{32,24},{40,32},{48,40},{56,48},{64,56},{72,6... | collective-permute-start | bytes 1032200 | tf_op jit(solution)/shard_map/ppermute | solution.py:24
  29.7 4.8 %grads_1.1 = (f32[32,384]{1,0:T(8,128)S(1)}, f32[16,384]{1,0:T(8,128)S(1)}, bf16[448,384]{1,0:T(8,128)(2,1)S(1)}, bf16[448,384]{1,0:T(8,128)(2,1)S(1)}) custom-call(bf16[4,448,384]{2,1,0:T(8,128)(2,1)S(1)} %get-tuple-element.86.refs_0_.act_last, bf16[4,448,384]{2,1,0:T(8,128)(2,1)S(1)} %get-tuple-element.88.refs_1_.act_older, bf16[25,384]{1,0:T(8,128)(2,1)S(1)} %bitcast.43, ...), custom_call_target="tpu_custom_call" | custom-call | flops 5000000000 | tf_op jit(solution)/shard_map/grads_1/pallas_call | solution.py:570
  34.4 0.0 collective-permute-done.3.out_in
  34.5 1.8 %five_2.1 = (f32[3,456,128]{2,1,0:T(8,128)S(1)}, bf16[448,384]{1,0:T(8,128)(2,1)S(1)}, bf16[448,384]{1,0:T(8,128)(2,1)S(1)}, f32[3,616,128]{2,1,0:T(8,128)S(1)}) custom-call(s32[1]{0:T(128)} %bitcast.top_ref, bf16[448,384]{1,0:T(8,128)(2,1)S(1)} %collective-permute-done.3.out_in, bf16[3,441,2,384]{3,2,1,0:T(2,128)(2,1)S(1)} %bitcast.27, ...), custom_call_target="tpu_custom_call" | custom-call | flops 3000000000 | tf_op jit(solution)/shard_map/five_2/pallas_call | solution.py:570
  36.3 0.0 collective-permute-done.2.pass_in
  36.3 1.6 %both_2.1 = (bf16[2,448,384]{2,1,0:T(8,128)(2,1)S(1)}, f32[3,616,128]{2,1,0:T(8,128)S(1)}) custom-call(s32[1]{0:T(128)} %bitcast.top_ref, bf16[448,384]{1,0:T(8,128)(2,1)S(1)} %collective-permute-done.2.pass_in, bf16[448,384]{1,0:T(8,128)(2,1)S(1)} %get-tuple-element.111.head_pass, bf16[448,384]{1,0:T(8,128)(2,1)S(1)} %get-tuple-element.112.grad_out.refs_10_, ...), custom_call_target="tpu_custom_call" | custom-call | flops 2000000000 | tf_op jit(solution)/shard_map/both_2/pallas_call | solution.py:570
  37.9 4.6 %collective-permute-start.4 = (bf16[2,448,384]{2,1,0:T(8,128)(2,1)S(1)}, bf16[2,448,384]{2,1,0:T(8,128)(2,1)S(1)}, u32[]{:S(2)}, u32[]{:S(2)}) collective-permute-start(bf16[2,448,384]{2,1,0:T(8,128)(2,1)S(1)} %get-tuple-element.114), channel_id=1, source_target_pairs={{8,0},{16,8},{24,16},{32,24},{40,32},{48,40},{56,48},{64,56},{72,6... | collective-permute-start | bytes 2064392 | tf_op jit(solution)/shard_map/ppermute | solution.py:24
  42.5 9.4 %gather_2.1 = (f32[384,384]{1,0:T(8,128)S(1)}, f32[384,384]{1,0:T(8,128)S(1)}, f32[32,384]{1,0:T(8,128)S(1)}, f32[16,384]{1,0:T(8,128)S(1)}, bf16[448,384]{1,0:T...) custom-call(bf16[4,448,384]{2,1,0:T(8,128)(2,1)S(1)} %get-tuple-element.86.re, ...), custom_call_target="tpu_custom_call" | custom-call | flops 10000000000 | tf_op jit(solution)/shard_map/gather_2/pallas_call | solution.py:570
  51.9 0.0 collective-permute-done.4.pair_in
  51.9 3.7 %last_grads.1 = (bf16[96,896]{1,0:T(8,128)(2,1)S(1)}, bf16[96,896]{1,0:T(8,128)(2,1)S(1)}, bf16[96,896]{1,0:T(8,128)(2,1)S(1)}, f32[96,896]{1,0:T(8,128)S(1)}, b...) custom-call(s32[1]{0:T(128)} %bitcast.top_ref, ...), custom_call_target="tpu_custom_call" | custom-call | flops 6000000000 | tf_op jit(solution)/shard_map/last_grads/pallas_call | solution.py:570
  55.6 3.3 %collective-permute-start.5 = (bf16[96,896]{1,0:T(8,128)(2,1)S(1)}, bf16[96,896]{1,0:T(8,128)(2,1)S(1)}, u32[]{:S(2)}, u32[]{:S(2)}) collective-permute-start(bf16[96,896]{1,0:T(8,128)(2,1)S(1)} %get-tuple-element.140), channel_id=1, source_target_pairs={{0,4},{1,5},{2,6},{3,7},{4,0},{5,1},{6,2},{7,3},{8,12},{9,13},{10,... | collective-permute-start | bytes 516104 | tf_op jit(solution)/shard_map/ppermute | solution.py:30
  58.9 0.7 collective-permute-start.6
  59.5 2.6 %collective-permute-start.7 = (bf16[96,896]{1,0:T(8,128)(2,1)S(1)}, bf16[96,896]{1,0:T(8,128)(2,1)S(1)}, u32[]{:S(2)}, u32[]{:S(2)}) collective-permute-start(bf16[96,896]{1,0:T(8,128)(2,1)S(1)} %get-tuple-element.142), channel_id=1, source_target_pairs={{0,6},{1,7},{2,0},{3,1},{4,2},{5,3},{6,4},{7,5},{8,14},{9,15},{10,... | collective-permute-start | bytes 516104 | tf_op jit(solution)/shard_map/ppermute | solution.py:30
  62.1 3.8 %last.1 = bf16[441,2,384]{2,1,0:T(2,128)(2,1)} custom-call(bf16[448,384]{1,0:T(8,128)(2,1)S(1)} %get-tuple-element.143.grad_out, bf16[448,384]{1,0:T(8,128)(2,1)S(1)} %get-tuple-element.144.grad_pass, f32[3,616,128]{2,1,0:T(8,128)S(1)} %get-tuple-element.145.back_five, f32[3,616,128]{2,1,0:T(8,128)S(1)} %get-tuple-element.146.back_three, ...), custom_call_target="tpu_custom_call" | custom-call | flops 4000000000 | tf_op jit(solution)/shard_map/last/pallas_call | solution.py:570
  65.9 0.0 collective-permute-done.5.one
  65.9 0.6 collective-permute-done.6.two
  66.4 0.0 collective-permute-done.7.three
  66.4 0.1 half_total.1
  66.5 3.3 %collective-permute-start.8 = (bf16[48,896]{1,0:T(8,128)(2,1)S(1)}, bf16[48,896]{1,0:T(8,128)(2,1)S(1)}, u32[]{:S(2)}, u32[]{:S(2)}) collective-permute-start(bf16[48,896]{1,0:T(8,128)(2,1)S(1)} %get-tuple-element.154), channel_id=1, source_target_pairs={{0,1},{1,0},{2,3},{3,2},{4,5},{5,4},{6,7},{7,6},{8,9},{9,8},{10,11... | collective-permute-start | bytes 258056 | tf_op jit(solution)/shard_map/ppermute | solution.py:34
  69.8 2.8 %collective-permute-done.8.landed = bf16[48,896]{1,0:T(8,128)(2,1)S(1)} collective-permute-done((bf16[48,896]{1,0:T(8,128)(2,1)S(1)}, bf16[48,896]{1,0:T(8,128)(2,1)S(1)}, u32[]{:S(2)}, u32[]{:S(2)}) %collective-permute-start.8) | collective-permute-done | bytes 86048 | tf_op jit(solution)/shard_map/ppermute | solution.py:34
  72.6 0.7 total.1
  (3 shorter events, 0.0 us)
Async XLA Ops:
  0.6 1.3 %copy-start.1 = (bf16[1,4,1,21,21,384]{5,1,4,3,2,0:T(4,128)(2,1)S(1)}, bf16[1,4,1,21,21,384]{5,1,4,3,2,0:T(4,128)(2,1)}, u32[]{:S(2)}) copy-start(bf16[1,4,1,21,21,384]{5,1,4,3,2,0:T(4,128)(2,1)} %param.9) | copy-start | bytes 4064260
  0.7 1.5 %copy-start.3 = (bf16[1,2,1,21,21,384]{5,1,4,3,2,0:T(2,128)(2,1)S(1)}, bf16[1,2,1,21,21,384]{5,1,4,3,2,0:T(2,128)(2,1)}, u32[]{:S(2)}) copy-start(bf16[1,2,1,21,21,384]{5,1,4,3,2,0:T(2,128)(2,1)} %param.11) | copy-start | bytes 2032132
  0.7 1.6 %copy-start.4 = (bf16[1,384,384]{2,1,0:T(8,128)(2,1)S(1)}, bf16[1,384,384]{2,1,0:T(8,128)(2,1)}, u32[]{:S(2)}) copy-start(bf16[1,384,384]{2,1,0:T(8,128)(2,1)} %param.16) | copy-start | bytes 884740
  0.7 1.5 %copy-start.6 = (bf16[1,25,384]{2,1,0:T(8,128)(2,1)S(1)}, bf16[1,25,384]{2,1,0:T(8,128)(2,1)}, u32[]{:S(2)}) copy-start(bf16[1,25,384]{2,1,0:T(8,128)(2,1)} %param.14) | copy-start | bytes 57604
  0.7 1.5 %copy-start.8 = (s32[1,4]{1,0:T(1,128)S(1)}, s32[1,4]{1,0:T(1,128)}, u32[]{:S(2)}) copy-start(s32[1,4]{1,0:T(1,128)} %plan_ref.3) | copy-start | bytes 52
  2.2 8.3 %copy-start.2 = (bf16[1,4,1,21,21,384]{5,1,4,3,2,0:T(4,128)(2,1)S(1)}, bf16[1,4,1,21,21,384]{5,1,4,3,2,0:T(4,128)(2,1)}, u32[]{:S(2)}) copy-start(bf16[1,4,1,21,21,384]{5,1,4,3,2,0:T(4,128)(2,1)} %param.10) | copy-start | bytes 4064260
  2.2 8.3 %copy-start.5 = (bf16[1,384,384]{2,1,0:T(8,128)(2,1)S(1)}, bf16[1,384,384]{2,1,0:T(8,128)(2,1)}, u32[]{:S(2)}) copy-start(bf16[1,384,384]{2,1,0:T(8,128)(2,1)} %param.17) | copy-start | bytes 884740
  2.2 8.3 %copy-start.7 = (bf16[1,9,384]{2,1,0:T(8,128)(2,1)S(1)}, bf16[1,9,384]{2,1,0:T(8,128)(2,1)}, u32[]{:S(2)}) copy-start(bf16[1,9,384]{2,1,0:T(8,128)(2,1)} %param.15) | copy-start | bytes 20740
  6.9 13.4 %collective-permute-start = (bf16[448,384]{1,0:T(8,128)(2,1)S(1)}, bf16[448,384]{1,0:T(8,128)(2,1)S(1)}, u32[]{:S(2)}, u32[]{:S(2)}) collective-permute-start(bf16[448,384]{1,0:T(8,128)(2,1)S(1)} %get-tuple-element.85), channel_id=1, source_target_pairs={{8,0},{16,8},{24,16},{32,24},{40,32},{48,40},{56,48},{64,56},{72,6... | collective-permute-start | bytes 1032200 | tf_op jit(solution)/shard_map/ppermute | solution.py:24
  12.9 9.2 %collective-permute-start.1 = (bf16[448,384]{1,0:T(8,128)(2,1)S(1)}, bf16[448,384]{1,0:T(8,128)(2,1)S(1)}, u32[]{:S(2)}, u32[]{:S(2)}) collective-permute-start(bf16[448,384]{1,0:T(8,128)(2,1)S(1)} %get-tuple-element.97), channel_id=1, source_target_pairs={{8,0},{16,8},{24,16},{32,24},{40,32},{48,40},{56,48},{64,56},{72,6... | collective-permute-start | bytes 1032200 | tf_op jit(solution)/shard_map/ppermute | solution.py:24
  15.5 4.8 %copy-start = (bf16[3,2,1,21,21,384]{5,1,4,3,2,0:T(2,128)(2,1)S(1)}, bf16[3,2,1,21,21,384]{5,1,4,3,2,0:T(2,128)(2,1)}, u32[]{:S(2)}) copy-start(bf16[3,2,1,21,21,384]{5,1,4,3,2,0:T(2,128)(2,1)} %param.12) | copy-start | bytes 6096388
  22.5 11.9 %collective-permute-start.3 = (bf16[448,384]{1,0:T(8,128)(2,1)S(1)}, bf16[448,384]{1,0:T(8,128)(2,1)S(1)}, u32[]{:S(2)}, u32[]{:S(2)}) collective-permute-start(bf16[448,384]{1,0:T(8,128)(2,1)S(1)} %finish_1.1), channel_id=1, source_target_pairs={{8,0},{16,8},{24,16},{32,24},{40,32},{48,40},{56,48},{64,56},{72,6... | collective-permute-start | bytes 1032200 | tf_op jit(solution)/shard_map/ppermute | solution.py:24
  27.8 8.5 %collective-permute-start.2 = (bf16[448,384]{1,0:T(8,128)(2,1)S(1)}, bf16[448,384]{1,0:T(8,128)(2,1)S(1)}, u32[]{:S(2)}, u32[]{:S(2)}) collective-permute-start(bf16[448,384]{1,0:T(8,128)(2,1)S(1)} %get-tuple-element.101), channel_id=1, source_target_pairs={{8,0},{16,8},{24,16},{32,24},{40,32},{48,40},{56,48},{64,56},{72,6... | collective-permute-start | bytes 1032200 | tf_op jit(solution)/shard_map/ppermute | solution.py:24
  37.9 14.0 %collective-permute-start.4 = (bf16[2,448,384]{2,1,0:T(8,128)(2,1)S(1)}, bf16[2,448,384]{2,1,0:T(8,128)(2,1)S(1)}, u32[]{:S(2)}, u32[]{:S(2)}) collective-permute-start(bf16[2,448,384]{2,1,0:T(8,128)(2,1)S(1)} %get-tuple-element.114), channel_id=1, source_target_pairs={{8,0},{16,8},{24,16},{32,24},{40,32},{48,40},{56,48},{64,56},{72,6... | collective-permute-start | bytes 2064392 | tf_op jit(solution)/shard_map/ppermute | solution.py:24
  55.6 10.3 %collective-permute-start.5 = (bf16[96,896]{1,0:T(8,128)(2,1)S(1)}, bf16[96,896]{1,0:T(8,128)(2,1)S(1)}, u32[]{:S(2)}, u32[]{:S(2)}) collective-permute-start(bf16[96,896]{1,0:T(8,128)(2,1)S(1)} %get-tuple-element.140), channel_id=1, source_target_pairs={{0,4},{1,5},{2,6},{3,7},{4,0},{5,1},{6,2},{7,3},{8,12},{9,13},{10,... | collective-permute-start | bytes 516104 | tf_op jit(solution)/shard_map/ppermute | solution.py:30
  58.9 7.6 %collective-permute-start.6 = (bf16[96,896]{1,0:T(8,128)(2,1)S(1)}, bf16[96,896]{1,0:T(8,128)(2,1)S(1)}, u32[]{:S(2)}, u32[]{:S(2)}) collective-permute-start(bf16[96,896]{1,0:T(8,128)(2,1)S(1)} %get-tuple-element.141), channel_id=1, source_target_pairs={{0,2},{1,3},{2,4},{3,5},{4,6},{5,7},{6,0},{7,1},{8,10},{9,11},{10,... | collective-permute-start | bytes 516104 | tf_op jit(solution)/shard_map/ppermute | solution.py:30
  59.5 6.9 %collective-permute-start.7 = (bf16[96,896]{1,0:T(8,128)(2,1)S(1)}, bf16[96,896]{1,0:T(8,128)(2,1)S(1)}, u32[]{:S(2)}, u32[]{:S(2)}) collective-permute-start(bf16[96,896]{1,0:T(8,128)(2,1)S(1)} %get-tuple-element.142), channel_id=1, source_target_pairs={{0,6},{1,7},{2,0},{3,1},{4,2},{5,3},{6,4},{7,5},{8,14},{9,15},{10,... | collective-permute-start | bytes 516104 | tf_op jit(solution)/shard_map/ppermute | solution.py:30
  66.5 6.1 %collective-permute-start.8 = (bf16[48,896]{1,0:T(8,128)(2,1)S(1)}, bf16[48,896]{1,0:T(8,128)(2,1)S(1)}, u32[]{:S(2)}, u32[]{:S(2)}) collective-permute-start(bf16[48,896]{1,0:T(8,128)(2,1)S(1)} %get-tuple-element.154), channel_id=1, source_target_pairs={{0,1},{1,0},{2,3},{3,2},{4,5},{5,4},{6,7},{7,6},{8,9},{9,8},{10,11... | collective-permute-start | bytes 258056 | tf_op jit(solution)/shard_map/ppermute | solution.py:34

commit v7 on v6

--- a/solution.py
+++ b/solution.py
@@ -64,7 +64,7 @@
             pitched[c, pl.ds(at, PITCH), :] = jnp.where(inside, got, 0.0)
         return carry
 
-    lax.fori_loop(0, SIDE, row, 0, unroll=3)
+    lax.fori_loop(0, SIDE, row, 0, unroll=7)
 
 
 def add_window(sums, got, weight_of, b, shift, rows, kernel):
@@ -164,7 +164,7 @@
         put(pl.multiple_of(i * 16, 16), jnp.swapaxes(read(i), 0, 1))
         return carry
 
-    lax.fori_loop(0, whole, body, 0)
+    lax.fori_loop(0, whole, body, 0, unroll=9)
     put(whole * 16, jnp.swapaxes(tail, 0, 1))
 
 
@@ -191,7 +191,7 @@
             grad_older[rows, lanes(c)] = masked(act_older, t, dense, c, rows).astype(BF16)
         return carry
 
-    lax.fori_loop(0, ROWS // 16, body, 0)
+    lax.fori_loop(0, ROWS // 16, body, 0, unroll=7)
 
 
 def last_piece(act_last, t, dense, grad_out, grad_pass, c, rows):
@@ -206,7 +206,7 @@
             grad_last[rows, lanes(c)] = last_piece(act_last, t, dense, grad_out, grad_pass, c, rows)
         return carry
 
-    lax.fori_loop(0, ROWS // 16, body, 0)
+    lax.fori_loop(0, ROWS // 16, body, 0, unroll=7)
 
 
 def three_part(t, grad_out, act_older, weight, taps, back, grad_older, wide, dense, ready):
@@ -355,7 +355,7 @@
             dense[c, rows, :] = act[t, rows, lanes(c)].astype(F32)
         return carry
 
-    lax.fori_loop(0, ROWS // 16, body, 0)
+    lax.fori_loop(0, ROWS // 16, body, 0, unroll=14)
 
 
 def mix(act, t, taps, mixed, pitched, dense, wide, kernel):
@@ -372,7 +372,7 @@
             mixed[rows, lanes(c)] = dense[c, rows, :].astype(BF16)
         return carry
 
-    lax.fori_loop(0, ROWS // 16, body, 0)
+    lax.fori_loop(0, ROWS // 16, body, 0, unroll=14)
 
 
 def across(mixed, left):

time: 73.8 us -> 72 us (0.976)
  Pallas kernels: 41.4 us -> 38 us
  starting transfers between devices: 26.6 us -> 27.7 us
    pallas_call x14, Pallas kernels: 40.7 us -> 37.3 us  [run(): pl.pallas_call(kernel, out_shape=tuple(shapes), in_specs=specs, out_specs...]
    ppermute x5, starting transfers between devices: 16.8 us -> 17.8 us  [from_next(): return lax.ppermute(block, 'sec', [(i + 1, i) for i in range(size - 1)])]
  transfers between devices with their start and end apart: 9 -> 9, of which waited for: 2 -> 3; matrix products, arithmetic and copies ran while one was open for 0% -> 0% of each run, Pallas kernels for 41% -> 38%
where the time goes in v7:
time: 72 us; the launch traced here: 71.4 us
  Pallas kernels  38 us (53%)
  starting transfers between devices  27.7 us (38%)
  waiting for transfers between devices  3.78 us (5%)
  local copies, waits for them, and re-layouts  1 us (1%)
  between operations  0.92 us (1%)
    pallas_call x14, Pallas kernels, run(): pl.pallas_call(kernel, out_shape=tuple(shapes), in_specs=specs, out_specs...  37.3 us
    ppermute x5, starting transfers between devices, from_next(): return lax.ppermute(block, 'sec', [(i + 1, i) for i in range(size - 1)])  17.8 us
    ppermute x3, starting transfers between devices, around_rows(): return lax.ppermute(block, 'img', route)  6.49 us
    ppermute x1, starting transfers between devices, with_partner(): lax.ppermute(block, 'img', [(i, i ^ 1) for i in range(lax.axis_size('img'...  3.34 us
    ppermute x1, waiting for transfers between devices, with_partner(): lax.ppermute(block, 'img', [(i, i ^ 1) for i in range(lax.axis_size('img'...  2.73 us
  transfers between devices with their start and end apart: 9, of which 3 were waited for; matrix products, arithmetic and copies ran while one was open for 0% of the time, Pallas kernels for 38%

profile of v7, /device:TPU:32, one launch (start us, length us, event | category | flops | bytes accessed | tf_op | source)
XLA Modules:
  0.0 71.4 jit_solution(5180701176931144527)
XLA Ops:
  0.6 0.0 copy-start.1
  0.7 0.0 copy-start.3
  0.7 0.0 copy-start.4
  0.7 0.0 copy-start.6
  0.7 0.0 copy-start.8
  0.7 0.5 opening.1.token_ref
  1.3 0.7 %copy-done.1 = bf16[1,4,1,21,21,384]{5,1,4,3,2,0:T(4,128)(2,1)S(1)} copy-done((bf16[1,4,1,21,21,384]{5,1,4,3,2,0:T(4,128)(2,1)S(1)}, bf16[1,4,1,21,21,384]{5,1,4,3,2,0:T(4,128)(2,1)}, u32[]{:S(2)}) %copy-start.1) | copy-done | bytes 1354776
  2.0 0.2 copy-done.3
  2.1 0.1 copy-done.4
  2.2 0.0 copy-done.6
  2.2 0.0 copy-done.8
  2.2 0.0 copy-start.7
  2.2 4.1 %first_five.1 = (bf16[448,384]{1,0:T(8,128)(2,1)S(1)}, bf16[4,448,384]{2,1,0:T(8,128)(2,1)S(1)}, bf16[448,384]{1,0:T(8,128)(2,1)S(1)}, f32[3,616,128]{2,1,0:T(8,128)S(1)}) custom-call(s32[1]{0:T(128)} %opening.1.token_ref, s32[1,4]{1,0:T(1,128)S(1)} %copy-done.8, bf16[441,4,384]{2,1,0:T(4,128)(2,1)S(1)} %bitcast.29, bf16[441,2,384]{2,1,0:T(2,128)(2,1)S(1)} %bitcast.31, ...), custom_call_target="tpu_custom_call" | custom-call | flops 4000000000 | tf_op jit(solution)/shard_map/first_five/pallas_call | solution.py:570
  6.3 3.6 %collective-permute-start = (bf16[448,384]{1,0:T(8,128)(2,1)S(1)}, bf16[448,384]{1,0:T(8,128)(2,1)S(1)}, u32[]{:S(2)}, u32[]{:S(2)}) collective-permute-start(bf16[448,384]{1,0:T(8,128)(2,1)S(1)} %get-tuple-element.85), channel_id=1, source_target_pairs={{8,0},{16,8},{24,16},{32,24},{40,32},{48,40},{56,48},{64,56},{72,6... | collective-permute-start | bytes 1032200 | tf_op jit(solution)/shard_map/ppermute | solution.py:24
  10.0 0.0 copy-done.2
  10.0 0.0 copy-done.5
  10.0 2.1 %first_three.1 = (bf16[448,384]{1,0:T(8,128)(2,1)S(1)}, bf16[4,448,384]{2,1,0:T(8,128)(2,1)S(1)}, f32[3,616,128]{2,1,0:T(8,128)S(1)}) custom-call(s32[1,4]{1,0:T(1,128)S(1)} %copy-done.8, bf16[441,4,384]{2,1,0:T(4,128)(2,1)S(1)} %bitcast.30, bf16[448,384]{1,0:T(8,128)(2,1)S(1)} %get-tuple-element.87.grad_out.refs_8_, bf16[384,384]{1,0:T(8,128)(2,1)S(1)} %bitcast.36, ...), custom_call_target="tpu_custom_call" | custom-call | flops 3000000000 | tf_op jit(solution)/shard_map/first_three/pallas_call | solution.py:570
  12.1 2.6 %collective-permute-start.1 = (bf16[448,384]{1,0:T(8,128)(2,1)S(1)}, bf16[448,384]{1,0:T(8,128)(2,1)S(1)}, u32[]{:S(2)}, u32[]{:S(2)}) collective-permute-start(bf16[448,384]{1,0:T(8,128)(2,1)S(1)} %get-tuple-element.97), channel_id=1, source_target_pairs={{8,0},{16,8},{24,16},{32,24},{40,32},{48,40},{56,48},{64,56},{72,6... | collective-permute-start | bytes 1032200 | tf_op jit(solution)/shard_map/ppermute | solution.py:24
  14.7 0.0 copy-start
  14.7 4.3 %grads_0.1 = (f32[32,384]{1,0:T(8,128)S(1)}, f32[16,384]{1,0:T(8,128)S(1)}, bf16[448,384]{1,0:T(8,128)(2,1)S(1)}, bf16[448,384]{1,0:T(8,128)(2,1)S(1)}) custom-call(bf16[4,448,384]{2,1,0:T(8,128)(2,1)S(1)} %get-tuple-element.86.refs_0_.act_last, bf16[4,448,384]{2,1,0:T(8,128)(2,1)S(1)} %get-tuple-element.88.refs_1_.act_older, bf16[25,384]{1,0:T(8,128)(2,1)S(1)} %bitcast.41, ...), custom_call_target="tpu_custom_call" | custom-call | flops 5000000000 | tf_op jit(solution)/shard_map/grads_0/pallas_call | solution.py:570
  19.0 0.0 collective-permute-done.out_in
  19.0 0.0 copy-done
  19.0 1.8 %five_1.1 = (f32[3,456,128]{2,1,0:T(8,128)S(1)}, bf16[448,384]{1,0:T(8,128)(2,1)S(1)}, bf16[448,384]{1,0:T(8,128)(2,1)S(1)}, f32[3,616,128]{2,1,0:T(8,128)S(1)}) custom-call(s32[1]{0:T(128)} %bitcast.top_ref, bf16[448,384]{1,0:T(8,128)(2,1)S(1)} %collective-permute-done.out_in, bf16[3,441,2,384]{3,2,1,0:T(2,128)(2,1)S(1)} %bitcast.26, ...), custom_call_target="tpu_custom_call" | custom-call | flops 3000000000 | tf_op jit(solution)/shard_map/five_1/pallas_call | solution.py:570
  20.8 0.0 collective-permute-done.1.pass_in
  20.8 0.3 finish_1.1
  21.1 4.5 %collective-permute-start.3 = (bf16[448,384]{1,0:T(8,128)(2,1)S(1)}, bf16[448,384]{1,0:T(8,128)(2,1)S(1)}, u32[]{:S(2)}, u32[]{:S(2)}) collective-permute-start(bf16[448,384]{1,0:T(8,128)(2,1)S(1)} %finish_1.1), channel_id=1, source_target_pairs={{8,0},{16,8},{24,16},{32,24},{40,32},{48,40},{56,48},{64,56},{72,6... | collective-permute-start | bytes 1032200 | tf_op jit(solution)/shard_map/ppermute | solution.py:24
  25.6 1.1 %three_1.1 = (bf16[448,384]{1,0:T(8,128)(2,1)S(1)}, f32[3,616,128]{2,1,0:T(8,128)S(1)}) custom-call(bf16[448,384]{1,0:T(8,128)(2,1)S(1)} %get-tuple-element.100.grad_out.refs_9_, bf16[4,448,384]{2,1,0:T(8,128)(2,1)S(1)} %get-tuple-element.88.refs_1_.act_older, bf16[384,384]{1,0:T(8,128)(2,1)S(1)} %bitcast.37, bf16[9,384]{1,0:T(8,128)(2,1)S(1)} %bitcast.49), custom_call_target="tpu_custom_call" | custom-call | flops 2000000000 | tf_op jit(solution)/shard_map/three_1/pallas_call | solution.py:570
  26.7 1.9 %collective-permute-start.2 = (bf16[448,384]{1,0:T(8,128)(2,1)S(1)}, bf16[448,384]{1,0:T(8,128)(2,1)S(1)}, u32[]{:S(2)}, u32[]{:S(2)}) collective-permute-start(bf16[448,384]{1,0:T(8,128)(2,1)S(1)} %get-tuple-element.101), channel_id=1, source_target_pairs={{8,0},{16,8},{24,16},{32,24},{40,32},{48,40},{56,48},{64,56},{72,6... | collective-permute-start | bytes 1032200 | tf_op jit(solution)/shard_map/ppermute | solution.py:24
  28.6 4.3 %grads_1.1 = (f32[32,384]{1,0:T(8,128)S(1)}, f32[16,384]{1,0:T(8,128)S(1)}, bf16[448,384]{1,0:T(8,128)(2,1)S(1)}, bf16[448,384]{1,0:T(8,128)(2,1)S(1)}) custom-call(bf16[4,448,384]{2,1,0:T(8,128)(2,1)S(1)} %get-tuple-element.86.refs_0_.act_last, bf16[4,448,384]{2,1,0:T(8,128)(2,1)S(1)} %get-tuple-element.88.refs_1_.act_older, bf16[25,384]{1,0:T(8,128)(2,1)S(1)} %bitcast.43, ...), custom_call_target="tpu_custom_call" | custom-call | flops 5000000000 | tf_op jit(solution)/shard_map/grads_1/pallas_call | solution.py:570
  32.9 0.0 collective-permute-done.3.out_in
  32.9 1.8 %five_2.1 = (f32[3,456,128]{2,1,0:T(8,128)S(1)}, bf16[448,384]{1,0:T(8,128)(2,1)S(1)}, bf16[448,384]{1,0:T(8,128)(2,1)S(1)}, f32[3,616,128]{2,1,0:T(8,128)S(1)}) custom-call(s32[1]{0:T(128)} %bitcast.top_ref, bf16[448,384]{1,0:T(8,128)(2,1)S(1)} %collective-permute-done.3.out_in, bf16[3,441,2,384]{3,2,1,0:T(2,128)(2,1)S(1)} %bitcast.27, ...), custom_call_target="tpu_custom_call" | custom-call | flops 3000000000 | tf_op jit(solution)/shard_map/five_2/pallas_call | solution.py:570
  34.8 0.0 collective-permute-done.2.pass_in
  34.8 1.3 %both_2.1 = (bf16[2,448,384]{2,1,0:T(8,128)(2,1)S(1)}, f32[3,616,128]{2,1,0:T(8,128)S(1)}) custom-call(s32[1]{0:T(128)} %bitcast.top_ref, bf16[448,384]{1,0:T(8,128)(2,1)S(1)} %collective-permute-done.2.pass_in, bf16[448,384]{1,0:T(8,128)(2,1)S(1)} %get-tuple-element.111.head_pass, bf16[448,384]{1,0:T(8,128)(2,1)S(1)} %get-tuple-element.112.grad_out.refs_10_, ...), custom_call_target="tpu_custom_call" | custom-call | flops 2000000000 | tf_op jit(solution)/shard_map/both_2/pallas_call | solution.py:570
  36.1 5.2 %collective-permute-start.4 = (bf16[2,448,384]{2,1,0:T(8,128)(2,1)S(1)}, bf16[2,448,384]{2,1,0:T(8,128)(2,1)S(1)}, u32[]{:S(2)}, u32[]{:S(2)}) collective-permute-start(bf16[2,448,384]{2,1,0:T(8,128)(2,1)S(1)} %get-tuple-element.114), channel_id=1, source_target_pairs={{8,0},{16,8},{24,16},{32,24},{40,32},{48,40},{56,48},{64,56},{72,6... | collective-permute-start | bytes 2064392 | tf_op jit(solution)/shard_map/ppermute | solution.py:24
  41.3 8.3 %gather_2.1 = (f32[384,384]{1,0:T(8,128)S(1)}, f32[384,384]{1,0:T(8,128)S(1)}, f32[32,384]{1,0:T(8,128)S(1)}, f32[16,384]{1,0:T(8,128)S(1)}, bf16[448,384]{1,0:T...) custom-call(bf16[4,448,384]{2,1,0:T(8,128)(2,1)S(1)} %get-tuple-element.86.re, ...), custom_call_target="tpu_custom_call" | custom-call | flops 10000000000 | tf_op jit(solution)/shard_map/gather_2/pallas_call | solution.py:570
  49.6 0.1 collective-permute-done.4.pair_in
  49.7 3.8 %last_grads.1 = (bf16[96,896]{1,0:T(8,128)(2,1)S(1)}, bf16[96,896]{1,0:T(8,128)(2,1)S(1)}, bf16[96,896]{1,0:T(8,128)(2,1)S(1)}, f32[96,896]{1,0:T(8,128)S(1)}, b...) custom-call(s32[1]{0:T(128)} %bitcast.top_ref, ...), custom_call_target="tpu_custom_call" | custom-call | flops 6000000000 | tf_op jit(solution)/shard_map/last_grads/pallas_call | solution.py:570
  53.5 3.3 %collective-permute-start.5 = (bf16[96,896]{1,0:T(8,128)(2,1)S(1)}, bf16[96,896]{1,0:T(8,128)(2,1)S(1)}, u32[]{:S(2)}, u32[]{:S(2)}) collective-permute-start(bf16[96,896]{1,0:T(8,128)(2,1)S(1)} %get-tuple-element.140), channel_id=1, source_target_pairs={{0,4},{1,5},{2,6},{3,7},{4,0},{5,1},{6,2},{7,3},{8,12},{9,13},{10,... | collective-permute-start | bytes 516104 | tf_op jit(solution)/shard_map/ppermute | solution.py:30
  56.8 0.7 collective-permute-start.6
  57.5 2.6 %collective-permute-start.7 = (bf16[96,896]{1,0:T(8,128)(2,1)S(1)}, bf16[96,896]{1,0:T(8,128)(2,1)S(1)}, u32[]{:S(2)}, u32[]{:S(2)}) collective-permute-start(bf16[96,896]{1,0:T(8,128)(2,1)S(1)} %get-tuple-element.142), channel_id=1, source_target_pairs={{0,6},{1,7},{2,0},{3,1},{4,2},{5,3},{6,4},{7,5},{8,14},{9,15},{10,... | collective-permute-start | bytes 516104 | tf_op jit(solution)/shard_map/ppermute | solution.py:30
  60.0 3.6 %last.1 = bf16[441,2,384]{2,1,0:T(2,128)(2,1)} custom-call(bf16[448,384]{1,0:T(8,128)(2,1)S(1)} %get-tuple-element.143.grad_out, bf16[448,384]{1,0:T(8,128)(2,1)S(1)} %get-tuple-element.144.grad_pass, f32[3,616,128]{2,1,0:T(8,128)S(1)} %get-tuple-element.145.back_five, f32[3,616,128]{2,1,0:T(8,128)S(1)} %get-tuple-element.146.back_three, ...), custom_call_target="tpu_custom_call" | custom-call | flops 4000000000 | tf_op jit(solution)/shard_map/last/pallas_call | solution.py:570
  63.7 0.0 collective-permute-done.5.one
  63.7 0.9 %collective-permute-done.6.two = bf16[96,896]{1,0:T(8,128)(2,1)S(1)} collective-permute-done((bf16[96,896]{1,0:T(8,128)(2,1)S(1)}, bf16[96,896]{1,0:T(8,128)(2,1)S(1)}, u32[]{:S(2)}, u32[]{:S(2)}) %collective-permute-start.6) | collective-permute-done | bytes 172064 | tf_op jit(solution)/shard_map/ppermute | solution.py:30
  64.6 0.0 collective-permute-done.7.three
  64.6 0.1 half_total.1
  64.7 3.3 %collective-permute-start.8 = (bf16[48,896]{1,0:T(8,128)(2,1)S(1)}, bf16[48,896]{1,0:T(8,128)(2,1)S(1)}, u32[]{:S(2)}, u32[]{:S(2)}) collective-permute-start(bf16[48,896]{1,0:T(8,128)(2,1)S(1)} %get-tuple-element.154), channel_id=1, source_target_pairs={{0,1},{1,0},{2,3},{3,2},{4,5},{5,4},{6,7},{7,6},{8,9},{9,8},{10,11... | collective-permute-start | bytes 258056 | tf_op jit(solution)/shard_map/ppermute | solution.py:34
  68.0 2.7 %collective-permute-done.8.landed = bf16[48,896]{1,0:T(8,128)(2,1)S(1)} collective-permute-done((bf16[48,896]{1,0:T(8,128)(2,1)S(1)}, bf16[48,896]{1,0:T(8,128)(2,1)S(1)}, u32[]{:S(2)}, u32[]{:S(2)}) %collective-permute-start.8) | collective-permute-done | bytes 86048 | tf_op jit(solution)/shard_map/ppermute | solution.py:34
  70.7 0.7 total.1
  (3 shorter events, 0.0 us)
Async XLA Ops:
  0.6 1.3 %copy-start.1 = (bf16[1,4,1,21,21,384]{5,1,4,3,2,0:T(4,128)(2,1)S(1)}, bf16[1,4,1,21,21,384]{5,1,4,3,2,0:T(4,128)(2,1)}, u32[]{:S(2)}) copy-start(bf16[1,4,1,21,21,384]{5,1,4,3,2,0:T(4,128)(2,1)} %param.9) | copy-start | bytes 4064260
  0.7 1.5 %copy-start.3 = (bf16[1,2,1,21,21,384]{5,1,4,3,2,0:T(2,128)(2,1)S(1)}, bf16[1,2,1,21,21,384]{5,1,4,3,2,0:T(2,128)(2,1)}, u32[]{:S(2)}) copy-start(bf16[1,2,1,21,21,384]{5,1,4,3,2,0:T(2,128)(2,1)} %param.11) | copy-start | bytes 2032132
  0.7 1.6 %copy-start.4 = (bf16[1,384,384]{2,1,0:T(8,128)(2,1)S(1)}, bf16[1,384,384]{2,1,0:T(8,128)(2,1)}, u32[]{:S(2)}) copy-start(bf16[1,384,384]{2,1,0:T(8,128)(2,1)} %param.16) | copy-start | bytes 884740
  0.7 1.5 %copy-start.6 = (bf16[1,25,384]{2,1,0:T(8,128)(2,1)S(1)}, bf16[1,25,384]{2,1,0:T(8,128)(2,1)}, u32[]{:S(2)}) copy-start(bf16[1,25,384]{2,1,0:T(8,128)(2,1)} %param.14) | copy-start | bytes 57604
  0.7 1.5 %copy-start.8 = (s32[1,4]{1,0:T(1,128)S(1)}, s32[1,4]{1,0:T(1,128)}, u32[]{:S(2)}) copy-start(s32[1,4]{1,0:T(1,128)} %plan_ref.3) | copy-start | bytes 52
  2.2 7.8 %copy-start.2 = (bf16[1,4,1,21,21,384]{5,1,4,3,2,0:T(4,128)(2,1)S(1)}, bf16[1,4,1,21,21,384]{5,1,4,3,2,0:T(4,128)(2,1)}, u32[]{:S(2)}) copy-start(bf16[1,4,1,21,21,384]{5,1,4,3,2,0:T(4,128)(2,1)} %param.10) | copy-start | bytes 4064260
  2.2 7.8 %copy-start.5 = (bf16[1,384,384]{2,1,0:T(8,128)(2,1)S(1)}, bf16[1,384,384]{2,1,0:T(8,128)(2,1)}, u32[]{:S(2)}) copy-start(bf16[1,384,384]{2,1,0:T(8,128)(2,1)} %param.17) | copy-start | bytes 884740
  2.2 7.8 %copy-start.7 = (bf16[1,9,384]{2,1,0:T(8,128)(2,1)S(1)}, bf16[1,9,384]{2,1,0:T(8,128)(2,1)}, u32[]{:S(2)}) copy-start(bf16[1,9,384]{2,1,0:T(8,128)(2,1)} %param.15) | copy-start | bytes 20740
  6.3 12.6 %collective-permute-start = (bf16[448,384]{1,0:T(8,128)(2,1)S(1)}, bf16[448,384]{1,0:T(8,128)(2,1)S(1)}, u32[]{:S(2)}, u32[]{:S(2)}) collective-permute-start(bf16[448,384]{1,0:T(8,128)(2,1)S(1)} %get-tuple-element.85), channel_id=1, source_target_pairs={{8,0},{16,8},{24,16},{32,24},{40,32},{48,40},{56,48},{64,56},{72,6... | collective-permute-start | bytes 1032200 | tf_op jit(solution)/shard_map/ppermute | solution.py:24
  12.1 8.7 %collective-permute-start.1 = (bf16[448,384]{1,0:T(8,128)(2,1)S(1)}, bf16[448,384]{1,0:T(8,128)(2,1)S(1)}, u32[]{:S(2)}, u32[]{:S(2)}) collective-permute-start(bf16[448,384]{1,0:T(8,128)(2,1)S(1)} %get-tuple-element.97), channel_id=1, source_target_pairs={{8,0},{16,8},{24,16},{32,24},{40,32},{48,40},{56,48},{64,56},{72,6... | collective-permute-start | bytes 1032200 | tf_op jit(solution)/shard_map/ppermute | solution.py:24
  14.7 4.3 %copy-start = (bf16[3,2,1,21,21,384]{5,1,4,3,2,0:T(2,128)(2,1)S(1)}, bf16[3,2,1,21,21,384]{5,1,4,3,2,0:T(2,128)(2,1)}, u32[]{:S(2)}) copy-start(bf16[3,2,1,21,21,384]{5,1,4,3,2,0:T(2,128)(2,1)} %param.12) | copy-start | bytes 6096388
  21.1 11.8 %collective-permute-start.3 = (bf16[448,384]{1,0:T(8,128)(2,1)S(1)}, bf16[448,384]{1,0:T(8,128)(2,1)S(1)}, u32[]{:S(2)}, u32[]{:S(2)}) collective-permute-start(bf16[448,384]{1,0:T(8,128)(2,1)S(1)} %finish_1.1), channel_id=1, source_target_pairs={{8,0},{16,8},{24,16},{32,24},{40,32},{48,40},{56,48},{64,56},{72,6... | collective-permute-start | bytes 1032200 | tf_op jit(solution)/shard_map/ppermute | solution.py:24
  26.7 8.1 %collective-permute-start.2 = (bf16[448,384]{1,0:T(8,128)(2,1)S(1)}, bf16[448,384]{1,0:T(8,128)(2,1)S(1)}, u32[]{:S(2)}, u32[]{:S(2)}) collective-permute-start(bf16[448,384]{1,0:T(8,128)(2,1)S(1)} %get-tuple-element.101), channel_id=1, source_target_pairs={{8,0},{16,8},{24,16},{32,24},{40,32},{48,40},{56,48},{64,56},{72,6... | collective-permute-start | bytes 1032200 | tf_op jit(solution)/shard_map/ppermute | solution.py:24
  36.1 13.6 %collective-permute-start.4 = (bf16[2,448,384]{2,1,0:T(8,128)(2,1)S(1)}, bf16[2,448,384]{2,1,0:T(8,128)(2,1)S(1)}, u32[]{:S(2)}, u32[]{:S(2)}) collective-permute-start(bf16[2,448,384]{2,1,0:T(8,128)(2,1)S(1)} %get-tuple-element.114), channel_id=1, source_target_pairs={{8,0},{16,8},{24,16},{32,24},{40,32},{48,40},{56,48},{64,56},{72,6... | collective-permute-start | bytes 2064392 | tf_op jit(solution)/shard_map/ppermute | solution.py:24
  53.5 10.1 %collective-permute-start.5 = (bf16[96,896]{1,0:T(8,128)(2,1)S(1)}, bf16[96,896]{1,0:T(8,128)(2,1)S(1)}, u32[]{:S(2)}, u32[]{:S(2)}) collective-permute-start(bf16[96,896]{1,0:T(8,128)(2,1)S(1)} %get-tuple-element.140), channel_id=1, source_target_pairs={{0,4},{1,5},{2,6},{3,7},{4,0},{5,1},{6,2},{7,3},{8,12},{9,13},{10,... | collective-permute-start | bytes 516104 | tf_op jit(solution)/shard_map/ppermute | solution.py:30
  56.8 7.8 %collective-permute-start.6 = (bf16[96,896]{1,0:T(8,128)(2,1)S(1)}, bf16[96,896]{1,0:T(8,128)(2,1)S(1)}, u32[]{:S(2)}, u32[]{:S(2)}) collective-permute-start(bf16[96,896]{1,0:T(8,128)(2,1)S(1)} %get-tuple-element.141), channel_id=1, source_target_pairs={{0,2},{1,3},{2,4},{3,5},{4,6},{5,7},{6,0},{7,1},{8,10},{9,11},{10,... | collective-permute-start | bytes 516104 | tf_op jit(solution)/shard_map/ppermute | solution.py:30
  57.5 7.1 %collective-permute-start.7 = (bf16[96,896]{1,0:T(8,128)(2,1)S(1)}, bf16[96,896]{1,0:T(8,128)(2,1)S(1)}, u32[]{:S(2)}, u32[]{:S(2)}) collective-permute-start(bf16[96,896]{1,0:T(8,128)(2,1)S(1)} %get-tuple-element.142), channel_id=1, source_target_pairs={{0,6},{1,7},{2,0},{3,1},{4,2},{5,3},{6,4},{7,5},{8,14},{9,15},{10,... | collective-permute-start | bytes 516104 | tf_op jit(solution)/shard_map/ppermute | solution.py:30
  64.7 6.1 %collective-permute-start.8 = (bf16[48,896]{1,0:T(8,128)(2,1)S(1)}, bf16[48,896]{1,0:T(8,128)(2,1)S(1)}, u32[]{:S(2)}, u32[]{:S(2)}) collective-permute-start(bf16[48,896]{1,0:T(8,128)(2,1)S(1)} %get-tuple-element.154), channel_id=1, source_target_pairs={{0,1},{1,0},{2,3},{3,2},{4,5},{5,4},{6,7},{7,6},{8,9},{9,8},{10,11... | collective-permute-start | bytes 258056 | tf_op jit(solution)/shard_map/ppermute | solution.py:34

commit v8 on v7

--- a/solution.py
+++ b/solution.py
@@ -324,26 +324,6 @@
     three_part(t, grad_out, act_older, weight, taps, back, grad_older, wide, dense, lambda: None)
 
 
-def both_kernel(
-    t,
-    top_ref,
-    pass_in,
-    head_pass,
-    grad_out,
-    act_last,
-    act_older,
-    through,
-    weight,
-    taps,
-    made,
-    back,
-    wide,
-    dense,
-):
-    three_part(t, grad_out, act_older, weight, taps, back, made.at[1], wide, dense, lambda: None)
-    finish(t, top_ref, pass_in, head_pass, grad_out, act_last, through, made.at[0])
-
-
 def copies(pairs, sems):
     return [pltpu.make_async_copy(a, b, sems.at[n]) for n, (a, b) in enumerate(pairs)]
 
@@ -420,7 +400,7 @@
     t,
     top_ref,
     row_ref,
-    pair_in,
+    out_in,
     head_hbm,
     weight_five,
     weight_three,
@@ -435,15 +415,10 @@
     *refs,
 ):
     sends, refs = refs[:3], refs[3:]
-    own, grad_out, grad_pass, back_five, back_three = refs[:5]
+    own, grad_out, head_pass, back_five, back_three = refs[:5]
     packed, head_in, dense, rows_ref, sem = refs[5:]
     scale = 1.0 / PIXELS
-    take(t, top_ref, pair_in.at[0], head_hbm, grad_out, grad_pass, head_in, sem)
-
-    @pl.when(top_ref[0] != 1)
-    def _():
-        grad_pass[...] = pair_in[1]
-
+    take(t, top_ref, out_in, head_hbm, grad_out, head_pass, head_in, sem)
     left = grad_out[...]
     packed[:, 0:CH] = (across(mixed_five[...], left) + old_five[...]) * scale
     packed[:, CH : 2 * CH] = (across(mixed_three[...], left) + old_three[...]) * scale
@@ -471,33 +446,30 @@
         send[...] = packed[rows(distance), :].astype(BF16)
 
 
-def last_kernel(
-    t,
-    grad_out,
-    grad_pass,
-    back_five,
-    back_three,
-    act_last,
-    act_older,
-    taps_five,
-    taps_three,
-    outgoing_hbm,
-    wide_five,
-    wide_three,
-    dense,
-    made_older,
-    outgoing,
-    sems,
+def last_convs_kernel(
+    t, back_five, back_three, act_older, taps_five, taps_three, through, grad_older, wide_five, wide_three, dense
 ):
     spread_taps(taps_five, wide_five, 25)
     spread_taps(taps_three, wide_three, 9)
     spread_conv(back_three, wide_three, dense, 3, True)
-    finish_older(act_older, t, dense, made_older)
-    spread_conv(back_five, wide_five, dense, 5, True)
+    finish_older(act_older, t, dense, grad_older)
+    spread_conv(back_five, wide_five, through, 5, True)
+
+
+def last_kernel(
+    t, top_ref, pass_in, head_pass, grad_out, act_last, through, grad_older, outgoing_hbm, outgoing, grad_pass, sems
+):
+    @pl.when(top_ref[0] == 1)
+    def _():
+        grad_pass[...] = head_pass[...]
+
+    @pl.when(top_ref[0] != 1)
+    def _():
+        grad_pass[...] = pass_in[...]
 
     def both(rows, c):
-        last = last_piece(act_last, t, dense, grad_out, grad_pass, c, rows)
-        return jnp.swapaxes(jnp.stack([last, made_older[rows, lanes(c)]], 0), 0, 1)
+        last = last_piece(act_last, t, through, grad_out, grad_pass, c, rows)
+        return jnp.swapaxes(jnp.stack([last, grad_older[rows, lanes(c)]], 0), 0, 1)
 
     def body(i, carry):
         rows = pl.ds(pl.multiple_of(i * 16, 16), 16)
@@ -506,7 +478,7 @@
         return carry
 
     half = 224
-    lax.fori_loop(0, half // 16, body, 0)
+    lax.fori_loop(0, half // 16, body, 0, unroll=7)
     put = copies(
         [
             (outgoing.at[pl.ds(0, half)], outgoing_hbm.at[pl.ds(0, half)]),
@@ -515,7 +487,7 @@
         sems,
     )
     put[0].start()
-    lax.fori_loop(half // 16, PIXELS // 16, body, 0)
+    lax.fori_loop(half // 16, PIXELS // 16, body, 0, unroll=13)
     at = PIXELS // 16 * 16
     for c in range(BLOCKS):
         outgoing[at:PIXELS, :, lanes(c)] = both(slice(at, at + 16), c)[: PIXELS - at]
@@ -653,19 +625,6 @@
         (grad_out, act, weight, taps),
         [VMEM] * 4,
         (FLAT, BACK),
-        (VMEM,) * 2,
-        [WIDE_THREE, DENSE],
-        2,
-    )
-
-
-def call_both(t, *operands):
-    return run(
-        functools.partial(both_kernel, t),
-        f"both_{t}",
-        operands,
-        [SMEM] + [VMEM] * 8,
-        (jax.ShapeDtypeStruct((2, ROWS, CH), BF16), BACK),
         (VMEM,) * 2,
         [WIDE_THREE, DENSE],
         2,
@@ -721,16 +680,29 @@
     )
 
 
-def call_last(t, grads, backs, acts, taps):
+def call_last_convs(t, *operands):
+    return run(
+        functools.partial(last_convs_kernel, t),
+        "last_convs",
+        operands,
+        [VMEM] * 5,
+        (THROUGH, FLAT),
+        (VMEM,) * 2,
+        [WIDE_FIVE, WIDE_THREE, DENSE],
+        3,
+    )
+
+
+def call_last(t, *operands):
     (outgoing,) = run(
         functools.partial(last_kernel, t),
         "last",
-        (*grads, *backs, *acts, *taps),
-        [VMEM] * 8,
+        operands,
+        [SMEM] + [VMEM] * 6,
         (jax.ShapeDtypeStruct((PIXELS, 2, CH), BF16),),
         (ANY,),
-        [WIDE_FIVE, WIDE_THREE, DENSE, FLAT_SCRATCH, PAIR_SCRATCH, pltpu.SemaphoreType.DMA((2,))],
-        4,
+        [PAIR_SCRATCH, FLAT_SCRATCH, pltpu.SemaphoreType.DMA((2,))],
+        2,
     )
     return outgoing
 
@@ -809,32 +781,37 @@
             t + 1, (top, next_out, head), weights[0], taps[0]
         )
         grads = (*grads, grad_out)
-        skip = (top, next_pass, head_pass, grad_out)
+        grad_last = call_finish(t + 1, top, next_pass, head_pass, grad_out, act_last, through)
+        next_out = from_next(grad_last)
+        ready, _ = lax.optimization_barrier((grad_out, grad_last))
+        grad_older, back_three = call_three(t + 1, ready, act_older, weights[1], taps[1])
         if t < turns - 3:
-            grad_last = call_finish(t + 1, *skip, act_last, through)
-            next_out = from_next(grad_last)
-            ready, _ = lax.optimization_barrier((grad_out, grad_last))
-            grad_older, back_three = call_three(t + 1, ready, act_older, weights[1], taps[1])
             next_pass = from_next(grad_older)
-    both, back_three = call_both(turns - 2, *skip, *acts, through, weights[1], taps[1])
-    next_pair = from_next(both)
     made = call_gather(turns - 2, acts, taps, (back_five, back_three), sums, grads, mixes)
-    next_pair, made = lax.optimization_barrier((next_pair, made))
-    *sends, own, grad_out, grad_pass, back_five, back_three = call_last_grads(
+    next_out, made = lax.optimization_barrier((next_out, made))
+    *sends, own, grad_out, head_pass, back_five, back_three = call_last_grads(
         turns - 1,
         CH * 2 // lax.axis_size("img"),
-        (top, group, next_pair, head),
+        (top, group, next_out, head),
         weights,
         made[4:],
         made[:4],
     )
+    *sends, grad_older = lax.optimization_barrier((*sends, grad_older))
     landed = [around_rows(sends[distance - 1], distance) for distance in (2, 1, 3)]
+    next_pass = from_next(grad_older)
+    through, made_older = call_last_convs(
+        turns - 1, back_five, back_three, act_older, taps[0], taps[1]
+    )
+    *landed, through = lax.optimization_barrier((*landed, through))
+    kept, send = call_half_total(half, own, landed)
+    through, kept, send = lax.optimization_barrier((through, kept, send))
+    partner = with_partner(send)
     outgoing = call_last(
-        turns - 1, (grad_out, grad_pass), (back_five, back_three), acts, taps
-    )
-    *landed, outgoing = lax.optimization_barrier((*landed, outgoing))
-    kept, send = call_half_total(half, own, landed)
-    five, three, tap_five, tap_three = call_total(kept, with_partner(send))
+        turns - 1, top, next_pass, head_pass, grad_out, act_last, through, made_older
+    )
+    partner, outgoing = lax.optimization_barrier((partner, outgoing))
+    five, three, tap_five, tap_three = call_total(kept, partner)
     outgoing = outgoing.reshape(1, 1, SIDE, SIDE, 2, CH).transpose(0, 4, 1, 2, 3, 5)
     return (
         outgoing,

time: 72 us -> 71.7 us (level)
  starting transfers between devices: 27.7 us -> 29.6 us
  waiting for transfers between devices: 3.78 us -> 1.89 us
    ppermute x5 -> x6, starting transfers between devices: 17.8 us -> 19.7 us  [from_next(): return lax.ppermute(block, 'sec', [(i + 1, i) for i in range(size - 1)])]
    ppermute x3, waiting for transfers between devices: 0.9 us -> 0.01 us  [around_rows(): return lax.ppermute(block, 'img', route)]
    ppermute x1, waiting for transfers between devices: 2.73 us -> 1.87 us  [with_partner(): lax.ppermute(block, 'img', [(i, i ^ 1) for i in range(lax.axis_size('img'...]
    pallas_call x14 -> x16, Pallas kernels: 37.3 us -> 37 us  [run(): pl.pallas_call(kernel, out_shape=tuple(shapes), in_specs=specs, out_specs...]
  transfers between devices with their start and end apart: 9 -> 10, of which waited for: 3 -> 1; matrix products, arithmetic and copies ran while one was open for 0% -> 0% of each run, Pallas kernels for 38% -> 40%
where the time goes in v8:
time: 71.7 us; the launch traced here: 71.2 us
  Pallas kernels  37.7 us (53%)
  starting transfers between devices  29.6 us (41%)
  waiting for transfers between devices  1.89 us (3%)
  local copies, waits for them, and re-layouts  1 us (1%)
  between operations  0.96 us (1%)
    pallas_call x16, Pallas kernels, run(): pl.pallas_call(kernel, out_shape=tuple(shapes), in_specs=specs, out_specs...  37 us
    ppermute x6, starting transfers between devices, from_next(): return lax.ppermute(block, 'sec', [(i + 1, i) for i in range(size - 1)])  19.7 us
    ppermute x3, starting transfers between devices, around_rows(): return lax.ppermute(block, 'img', route)  6.51 us
    ppermute x1, starting transfers between devices, with_partner(): lax.ppermute(block, 'img', [(i, i ^ 1) for i in range(lax.axis_size('img'...  3.35 us
    ppermute x1, waiting for transfers between devices, with_partner(): lax.ppermute(block, 'img', [(i, i ^ 1) for i in range(lax.axis_size('img'...  1.87 us
  transfers between devices with their start and end apart: 10, of which 1 were waited for; matrix products, arithmetic and copies ran while one was open for 0% of the time, Pallas kernels for 40%

profile of v8, /device:TPU:32, one launch (start us, length us, event | category | flops | bytes accessed | tf_op | source)
XLA Modules:
  0.0 71.2 jit_solution(9929659569118715891)
XLA Ops:
  0.6 0.0 copy-start.1
  0.7 0.0 copy-start.3
  0.7 0.0 copy-start.4
  0.7 0.0 copy-start.6
  0.7 0.0 copy-start.8
  0.7 0.5 opening.1.token_ref
  1.3 0.7 %copy-done.1 = bf16[1,4,1,21,21,384]{5,1,4,3,2,0:T(4,128)(2,1)S(1)} copy-done((bf16[1,4,1,21,21,384]{5,1,4,3,2,0:T(4,128)(2,1)S(1)}, bf16[1,4,1,21,21,384]{5,1,4,3,2,0:T(4,128)(2,1)}, u32[]{:S(2)}) %copy-start.1) | copy-done | bytes 1354776
  2.0 0.2 copy-done.3
  2.1 0.1 copy-done.4
  2.2 0.0 copy-done.6
  2.2 0.0 copy-start.7
  2.2 4.1 %first_five.1 = (bf16[448,384]{1,0:T(8,128)(2,1)S(1)}, bf16[4,448,384]{2,1,0:T(8,128)(2,1)S(1)}, bf16[448,384]{1,0:T(8,128)(2,1)S(1)}, f32[3,616,128]{2,1,0:T(8,128)S(1)}) custom-call(s32[1]{0:T(128)} %opening.1.token_ref, s32[1,4]{1,0:T(1,128)S(1)} %copy-done.8, bf16[441,4,384]{2,1,0:T(4,128)(2,1)S(1)} %bitcast.29, bf16[441,2,384]{2,1,0:T(2,128)(2,1)S(1)} %bitcast.31, ...), custom_call_target="tpu_custom_call" | custom-call | flops 4000000000 | tf_op jit(solution)/shard_map/first_five/pallas_call | solution.py:542
  6.3 3.6 %collective-permute-start = (bf16[448,384]{1,0:T(8,128)(2,1)S(1)}, bf16[448,384]{1,0:T(8,128)(2,1)S(1)}, u32[]{:S(2)}, u32[]{:S(2)}) collective-permute-start(bf16[448,384]{1,0:T(8,128)(2,1)S(1)} %get-tuple-element.97), channel_id=1, source_target_pairs={{8,0},{16,8},{24,16},{32,24},{40,32},{48,40},{56,48},{64,56},{72,6... | collective-permute-start | bytes 1032200 | tf_op jit(solution)/shard_map/ppermute | solution.py:24
  10.0 2.1 %first_three.1 = (bf16[448,384]{1,0:T(8,128)(2,1)S(1)}, bf16[4,448,384]{2,1,0:T(8,128)(2,1)S(1)}, f32[3,616,128]{2,1,0:T(8,128)S(1)}) custom-call(s32[1,4]{1,0:T(1,128)S(1)} %copy-done.8, bf16[441,4,384]{2,1,0:T(4,128)(2,1)S(1)} %bitcast.30, bf16[448,384]{1,0:T(8,128)(2,1)S(1)} %get-tuple-element.99.grad_out.refs_8_, bf16[384,384]{1,0:T(8,128)(2,1)S(1)} %bitcast.36, ...), custom_call_target="tpu_custom_call" | custom-call | flops 3000000000 | tf_op jit(solution)/shard_map/first_three/pallas_call | solution.py:542
  12.1 2.6 %collective-permute-start.1 = (bf16[448,384]{1,0:T(8,128)(2,1)S(1)}, bf16[448,384]{1,0:T(8,128)(2,1)S(1)}, u32[]{:S(2)}, u32[]{:S(2)}) collective-permute-start(bf16[448,384]{1,0:T(8,128)(2,1)S(1)} %get-tuple-element.109), channel_id=1, source_target_pairs={{8,0},{16,8},{24,16},{32,24},{40,32},{48,40},{56,48},{64,56},{72,6... | collective-permute-start | bytes 1032200 | tf_op jit(solution)/shard_map/ppermute | solution.py:24
  14.7 0.0 copy-start
  14.7 4.3 %grads_0.1 = (f32[32,384]{1,0:T(8,128)S(1)}, f32[16,384]{1,0:T(8,128)S(1)}, bf16[448,384]{1,0:T(8,128)(2,1)S(1)}, bf16[448,384]{1,0:T(8,128)(2,1)S(1)}) custom-call(bf16[4,448,384]{2,1,0:T(8,128)(2,1)S(1)} %get-tuple-element.98.refs_0_.act_last, bf16[4,448,384]{2,1,0:T(8,128)(2,1)S(1)} %get-tuple-element.100.refs_1_.act_older, bf16[25,384]{1,0:T(8,128)(2,1)S(1)} %bitcast.41, ...), custom_call_target="tpu_custom_call" | custom-call | flops 5000000000 | tf_op jit(solution)/shard_map/grads_0/pallas_call | solution.py:542
  18.9 0.0 collective-permute-done.out_in
  19.0 1.8 %five_1.1 = (f32[3,456,128]{2,1,0:T(8,128)S(1)}, bf16[448,384]{1,0:T(8,128)(2,1)S(1)}, bf16[448,384]{1,0:T(8,128)(2,1)S(1)}, f32[3,616,128]{2,1,0:T(8,128)S(1)}) custom-call(s32[1]{0:T(128)} %bitcast.top_ref, bf16[448,384]{1,0:T(8,128)(2,1)S(1)} %collective-permute-done.out_in, bf16[3,441,2,384]{3,2,1,0:T(2,128)(2,1)S(1)} %bitcast.26, ...), custom_call_target="tpu_custom_call" | custom-call | flops 3000000000 | tf_op jit(solution)/shard_map/five_1/pallas_call | solution.py:542
  20.8 0.0 collective-permute-done.1.pass_in
  20.8 0.3 finish_1.1
  21.1 4.5 %collective-permute-start.3 = (bf16[448,384]{1,0:T(8,128)(2,1)S(1)}, bf16[448,384]{1,0:T(8,128)(2,1)S(1)}, u32[]{:S(2)}, u32[]{:S(2)}) collective-permute-start(bf16[448,384]{1,0:T(8,128)(2,1)S(1)} %finish_1.1), channel_id=1, source_target_pairs={{8,0},{16,8},{24,16},{32,24},{40,32},{48,40},{56,48},{64,56},{72,6... | collective-permute-start | bytes 1032200 | tf_op jit(solution)/shard_map/ppermute | solution.py:24
  25.6 1.1 %three_1.1 = (bf16[448,384]{1,0:T(8,128)(2,1)S(1)}, f32[3,616,128]{2,1,0:T(8,128)S(1)}) custom-call(bf16[448,384]{1,0:T(8,128)(2,1)S(1)} %get-tuple-element.112.grad_out.refs_9_, bf16[4,448,384]{2,1,0:T(8,128)(2,1)S(1)} %get-tuple-element.100.refs_1_.act_older, bf16[384,384]{1,0:T(8,128)(2,1)S(1)} %bitcast.37, bf16[9,384]{1,0:T(8,128)(2,1)S(1)} %bitcast.49), custom_call_target="tpu_custom_call" | custom-call | flops 2000000000 | tf_op jit(solution)/shard_map/three_1/pallas_call | solution.py:542
  26.7 1.9 %collective-permute-start.2 = (bf16[448,384]{1,0:T(8,128)(2,1)S(1)}, bf16[448,384]{1,0:T(8,128)(2,1)S(1)}, u32[]{:S(2)}, u32[]{:S(2)}) collective-permute-start(bf16[448,384]{1,0:T(8,128)(2,1)S(1)} %get-tuple-element.113), channel_id=1, source_target_pairs={{8,0},{16,8},{24,16},{32,24},{40,32},{48,40},{56,48},{64,56},{72,6... | collective-permute-start | bytes 1032200 | tf_op jit(solution)/shard_map/ppermute | solution.py:24
  28.6 4.3 %grads_1.1 = (f32[32,384]{1,0:T(8,128)S(1)}, f32[16,384]{1,0:T(8,128)S(1)}, bf16[448,384]{1,0:T(8,128)(2,1)S(1)}, bf16[448,384]{1,0:T(8,128)(2,1)S(1)}) custom-call(bf16[4,448,384]{2,1,0:T(8,128)(2,1)S(1)} %get-tuple-element.98.refs_0_.act_last, bf16[4,448,384]{2,1,0:T(8,128)(2,1)S(1)} %get-tuple-element.100.refs_1_.act_older, bf16[25,384]{1,0:T(8,128)(2,1)S(1)} %bitcast.43, ...), custom_call_target="tpu_custom_call" | custom-call | flops 5000000000 | tf_op jit(solution)/shard_map/grads_1/pallas_call | solution.py:542
  32.9 0.0 collective-permute-done.3.out_in
  32.9 1.8 %five_2.1 = (f32[3,456,128]{2,1,0:T(8,128)S(1)}, bf16[448,384]{1,0:T(8,128)(2,1)S(1)}, bf16[448,384]{1,0:T(8,128)(2,1)S(1)}, f32[3,616,128]{2,1,0:T(8,128)S(1)}) custom-call(s32[1]{0:T(128)} %bitcast.top_ref, bf16[448,384]{1,0:T(8,128)(2,1)S(1)} %collective-permute-done.3.out_in, bf16[3,441,2,384]{3,2,1,0:T(2,128)(2,1)S(1)} %bitcast.27, ...), custom_call_target="tpu_custom_call" | custom-call | flops 3000000000 | tf_op jit(solution)/shard_map/five_2/pallas_call | solution.py:542
  34.7 0.0 collective-permute-done.2.pass_in
  34.7 0.3 finish_2.1
  35.0 5.2 %collective-permute-start.4 = (bf16[448,384]{1,0:T(8,128)(2,1)S(1)}, bf16[448,384]{1,0:T(8,128)(2,1)S(1)}, u32[]{:S(2)}, u32[]{:S(2)}) collective-permute-start(bf16[448,384]{1,0:T(8,128)(2,1)S(1)} %finish_2.1), channel_id=1, source_target_pairs={{8,0},{16,8},{24,16},{32,24},{40,32},{48,40},{56,48},{64,56},{72,6... | collective-permute-start | bytes 1032200 | tf_op jit(solution)/shard_map/ppermute | solution.py:24
  40.2 1.1 %three_2.1 = (bf16[448,384]{1,0:T(8,128)(2,1)S(1)}, f32[3,616,128]{2,1,0:T(8,128)S(1)}) custom-call(bf16[448,384]{1,0:T(8,128)(2,1)S(1)} %get-tuple-element.127.grad_out.refs_10_, bf16[4,448,384]{2,1,0:T(8,128)(2,1)S(1)} %get-tuple-element.100.refs_1_.act_older, bf16[384,384]{1,0:T(8,128)(2,1)S(1)} %bitcast.38, bf16[9,384]{1,0:T(8,128)(2,1)S(1)} %bitcast.51), custom_call_target="tpu_custom_call" | custom-call | flops 2000000000 | tf_op jit(solution)/shard_map/three_2/pallas_call | solution.py:542
  41.3 8.3 %gather_2.1 = (f32[384,384]{1,0:T(8,128)S(1)}, f32[384,384]{1,0:T(8,128)S(1)}, f32[32,384]{1,0:T(8,128)S(1)}, f32[16,384]{1,0:T(8,128)S(1)}, bf16[448,384]{1,0:T...) custom-call(bf16[4,448,384]{2,1,0:T(8,128)(2,1)S(1)} %get-tuple-element.98.re, ...), custom_call_target="tpu_custom_call" | custom-call | flops 10000000000 | tf_op jit(solution)/shard_map/gather_2/pallas_call | solution.py:542
  49.6 0.0 collective-permute-done.4.out_in
  49.6 3.8 %last_grads.1 = (bf16[96,896]{1,0:T(8,128)(2,1)S(1)}, bf16[96,896]{1,0:T(8,128)(2,1)S(1)}, bf16[96,896]{1,0:T(8,128)(2,1)S(1)}, f32[96,896]{1,0:T(8,128)S(1)}, b...) custom-call(s32[1]{0:T(128)} %bitcast.top_ref, ...), custom_call_target="tpu_custom_call" | custom-call | flops 6000000000 | tf_op jit(solution)/shard_map/last_grads/pallas_call | solution.py:542
  53.4 3.3 %collective-permute-start.5 = (bf16[96,896]{1,0:T(8,128)(2,1)S(1)}, bf16[96,896]{1,0:T(8,128)(2,1)S(1)}, u32[]{:S(2)}, u32[]{:S(2)}) collective-permute-start(bf16[96,896]{1,0:T(8,128)(2,1)S(1)} %get-tuple-element.156), channel_id=1, source_target_pairs={{0,4},{1,5},{2,6},{3,7},{4,0},{5,1},{6,2},{7,3},{8,12},{9,13},{10,... | collective-permute-start | bytes 516104 | tf_op jit(solution)/shard_map/ppermute | solution.py:30
  56.6 0.7 collective-permute-start.6
  57.3 2.6 %collective-permute-start.7 = (bf16[96,896]{1,0:T(8,128)(2,1)S(1)}, bf16[96,896]{1,0:T(8,128)(2,1)S(1)}, u32[]{:S(2)}, u32[]{:S(2)}) collective-permute-start(bf16[96,896]{1,0:T(8,128)(2,1)S(1)} %get-tuple-element.158), channel_id=1, source_target_pairs={{0,6},{1,7},{2,0},{3,1},{4,2},{5,3},{6,4},{7,5},{8,14},{9,15},{10,... | collective-permute-start | bytes 516104 | tf_op jit(solution)/shard_map/ppermute | solution.py:30
  59.9 1.9 %collective-permute-start.9 = (bf16[448,384]{1,0:T(8,128)(2,1)S(1)}, bf16[448,384]{1,0:T(8,128)(2,1)S(1)}, u32[]{:S(2)}, u32[]{:S(2)}) collective-permute-start(bf16[448,384]{1,0:T(8,128)(2,1)S(1)} %get-tuple-element.171), channel_id=1, source_target_pairs={{8,0},{16,8},{24,16},{32,24},{40,32},{48,40},{56,48},{64,56},{72,6... | collective-permute-start | bytes 1032200 | tf_op jit(solution)/shard_map/ppermute | solution.py:24
  61.8 2.0 %last_convs.1 = (f32[3,456,128]{2,1,0:T(8,128)S(1)}, bf16[448,384]{1,0:T(8,128)(2,1)S(1)}) custom-call(f32[3,616,128]{2,1,0:T(8,128)S(1)} %get-tuple-element.159.back_five, f32[3,616,128]{2,1,0:T(8,128)S(1)} %get-tuple-element.160.back_three, bf16[4,448,384]{2,1,0:T(8,128)(2,1)S(1)} %get-tuple-element.100.refs_1_.act_older, bf16[25,384]{1,0:T(8,128)(2,1)S(1)} %bitcast.46, ...), custom_call_target="tpu_custom_call" | custom-call | flops 3000000000 | tf_op jit(solution)/shard_map/last_convs/pallas_call | solution.py:542
  63.8 0.0 collective-permute-done.5.one
  63.8 0.0 collective-permute-done.6.two
  63.8 0.0 collective-permute-done.7.three
  63.8 0.1 half_total.1
  63.9 3.4 %collective-permute-start.8 = (bf16[48,896]{1,0:T(8,128)(2,1)S(1)}, bf16[48,896]{1,0:T(8,128)(2,1)S(1)}, u32[]{:S(2)}, u32[]{:S(2)}) collective-permute-start(bf16[48,896]{1,0:T(8,128)(2,1)S(1)} %get-tuple-element.170), channel_id=1, source_target_pairs={{0,1},{1,0},{2,3},{3,2},{4,5},{5,4},{6,7},{7,6},{8,9},{9,8},{10,11... | collective-permute-start | bytes 258056 | tf_op jit(solution)/shard_map/ppermute | solution.py:34
  67.3 0.0 collective-permute-done.9.pass_in
  67.3 1.3 %last.1 = bf16[441,2,384]{2,1,0:T(2,128)(2,1)} custom-call(s32[1]{0:T(128)} %bitcast.top_ref, bf16[448,384]{1,0:T(8,128)(2,1)S(1)} %collective-permute-done.9.pass_in, bf16[448,384]{1,0:T(8,128)(2,1)S(1)} %get-tuple-element.172.head_pass, bf16[448,384]{1,0:T(8,128)(2,1)S(1)} %get-tuple-element.173.grad_out, ...), custom_call_target="tpu_custom_call" | custom-call | flops 2000000000 | tf_op jit(solution)/shard_map/last/pallas_call | solution.py:542
  68.6 1.9 %collective-permute-done.8.landed = bf16[48,896]{1,0:T(8,128)(2,1)S(1)} collective-permute-done((bf16[48,896]{1,0:T(8,128)(2,1)S(1)}, bf16[48,896]{1,0:T(8,128)(2,1)S(1)}, u32[]{:S(2)}, u32[]{:S(2)}) %collective-permute-start.8) | collective-permute-done | bytes 86048 | tf_op jit(solution)/shard_map/ppermute | solution.py:34
  70.5 0.7 total.1
  (7 shorter events, 0.0 us)
Async XLA Ops:
  0.6 1.3 %copy-start.1 = (bf16[1,4,1,21,21,384]{5,1,4,3,2,0:T(4,128)(2,1)S(1)}, bf16[1,4,1,21,21,384]{5,1,4,3,2,0:T(4,128)(2,1)}, u32[]{:S(2)}) copy-start(bf16[1,4,1,21,21,384]{5,1,4,3,2,0:T(4,128)(2,1)} %param.9) | copy-start | bytes 4064260
  0.7 1.5 %copy-start.3 = (bf16[1,2,1,21,21,384]{5,1,4,3,2,0:T(2,128)(2,1)S(1)}, bf16[1,2,1,21,21,384]{5,1,4,3,2,0:T(2,128)(2,1)}, u32[]{:S(2)}) copy-start(bf16[1,2,1,21,21,384]{5,1,4,3,2,0:T(2,128)(2,1)} %param.11) | copy-start | bytes 2032132
  0.7 1.6 %copy-start.4 = (bf16[1,384,384]{2,1,0:T(8,128)(2,1)S(1)}, bf16[1,384,384]{2,1,0:T(8,128)(2,1)}, u32[]{:S(2)}) copy-start(bf16[1,384,384]{2,1,0:T(8,128)(2,1)} %param.16) | copy-start | bytes 884740
  0.7 1.5 %copy-start.6 = (bf16[1,25,384]{2,1,0:T(8,128)(2,1)S(1)}, bf16[1,25,384]{2,1,0:T(8,128)(2,1)}, u32[]{:S(2)}) copy-start(bf16[1,25,384]{2,1,0:T(8,128)(2,1)} %param.14) | copy-start | bytes 57604
  0.7 1.5 %copy-start.8 = (s32[1,4]{1,0:T(1,128)S(1)}, s32[1,4]{1,0:T(1,128)}, u32[]{:S(2)}) copy-start(s32[1,4]{1,0:T(1,128)} %plan_ref.3) | copy-start | bytes 52
  2.2 7.8 %copy-start.2 = (bf16[1,4,1,21,21,384]{5,1,4,3,2,0:T(4,128)(2,1)S(1)}, bf16[1,4,1,21,21,384]{5,1,4,3,2,0:T(4,128)(2,1)}, u32[]{:S(2)}) copy-start(bf16[1,4,1,21,21,384]{5,1,4,3,2,0:T(4,128)(2,1)} %param.10) | copy-start | bytes 4064260
  2.2 7.8 %copy-start.5 = (bf16[1,384,384]{2,1,0:T(8,128)(2,1)S(1)}, bf16[1,384,384]{2,1,0:T(8,128)(2,1)}, u32[]{:S(2)}) copy-start(bf16[1,384,384]{2,1,0:T(8,128)(2,1)} %param.17) | copy-start | bytes 884740
  2.2 7.8 %copy-start.7 = (bf16[1,9,384]{2,1,0:T(8,128)(2,1)S(1)}, bf16[1,9,384]{2,1,0:T(8,128)(2,1)}, u32[]{:S(2)}) copy-start(bf16[1,9,384]{2,1,0:T(8,128)(2,1)} %param.15) | copy-start | bytes 20740
  6.3 12.6 %collective-permute-start = (bf16[448,384]{1,0:T(8,128)(2,1)S(1)}, bf16[448,384]{1,0:T(8,128)(2,1)S(1)}, u32[]{:S(2)}, u32[]{:S(2)}) collective-permute-start(bf16[448,384]{1,0:T(8,128)(2,1)S(1)} %get-tuple-element.97), channel_id=1, source_target_pairs={{8,0},{16,8},{24,16},{32,24},{40,32},{48,40},{56,48},{64,56},{72,6... | collective-permute-start | bytes 1032200 | tf_op jit(solution)/shard_map/ppermute | solution.py:24
  12.1 8.7 %collective-permute-start.1 = (bf16[448,384]{1,0:T(8,128)(2,1)S(1)}, bf16[448,384]{1,0:T(8,128)(2,1)S(1)}, u32[]{:S(2)}, u32[]{:S(2)}) collective-permute-start(bf16[448,384]{1,0:T(8,128)(2,1)S(1)} %get-tuple-element.109), channel_id=1, source_target_pairs={{8,0},{16,8},{24,16},{32,24},{40,32},{48,40},{56,48},{64,56},{72,6... | collective-permute-start | bytes 1032200 | tf_op jit(solution)/shard_map/ppermute | solution.py:24
  14.7 4.3 %copy-start = (bf16[3,2,1,21,21,384]{5,1,4,3,2,0:T(2,128)(2,1)S(1)}, bf16[3,2,1,21,21,384]{5,1,4,3,2,0:T(2,128)(2,1)}, u32[]{:S(2)}) copy-start(bf16[3,2,1,21,21,384]{5,1,4,3,2,0:T(2,128)(2,1)} %param.12) | copy-start | bytes 6096388
  21.1 11.8 %collective-permute-start.3 = (bf16[448,384]{1,0:T(8,128)(2,1)S(1)}, bf16[448,384]{1,0:T(8,128)(2,1)S(1)}, u32[]{:S(2)}, u32[]{:S(2)}) collective-permute-start(bf16[448,384]{1,0:T(8,128)(2,1)S(1)} %finish_1.1), channel_id=1, source_target_pairs={{8,0},{16,8},{24,16},{32,24},{40,32},{48,40},{56,48},{64,56},{72,6... | collective-permute-start | bytes 1032200 | tf_op jit(solution)/shard_map/ppermute | solution.py:24
  26.7 8.1 %collective-permute-start.2 = (bf16[448,384]{1,0:T(8,128)(2,1)S(1)}, bf16[448,384]{1,0:T(8,128)(2,1)S(1)}, u32[]{:S(2)}, u32[]{:S(2)}) collective-permute-start(bf16[448,384]{1,0:T(8,128)(2,1)S(1)} %get-tuple-element.113), channel_id=1, source_target_pairs={{8,0},{16,8},{24,16},{32,24},{40,32},{48,40},{56,48},{64,56},{72,6... | collective-permute-start | bytes 1032200 | tf_op jit(solution)/shard_map/ppermute | solution.py:24
  35.0 14.6 %collective-permute-start.4 = (bf16[448,384]{1,0:T(8,128)(2,1)S(1)}, bf16[448,384]{1,0:T(8,128)(2,1)S(1)}, u32[]{:S(2)}, u32[]{:S(2)}) collective-permute-start(bf16[448,384]{1,0:T(8,128)(2,1)S(1)} %finish_2.1), channel_id=1, source_target_pairs={{8,0},{16,8},{24,16},{32,24},{40,32},{48,40},{56,48},{64,56},{72,6... | collective-permute-start | bytes 1032200 | tf_op jit(solution)/shard_map/ppermute | solution.py:24
  53.4 10.4 %collective-permute-start.5 = (bf16[96,896]{1,0:T(8,128)(2,1)S(1)}, bf16[96,896]{1,0:T(8,128)(2,1)S(1)}, u32[]{:S(2)}, u32[]{:S(2)}) collective-permute-start(bf16[96,896]{1,0:T(8,128)(2,1)S(1)} %get-tuple-element.156), channel_id=1, source_target_pairs={{0,4},{1,5},{2,6},{3,7},{4,0},{5,1},{6,2},{7,3},{8,12},{9,13},{10,... | collective-permute-start | bytes 516104 | tf_op jit(solution)/shard_map/ppermute | solution.py:30
  56.6 7.2 %collective-permute-start.6 = (bf16[96,896]{1,0:T(8,128)(2,1)S(1)}, bf16[96,896]{1,0:T(8,128)(2,1)S(1)}, u32[]{:S(2)}, u32[]{:S(2)}) collective-permute-start(bf16[96,896]{1,0:T(8,128)(2,1)S(1)} %get-tuple-element.157), channel_id=1, source_target_pairs={{0,2},{1,3},{2,4},{3,5},{4,6},{5,7},{6,0},{7,1},{8,10},{9,11},{10,... | collective-permute-start | bytes 516104 | tf_op jit(solution)/shard_map/ppermute | solution.py:30
  57.3 6.5 %collective-permute-start.7 = (bf16[96,896]{1,0:T(8,128)(2,1)S(1)}, bf16[96,896]{1,0:T(8,128)(2,1)S(1)}, u32[]{:S(2)}, u32[]{:S(2)}) collective-permute-start(bf16[96,896]{1,0:T(8,128)(2,1)S(1)} %get-tuple-element.158), channel_id=1, source_target_pairs={{0,6},{1,7},{2,0},{3,1},{4,2},{5,3},{6,4},{7,5},{8,14},{9,15},{10,... | collective-permute-start | bytes 516104 | tf_op jit(solution)/shard_map/ppermute | solution.py:30
  59.9 7.4 %collective-permute-start.9 = (bf16[448,384]{1,0:T(8,128)(2,1)S(1)}, bf16[448,384]{1,0:T(8,128)(2,1)S(1)}, u32[]{:S(2)}, u32[]{:S(2)}) collective-permute-start(bf16[448,384]{1,0:T(8,128)(2,1)S(1)} %get-tuple-element.171), channel_id=1, source_target_pairs={{8,0},{16,8},{24,16},{32,24},{40,32},{48,40},{56,48},{64,56},{72,6... | collective-permute-start | bytes 1032200 | tf_op jit(solution)/shard_map/ppermute | solution.py:24
  63.9 6.5 %collective-permute-start.8 = (bf16[48,896]{1,0:T(8,128)(2,1)S(1)}, bf16[48,896]{1,0:T(8,128)(2,1)S(1)}, u32[]{:S(2)}, u32[]{:S(2)}) collective-permute-start(bf16[48,896]{1,0:T(8,128)(2,1)S(1)} %get-tuple-element.170), channel_id=1, source_target_pairs={{0,1},{1,0},{2,3},{3,2},{4,5},{5,4},{6,7},{7,6},{8,9},{9,8},{10,11... | collective-permute-start | bytes 258056 | tf_op jit(solution)/shard_map/ppermute | solution.py:34

commit v9 on v8

--- a/solution.py
+++ b/solution.py
@@ -64,7 +64,7 @@
             pitched[c, pl.ds(at, PITCH), :] = jnp.where(inside, got, 0.0)
         return carry
 
-    lax.fori_loop(0, SIDE, row, 0, unroll=7)
+    lax.fori_loop(0, SIDE, row, 0, unroll=21)
 
 
 def add_window(sums, got, weight_of, b, shift, rows, kernel):
@@ -798,7 +798,7 @@
         made[:4],
     )
     *sends, grad_older = lax.optimization_barrier((*sends, grad_older))
-    landed = [around_rows(sends[distance - 1], distance) for distance in (2, 1, 3)]
+    landed = [around_rows(sends[distance - 1], distance) for distance in (1, 3, 2)]
     next_pass = from_next(grad_older)
     through, made_older = call_last_convs(
         turns - 1, back_five, back_three, act_older, taps[0], taps[1]

time: 71.7 us -> 70.9 us (0.989)
  starting transfers between devices: 29.6 us -> 28.4 us
    ppermute x3, starting transfers between devices: 6.51 us -> 5.28 us  [around_rows(): return lax.ppermute(block, 'img', route)]
    ppermute x3, waiting for transfers between devices: 0.01 us -> 0.98 us  [around_rows(): return lax.ppermute(block, 'img', route)]
  transfers between devices with their start and end apart: 10 -> 10, of which waited for: 1 -> 2; matrix products, arithmetic and copies ran while one was open for 0% -> 0% of each run, Pallas kernels for 40% -> 40%
where the time goes in v9:
time: 70.9 us; the launch traced here: 70.4 us
  Pallas kernels  37.6 us (53%)
  starting transfers between devices  28.4 us (40%)
  waiting for transfers between devices  2.4 us (3%)
  local copies, waits for them, and re-layouts  1 us (1%)
  between operations  0.96 us (1%)
    pallas_call x16, Pallas kernels, run(): pl.pallas_call(kernel, out_shape=tuple(shapes), in_specs=specs, out_specs...  36.9 us
    ppermute x6, starting transfers between devices, from_next(): return lax.ppermute(block, 'sec', [(i + 1, i) for i in range(size - 1)])  19.8 us
    ppermute x3, starting transfers between devices, around_rows(): return lax.ppermute(block, 'img', route)  5.28 us
    ppermute x1, starting transfers between devices, with_partner(): lax.ppermute(block, 'img', [(i, i ^ 1) for i in range(lax.axis_size('img'...  3.34 us
  transfers between devices with their start and end apart: 10, of which 2 were waited for; matrix products, arithmetic and copies ran while one was open for 0% of the time, Pallas kernels for 40%

profile of v9, /device:TPU:32, one launch (start us, length us, event | category | flops | bytes accessed | tf_op | source)
XLA Modules:
  0.0 70.4 jit_solution(12849968265151379204)
XLA Ops:
  0.6 0.0 copy-start.1
  0.7 0.0 copy-start.3
  0.7 0.0 copy-start.4
  0.7 0.0 copy-start.6
  0.7 0.0 copy-start.8
  0.7 0.5 opening.1.token_ref
  1.3 0.7 %copy-done.1 = bf16[1,4,1,21,21,384]{5,1,4,3,2,0:T(4,128)(2,1)S(1)} copy-done((bf16[1,4,1,21,21,384]{5,1,4,3,2,0:T(4,128)(2,1)S(1)}, bf16[1,4,1,21,21,384]{5,1,4,3,2,0:T(4,128)(2,1)}, u32[]{:S(2)}) %copy-start.1) | copy-done | bytes 1354776
  2.0 0.2 copy-done.3
  2.1 0.1 copy-done.4
  2.2 0.0 copy-done.6
  2.2 0.0 copy-start.7
  2.2 4.1 %first_five.1 = (bf16[448,384]{1,0:T(8,128)(2,1)S(1)}, bf16[4,448,384]{2,1,0:T(8,128)(2,1)S(1)}, bf16[448,384]{1,0:T(8,128)(2,1)S(1)}, f32[3,616,128]{2,1,0:T(8,128)S(1)}) custom-call(s32[1]{0:T(128)} %opening.1.token_ref, s32[1,4]{1,0:T(1,128)S(1)} %copy-done.8, bf16[441,4,384]{2,1,0:T(4,128)(2,1)S(1)} %bitcast.29, bf16[441,2,384]{2,1,0:T(2,128)(2,1)S(1)} %bitcast.31, ...), custom_call_target="tpu_custom_call" | custom-call | flops 4000000000 | tf_op jit(solution)/shard_map/first_five/pallas_call | solution.py:542
  6.3 3.6 %collective-permute-start = (bf16[448,384]{1,0:T(8,128)(2,1)S(1)}, bf16[448,384]{1,0:T(8,128)(2,1)S(1)}, u32[]{:S(2)}, u32[]{:S(2)}) collective-permute-start(bf16[448,384]{1,0:T(8,128)(2,1)S(1)} %get-tuple-element.97), channel_id=1, source_target_pairs={{8,0},{16,8},{24,16},{32,24},{40,32},{48,40},{56,48},{64,56},{72,6... | collective-permute-start | bytes 1032200 | tf_op jit(solution)/shard_map/ppermute | solution.py:24
  10.0 2.1 %first_three.1 = (bf16[448,384]{1,0:T(8,128)(2,1)S(1)}, bf16[4,448,384]{2,1,0:T(8,128)(2,1)S(1)}, f32[3,616,128]{2,1,0:T(8,128)S(1)}) custom-call(s32[1,4]{1,0:T(1,128)S(1)} %copy-done.8, bf16[441,4,384]{2,1,0:T(4,128)(2,1)S(1)} %bitcast.30, bf16[448,384]{1,0:T(8,128)(2,1)S(1)} %get-tuple-element.99.grad_out.refs_8_, bf16[384,384]{1,0:T(8,128)(2,1)S(1)} %bitcast.36, ...), custom_call_target="tpu_custom_call" | custom-call | flops 3000000000 | tf_op jit(solution)/shard_map/first_three/pallas_call | solution.py:542
  12.1 2.6 %collective-permute-start.1 = (bf16[448,384]{1,0:T(8,128)(2,1)S(1)}, bf16[448,384]{1,0:T(8,128)(2,1)S(1)}, u32[]{:S(2)}, u32[]{:S(2)}) collective-permute-start(bf16[448,384]{1,0:T(8,128)(2,1)S(1)} %get-tuple-element.109), channel_id=1, source_target_pairs={{8,0},{16,8},{24,16},{32,24},{40,32},{48,40},{56,48},{64,56},{72,6... | collective-permute-start | bytes 1032200 | tf_op jit(solution)/shard_map/ppermute | solution.py:24
  14.7 0.0 copy-start
  14.7 4.2 %grads_0.1 = (f32[32,384]{1,0:T(8,128)S(1)}, f32[16,384]{1,0:T(8,128)S(1)}, bf16[448,384]{1,0:T(8,128)(2,1)S(1)}, bf16[448,384]{1,0:T(8,128)(2,1)S(1)}) custom-call(bf16[4,448,384]{2,1,0:T(8,128)(2,1)S(1)} %get-tuple-element.98.refs_0_.act_last, bf16[4,448,384]{2,1,0:T(8,128)(2,1)S(1)} %get-tuple-element.100.refs_1_.act_older, bf16[25,384]{1,0:T(8,128)(2,1)S(1)} %bitcast.41, ...), custom_call_target="tpu_custom_call" | custom-call | flops 5000000000 | tf_op jit(solution)/shard_map/grads_0/pallas_call | solution.py:542
  18.9 0.0 collective-permute-done.out_in
  18.9 1.8 %five_1.1 = (f32[3,456,128]{2,1,0:T(8,128)S(1)}, bf16[448,384]{1,0:T(8,128)(2,1)S(1)}, bf16[448,384]{1,0:T(8,128)(2,1)S(1)}, f32[3,616,128]{2,1,0:T(8,128)S(1)}) custom-call(s32[1]{0:T(128)} %bitcast.top_ref, bf16[448,384]{1,0:T(8,128)(2,1)S(1)} %collective-permute-done.out_in, bf16[3,441,2,384]{3,2,1,0:T(2,128)(2,1)S(1)} %bitcast.26, ...), custom_call_target="tpu_custom_call" | custom-call | flops 3000000000 | tf_op jit(solution)/shard_map/five_1/pallas_call | solution.py:542
  20.8 0.0 collective-permute-done.1.pass_in
  20.8 0.3 finish_1.1
  21.1 4.5 %collective-permute-start.3 = (bf16[448,384]{1,0:T(8,128)(2,1)S(1)}, bf16[448,384]{1,0:T(8,128)(2,1)S(1)}, u32[]{:S(2)}, u32[]{:S(2)}) collective-permute-start(bf16[448,384]{1,0:T(8,128)(2,1)S(1)} %finish_1.1), channel_id=1, source_target_pairs={{8,0},{16,8},{24,16},{32,24},{40,32},{48,40},{56,48},{64,56},{72,6... | collective-permute-start | bytes 1032200 | tf_op jit(solution)/shard_map/ppermute | solution.py:24
  25.6 1.1 %three_1.1 = (bf16[448,384]{1,0:T(8,128)(2,1)S(1)}, f32[3,616,128]{2,1,0:T(8,128)S(1)}) custom-call(bf16[448,384]{1,0:T(8,128)(2,1)S(1)} %get-tuple-element.112.grad_out.refs_9_, bf16[4,448,384]{2,1,0:T(8,128)(2,1)S(1)} %get-tuple-element.100.refs_1_.act_older, bf16[384,384]{1,0:T(8,128)(2,1)S(1)} %bitcast.37, bf16[9,384]{1,0:T(8,128)(2,1)S(1)} %bitcast.49), custom_call_target="tpu_custom_call" | custom-call | flops 2000000000 | tf_op jit(solution)/shard_map/three_1/pallas_call | solution.py:542
  26.7 1.9 %collective-permute-start.2 = (bf16[448,384]{1,0:T(8,128)(2,1)S(1)}, bf16[448,384]{1,0:T(8,128)(2,1)S(1)}, u32[]{:S(2)}, u32[]{:S(2)}) collective-permute-start(bf16[448,384]{1,0:T(8,128)(2,1)S(1)} %get-tuple-element.113), channel_id=1, source_target_pairs={{8,0},{16,8},{24,16},{32,24},{40,32},{48,40},{56,48},{64,56},{72,6... | collective-permute-start | bytes 1032200 | tf_op jit(solution)/shard_map/ppermute | solution.py:24
  28.6 4.3 %grads_1.1 = (f32[32,384]{1,0:T(8,128)S(1)}, f32[16,384]{1,0:T(8,128)S(1)}, bf16[448,384]{1,0:T(8,128)(2,1)S(1)}, bf16[448,384]{1,0:T(8,128)(2,1)S(1)}) custom-call(bf16[4,448,384]{2,1,0:T(8,128)(2,1)S(1)} %get-tuple-element.98.refs_0_.act_last, bf16[4,448,384]{2,1,0:T(8,128)(2,1)S(1)} %get-tuple-element.100.refs_1_.act_older, bf16[25,384]{1,0:T(8,128)(2,1)S(1)} %bitcast.43, ...), custom_call_target="tpu_custom_call" | custom-call | flops 5000000000 | tf_op jit(solution)/shard_map/grads_1/pallas_call | solution.py:542
  32.9 0.0 collective-permute-done.3.out_in
  32.9 1.8 %five_2.1 = (f32[3,456,128]{2,1,0:T(8,128)S(1)}, bf16[448,384]{1,0:T(8,128)(2,1)S(1)}, bf16[448,384]{1,0:T(8,128)(2,1)S(1)}, f32[3,616,128]{2,1,0:T(8,128)S(1)}) custom-call(s32[1]{0:T(128)} %bitcast.top_ref, bf16[448,384]{1,0:T(8,128)(2,1)S(1)} %collective-permute-done.3.out_in, bf16[3,441,2,384]{3,2,1,0:T(2,128)(2,1)S(1)} %bitcast.27, ...), custom_call_target="tpu_custom_call" | custom-call | flops 3000000000 | tf_op jit(solution)/shard_map/five_2/pallas_call | solution.py:542
  34.7 0.0 collective-permute-done.2.pass_in
  34.7 0.3 finish_2.1
  35.0 5.2 %collective-permute-start.4 = (bf16[448,384]{1,0:T(8,128)(2,1)S(1)}, bf16[448,384]{1,0:T(8,128)(2,1)S(1)}, u32[]{:S(2)}, u32[]{:S(2)}) collective-permute-start(bf16[448,384]{1,0:T(8,128)(2,1)S(1)} %finish_2.1), channel_id=1, source_target_pairs={{8,0},{16,8},{24,16},{32,24},{40,32},{48,40},{56,48},{64,56},{72,6... | collective-permute-start | bytes 1032200 | tf_op jit(solution)/shard_map/ppermute | solution.py:24
  40.2 1.1 %three_2.1 = (bf16[448,384]{1,0:T(8,128)(2,1)S(1)}, f32[3,616,128]{2,1,0:T(8,128)S(1)}) custom-call(bf16[448,384]{1,0:T(8,128)(2,1)S(1)} %get-tuple-element.127.grad_out.refs_10_, bf16[4,448,384]{2,1,0:T(8,128)(2,1)S(1)} %get-tuple-element.100.refs_1_.act_older, bf16[384,384]{1,0:T(8,128)(2,1)S(1)} %bitcast.38, bf16[9,384]{1,0:T(8,128)(2,1)S(1)} %bitcast.51), custom_call_target="tpu_custom_call" | custom-call | flops 2000000000 | tf_op jit(solution)/shard_map/three_2/pallas_call | solution.py:542
  41.3 8.2 %gather_2.1 = (f32[384,384]{1,0:T(8,128)S(1)}, f32[384,384]{1,0:T(8,128)S(1)}, f32[32,384]{1,0:T(8,128)S(1)}, f32[16,384]{1,0:T(8,128)S(1)}, bf16[448,384]{1,0:T...) custom-call(bf16[4,448,384]{2,1,0:T(8,128)(2,1)S(1)} %get-tuple-element.98.re, ...), custom_call_target="tpu_custom_call" | custom-call | flops 10000000000 | tf_op jit(solution)/shard_map/gather_2/pallas_call | solution.py:542
  49.5 0.0 collective-permute-done.4.out_in
  49.5 3.8 %last_grads.1 = (bf16[96,896]{1,0:T(8,128)(2,1)S(1)}, bf16[96,896]{1,0:T(8,128)(2,1)S(1)}, bf16[96,896]{1,0:T(8,128)(2,1)S(1)}, f32[96,896]{1,0:T(8,128)S(1)}, b...) custom-call(s32[1]{0:T(128)} %bitcast.top_ref, ...), custom_call_target="tpu_custom_call" | custom-call | flops 6000000000 | tf_op jit(solution)/shard_map/last_grads/pallas_call | solution.py:542
  53.3 1.6 %collective-permute-start.5 = (bf16[96,896]{1,0:T(8,128)(2,1)S(1)}, bf16[96,896]{1,0:T(8,128)(2,1)S(1)}, u32[]{:S(2)}, u32[]{:S(2)}) collective-permute-start(bf16[96,896]{1,0:T(8,128)(2,1)S(1)} %get-tuple-element.156), channel_id=1, source_target_pairs={{0,2},{1,3},{2,4},{3,5},{4,6},{5,7},{6,0},{7,1},{8,10},{9,11},{10,... | collective-permute-start | bytes 516104 | tf_op jit(solution)/shard_map/ppermute | solution.py:30
  55.0 1.7 %collective-permute-start.6 = (bf16[96,896]{1,0:T(8,128)(2,1)S(1)}, bf16[96,896]{1,0:T(8,128)(2,1)S(1)}, u32[]{:S(2)}, u32[]{:S(2)}) collective-permute-start(bf16[96,896]{1,0:T(8,128)(2,1)S(1)} %get-tuple-element.157), channel_id=1, source_target_pairs={{0,6},{1,7},{2,0},{3,1},{4,2},{5,3},{6,4},{7,5},{8,14},{9,15},{10,... | collective-permute-start | bytes 516104 | tf_op jit(solution)/shard_map/ppermute | solution.py:30
  56.6 2.0 %collective-permute-start.7 = (bf16[96,896]{1,0:T(8,128)(2,1)S(1)}, bf16[96,896]{1,0:T(8,128)(2,1)S(1)}, u32[]{:S(2)}, u32[]{:S(2)}) collective-permute-start(bf16[96,896]{1,0:T(8,128)(2,1)S(1)} %get-tuple-element.158), channel_id=1, source_target_pairs={{0,4},{1,5},{2,6},{3,7},{4,0},{5,1},{6,2},{7,3},{8,12},{9,13},{10,... | collective-permute-start | bytes 516104 | tf_op jit(solution)/shard_map/ppermute | solution.py:30
  58.6 1.9 %collective-permute-start.9 = (bf16[448,384]{1,0:T(8,128)(2,1)S(1)}, bf16[448,384]{1,0:T(8,128)(2,1)S(1)}, u32[]{:S(2)}, u32[]{:S(2)}) collective-permute-start(bf16[448,384]{1,0:T(8,128)(2,1)S(1)} %get-tuple-element.171), channel_id=1, source_target_pairs={{8,0},{16,8},{24,16},{32,24},{40,32},{48,40},{56,48},{64,56},{72,6... | collective-permute-start | bytes 1032200 | tf_op jit(solution)/shard_map/ppermute | solution.py:24
  60.5 2.0 %last_convs.1 = (f32[3,456,128]{2,1,0:T(8,128)S(1)}, bf16[448,384]{1,0:T(8,128)(2,1)S(1)}) custom-call(f32[3,616,128]{2,1,0:T(8,128)S(1)} %get-tuple-element.159.back_five, f32[3,616,128]{2,1,0:T(8,128)S(1)} %get-tuple-element.160.back_three, bf16[4,448,384]{2,1,0:T(8,128)(2,1)S(1)} %get-tuple-element.100.refs_1_.act_older, bf16[25,384]{1,0:T(8,128)(2,1)S(1)} %bitcast.46, ...), custom_call_target="tpu_custom_call" | custom-call | flops 3000000000 | tf_op jit(solution)/shard_map/last_convs/pallas_call | solution.py:542
  62.5 0.0 collective-permute-done.5.one
  62.5 0.0 collective-permute-done.6.two
  62.6 1.0 %collective-permute-done.7.three = bf16[96,896]{1,0:T(8,128)(2,1)S(1)} collective-permute-done((bf16[96,896]{1,0:T(8,128)(2,1)S(1)}, bf16[96,896]{1,0:T(8,128)(2,1)S(1)}, u32[]{:S(2)}, u32[]{:S(2)}) %collective-permute-start.7) | collective-permute-done | bytes 172064 | tf_op jit(solution)/shard_map/ppermute | solution.py:30
  63.5 0.1 half_total.1
  63.6 3.3 %collective-permute-start.8 = (bf16[48,896]{1,0:T(8,128)(2,1)S(1)}, bf16[48,896]{1,0:T(8,128)(2,1)S(1)}, u32[]{:S(2)}, u32[]{:S(2)}) collective-permute-start(bf16[48,896]{1,0:T(8,128)(2,1)S(1)} %get-tuple-element.170), channel_id=1, source_target_pairs={{0,1},{1,0},{2,3},{3,2},{4,5},{5,4},{6,7},{7,6},{8,9},{9,8},{10,11... | collective-permute-start | bytes 258056 | tf_op jit(solution)/shard_map/ppermute | solution.py:34
  67.0 0.0 collective-permute-done.9.pass_in
  67.0 1.3 %last.1 = bf16[441,2,384]{2,1,0:T(2,128)(2,1)} custom-call(s32[1]{0:T(128)} %bitcast.top_ref, bf16[448,384]{1,0:T(8,128)(2,1)S(1)} %collective-permute-done.9.pass_in, bf16[448,384]{1,0:T(8,128)(2,1)S(1)} %get-tuple-element.172.head_pass, bf16[448,384]{1,0:T(8,128)(2,1)S(1)} %get-tuple-element.173.grad_out, ...), custom_call_target="tpu_custom_call" | custom-call | flops 2000000000 | tf_op jit(solution)/shard_map/last/pallas_call | solution.py:542
  68.3 1.4 %collective-permute-done.8.landed = bf16[48,896]{1,0:T(8,128)(2,1)S(1)} collective-permute-done((bf16[48,896]{1,0:T(8,128)(2,1)S(1)}, bf16[48,896]{1,0:T(8,128)(2,1)S(1)}, u32[]{:S(2)}, u32[]{:S(2)}) %collective-permute-start.8) | collective-permute-done | bytes 86048 | tf_op jit(solution)/shard_map/ppermute | solution.py:34
  69.7 0.7 total.1
  (7 shorter events, 0.0 us)
Async XLA Ops:
  0.6 1.3 %copy-start.1 = (bf16[1,4,1,21,21,384]{5,1,4,3,2,0:T(4,128)(2,1)S(1)}, bf16[1,4,1,21,21,384]{5,1,4,3,2,0:T(4,128)(2,1)}, u32[]{:S(2)}) copy-start(bf16[1,4,1,21,21,384]{5,1,4,3,2,0:T(4,128)(2,1)} %param.9) | copy-start | bytes 4064260
  0.7 1.5 %copy-start.3 = (bf16[1,2,1,21,21,384]{5,1,4,3,2,0:T(2,128)(2,1)S(1)}, bf16[1,2,1,21,21,384]{5,1,4,3,2,0:T(2,128)(2,1)}, u32[]{:S(2)}) copy-start(bf16[1,2,1,21,21,384]{5,1,4,3,2,0:T(2,128)(2,1)} %param.11) | copy-start | bytes 2032132
  0.7 1.6 %copy-start.4 = (bf16[1,384,384]{2,1,0:T(8,128)(2,1)S(1)}, bf16[1,384,384]{2,1,0:T(8,128)(2,1)}, u32[]{:S(2)}) copy-start(bf16[1,384,384]{2,1,0:T(8,128)(2,1)} %param.16) | copy-start | bytes 884740
  0.7 1.5 %copy-start.6 = (bf16[1,25,384]{2,1,0:T(8,128)(2,1)S(1)}, bf16[1,25,384]{2,1,0:T(8,128)(2,1)}, u32[]{:S(2)}) copy-start(bf16[1,25,384]{2,1,0:T(8,128)(2,1)} %param.14) | copy-start | bytes 57604
  0.7 1.5 %copy-start.8 = (s32[1,4]{1,0:T(1,128)S(1)}, s32[1,4]{1,0:T(1,128)}, u32[]{:S(2)}) copy-start(s32[1,4]{1,0:T(1,128)} %plan_ref.3) | copy-start | bytes 52
  2.2 7.8 %copy-start.2 = (bf16[1,4,1,21,21,384]{5,1,4,3,2,0:T(4,128)(2,1)S(1)}, bf16[1,4,1,21,21,384]{5,1,4,3,2,0:T(4,128)(2,1)}, u32[]{:S(2)}) copy-start(bf16[1,4,1,21,21,384]{5,1,4,3,2,0:T(4,128)(2,1)} %param.10) | copy-start | bytes 4064260
  2.2 7.8 %copy-start.5 = (bf16[1,384,384]{2,1,0:T(8,128)(2,1)S(1)}, bf16[1,384,384]{2,1,0:T(8,128)(2,1)}, u32[]{:S(2)}) copy-start(bf16[1,384,384]{2,1,0:T(8,128)(2,1)} %param.17) | copy-start | bytes 884740
  2.2 7.8 %copy-start.7 = (bf16[1,9,384]{2,1,0:T(8,128)(2,1)S(1)}, bf16[1,9,384]{2,1,0:T(8,128)(2,1)}, u32[]{:S(2)}) copy-start(bf16[1,9,384]{2,1,0:T(8,128)(2,1)} %param.15) | copy-start | bytes 20740
  6.3 12.6 %collective-permute-start = (bf16[448,384]{1,0:T(8,128)(2,1)S(1)}, bf16[448,384]{1,0:T(8,128)(2,1)S(1)}, u32[]{:S(2)}, u32[]{:S(2)}) collective-permute-start(bf16[448,384]{1,0:T(8,128)(2,1)S(1)} %get-tuple-element.97), channel_id=1, source_target_pairs={{8,0},{16,8},{24,16},{32,24},{40,32},{48,40},{56,48},{64,56},{72,6... | collective-permute-start | bytes 1032200 | tf_op jit(solution)/shard_map/ppermute | solution.py:24
  12.1 8.7 %collective-permute-start.1 = (bf16[448,384]{1,0:T(8,128)(2,1)S(1)}, bf16[448,384]{1,0:T(8,128)(2,1)S(1)}, u32[]{:S(2)}, u32[]{:S(2)}) collective-permute-start(bf16[448,384]{1,0:T(8,128)(2,1)S(1)} %get-tuple-element.109), channel_id=1, source_target_pairs={{8,0},{16,8},{24,16},{32,24},{40,32},{48,40},{56,48},{64,56},{72,6... | collective-permute-start | bytes 1032200 | tf_op jit(solution)/shard_map/ppermute | solution.py:24
  14.7 4.3 %copy-start = (bf16[3,2,1,21,21,384]{5,1,4,3,2,0:T(2,128)(2,1)S(1)}, bf16[3,2,1,21,21,384]{5,1,4,3,2,0:T(2,128)(2,1)}, u32[]{:S(2)}) copy-start(bf16[3,2,1,21,21,384]{5,1,4,3,2,0:T(2,128)(2,1)} %param.12) | copy-start | bytes 6096388
  21.1 11.8 %collective-permute-start.3 = (bf16[448,384]{1,0:T(8,128)(2,1)S(1)}, bf16[448,384]{1,0:T(8,128)(2,1)S(1)}, u32[]{:S(2)}, u32[]{:S(2)}) collective-permute-start(bf16[448,384]{1,0:T(8,128)(2,1)S(1)} %finish_1.1), channel_id=1, source_target_pairs={{8,0},{16,8},{24,16},{32,24},{40,32},{48,40},{56,48},{64,56},{72,6... | collective-permute-start | bytes 1032200 | tf_op jit(solution)/shard_map/ppermute | solution.py:24
  26.7 8.0 %collective-permute-start.2 = (bf16[448,384]{1,0:T(8,128)(2,1)S(1)}, bf16[448,384]{1,0:T(8,128)(2,1)S(1)}, u32[]{:S(2)}, u32[]{:S(2)}) collective-permute-start(bf16[448,384]{1,0:T(8,128)(2,1)S(1)} %get-tuple-element.113), channel_id=1, source_target_pairs={{8,0},{16,8},{24,16},{32,24},{40,32},{48,40},{56,48},{64,56},{72,6... | collective-permute-start | bytes 1032200 | tf_op jit(solution)/shard_map/ppermute | solution.py:24
  35.0 14.5 %collective-permute-start.4 = (bf16[448,384]{1,0:T(8,128)(2,1)S(1)}, bf16[448,384]{1,0:T(8,128)(2,1)S(1)}, u32[]{:S(2)}, u32[]{:S(2)}) collective-permute-start(bf16[448,384]{1,0:T(8,128)(2,1)S(1)} %finish_2.1), channel_id=1, source_target_pairs={{8,0},{16,8},{24,16},{32,24},{40,32},{48,40},{56,48},{64,56},{72,6... | collective-permute-start | bytes 1032200 | tf_op jit(solution)/shard_map/ppermute | solution.py:24
  53.3 9.2 %collective-permute-start.5 = (bf16[96,896]{1,0:T(8,128)(2,1)S(1)}, bf16[96,896]{1,0:T(8,128)(2,1)S(1)}, u32[]{:S(2)}, u32[]{:S(2)}) collective-permute-start(bf16[96,896]{1,0:T(8,128)(2,1)S(1)} %get-tuple-element.156), channel_id=1, source_target_pairs={{0,2},{1,3},{2,4},{3,5},{4,6},{5,7},{6,0},{7,1},{8,10},{9,11},{10,... | collective-permute-start | bytes 516104 | tf_op jit(solution)/shard_map/ppermute | solution.py:30
  55.0 7.6 %collective-permute-start.6 = (bf16[96,896]{1,0:T(8,128)(2,1)S(1)}, bf16[96,896]{1,0:T(8,128)(2,1)S(1)}, u32[]{:S(2)}, u32[]{:S(2)}) collective-permute-start(bf16[96,896]{1,0:T(8,128)(2,1)S(1)} %get-tuple-element.157), channel_id=1, source_target_pairs={{0,6},{1,7},{2,0},{3,1},{4,2},{5,3},{6,4},{7,5},{8,14},{9,15},{10,... | collective-permute-start | bytes 516104 | tf_op jit(solution)/shard_map/ppermute | solution.py:30
  56.6 6.9 %collective-permute-start.7 = (bf16[96,896]{1,0:T(8,128)(2,1)S(1)}, bf16[96,896]{1,0:T(8,128)(2,1)S(1)}, u32[]{:S(2)}, u32[]{:S(2)}) collective-permute-start(bf16[96,896]{1,0:T(8,128)(2,1)S(1)} %get-tuple-element.158), channel_id=1, source_target_pairs={{0,4},{1,5},{2,6},{3,7},{4,0},{5,1},{6,2},{7,3},{8,12},{9,13},{10,... | collective-permute-start | bytes 516104 | tf_op jit(solution)/shard_map/ppermute | solution.py:30
  58.6 8.4 %collective-permute-start.9 = (bf16[448,384]{1,0:T(8,128)(2,1)S(1)}, bf16[448,384]{1,0:T(8,128)(2,1)S(1)}, u32[]{:S(2)}, u32[]{:S(2)}) collective-permute-start(bf16[448,384]{1,0:T(8,128)(2,1)S(1)} %get-tuple-element.171), channel_id=1, source_target_pairs={{8,0},{16,8},{24,16},{32,24},{40,32},{48,40},{56,48},{64,56},{72,6... | collective-permute-start | bytes 1032200 | tf_op jit(solution)/shard_map/ppermute | solution.py:24
  63.6 6.1 %collective-permute-start.8 = (bf16[48,896]{1,0:T(8,128)(2,1)S(1)}, bf16[48,896]{1,0:T(8,128)(2,1)S(1)}, u32[]{:S(2)}, u32[]{:S(2)}) collective-permute-start(bf16[48,896]{1,0:T(8,128)(2,1)S(1)} %get-tuple-element.170), channel_id=1, source_target_pairs={{0,1},{1,0},{2,3},{3,2},{4,5},{5,4},{6,7},{7,6},{8,9},{9,8},{10,11... | collective-permute-start | bytes 258056 | tf_op jit(solution)/shard_map/ppermute | solution.py:34
